TPU v7x, 32 devices: a whole 2x2x4 slice. The times are simulated.
32 devices in a mesh: dp: 4 (over z), fsdp: 8 (over y, x, core).
Axes of the slice: x: 2, y: 2, z: 4, core: 2. Of those that a mesh axis runs over, the one named last changes fastest.
Arguments:
- long_x: float32 [32, 1024, 768], P(('dp', 'fsdp')), may hold values from -6 to 6
- short_x: float32 [32, 512, 768], P(('dp', 'fsdp')), may hold values from -6 to 6
- long_len: int32 [32], P(('dp', 'fsdp')), may hold values from 256 to 1024
- short_len: int32 [32], P(('dp', 'fsdp')), may hold values from 128 to 512
- expert_ids: int32 [49152, 1], P(('dp', 'fsdp')), may hold values from 0 to 7; in each aligned block of 1536 rows (0 to 1535, 1536 to 3071, ...) at most 256 rows name the same one
- ln1_gain: bfloat16 [768], P(('dp', 'fsdp')), may hold values from 0.5 to 1.5
- ln1_bias: bfloat16 [768], P(('dp', 'fsdp')), may hold values from -1.5 to 1.5
- w_qkv: bfloat16 [768, 2304], P(('dp', 'fsdp')), may hold values from -0.21875 to 0.21875
- w_proj: bfloat16 [768, 768], P(None, ('dp', 'fsdp')), may hold values from -1.75 to 1.75
- ln2_gain: bfloat16 [768], P(('dp', 'fsdp')), may hold values from 0.5 to 1.5
- ln2_bias: bfloat16 [768], P(('dp', 'fsdp')), may hold values from -1.5 to 1.5
- w_up: bfloat16 [8, 768, 3072], P('fsdp', None, 'dp'), may hold values from -0.21875 to 0.21875
- w_down: bfloat16 [8, 3072, 768], P('fsdp', 'dp'), may hold values from -0.109375 to 0.109375
- long_cot: float32 [32, 1024, 768], P(('dp', 'fsdp')), may hold values from -6 to 6
- short_cot: float32 [32, 512, 768], P(('dp', 'fsdp')), may hold values from -6 to 6
Outputs:
- long_out: float32 [32, 1024, 768], P(('dp', 'fsdp'))
- short_out: float32 [32, 512, 768], P(('dp', 'fsdp'))
- long_grad: float32 [32, 1024, 768], P(('dp', 'fsdp'))
- short_grad: float32 [32, 512, 768], P(('dp', 'fsdp'))
- grad_ln1_gain: float32 [768], P(('dp', 'fsdp'))
- grad_ln1_bias: float32 [768], P(('dp', 'fsdp'))
- grad_qkv: float32 [768, 2304], P(('dp', 'fsdp'))
- grad_proj: float32 [768, 768], P(None, ('dp', 'fsdp'))
- grad_ln2_gain: float32 [768], P(('dp', 'fsdp'))
- grad_ln2_bias: float32 [768], P(('dp', 'fsdp'))
- grad_up: float32 [8, 768, 3072], P('fsdp', None, 'dp')
- grad_down: float32 [8, 3072, 768], P('fsdp', 'dp')
Inputs may be any that keep to these rules, and one draw needn't show every extreme that they name: `expert_ids`: in each aligned block of 1536 rows (the token slots of one device), no expert is named by more than 256 rows.
All inputs are finite; a program needn't handle non-finite values.
Results may differ from a plain program's by a relative error of at most 0.012.
Values may be sent and summed in bfloat16 or wider, within the bound.
A program may use at most 320 MiB of HBM per device.

v0:
```python
import jax
import jax.numpy as jnp
from jax import lax
from jax.sharding import PartitionSpec as P

HEADS = 12
HEAD_DIM = 64


EPSILON = 1e-05
MASKED = -1e30


def norm_parts(inputs):
    average = jnp.mean(inputs, -1, keepdims=True)
    centred = inputs - average
    inv_scale = lax.rsqrt(jnp.mean(centred * centred, -1, keepdims=True) + EPSILON)
    return (centred * inv_scale, inv_scale)


def norm_back(grad_normed, normed, inv_scale):
    centre_term = jnp.mean(grad_normed, -1, keepdims=True)
    slope_term = jnp.mean(grad_normed * normed, -1, keepdims=True)
    return inv_scale * (grad_normed - centre_term - normed * slope_term)


def gelu_back(pre_act, grad_act):
    unused_value, pullback = jax.vjp(jax.nn.gelu, pre_act)
    return pullback(grad_act)[0]


def split_heads(query_key_value):
    seq_count, length = (query_key_value.shape[0], query_key_value.shape[1])
    split_parts = query_key_value.reshape(seq_count, length, 3, HEADS, HEAD_DIM)
    return (split_parts[:, :, 0], split_parts[:, :, 1], split_parts[:, :, 2])


def block_scores(queries, keys_all, start_row, block_rows, lengths):
    stop_row = start_row + block_rows
    scores = jnp.einsum(
        "sqhc,skhc->shqk",
        queries[:, start_row:stop_row],
        keys_all[:, :stop_row],
        preferred_element_type=jnp.float32,
    ) * HEAD_DIM ** (-0.5)
    query_pos = start_row + jnp.arange(block_rows, dtype=jnp.int32)
    key_pos = jnp.arange(stop_row, dtype=jnp.int32)
    causal = key_pos[None, :] <= query_pos[:, None]
    inside = key_pos[None, None, :] < lengths[:, None, None]
    allowed = (causal[None] & inside)[:, None]
    return jnp.where(allowed, scores, MASKED)


def attend(query_key_value, lengths):
    queries, keys_all, values = split_heads(query_key_value)
    seq_count, length = (query_key_value.shape[0], query_key_value.shape[1])
    block_rows = min(512, length)
    pieces = []
    totals = []
    for start_row in range(0, length, block_rows):
        stop_row = start_row + block_rows
        scores = block_scores(queries, keys_all, start_row, block_rows, lengths)
        highest = jnp.max(scores, -1, keepdims=True)
        exponent = jnp.exp(scores - highest)
        denominator = jnp.sum(exponent, -1, keepdims=True)
        probability = (exponent / denominator).astype(jnp.bfloat16)
        pieces.append(
            jnp.einsum(
                "shqk,skhc->sqhc",
                probability,
                values[:, :stop_row],
                preferred_element_type=jnp.float32,
            )
        )
        totals.append(highest + jnp.log(denominator))
    expert_mixture = jnp.concatenate(pieces, 1)
    return (expert_mixture.reshape(seq_count, length, -1), jnp.concatenate(totals, 2))


def attend_back(query_key_value, log_sums, grad_mixture, lengths):
    queries, keys_all, values = split_heads(query_key_value)
    head_gradients = grad_mixture.reshape(queries.shape)
    length = query_key_value.shape[1]
    block_rows = min(512, length)
    score_scale = HEAD_DIM ** (-0.5)
    grad_queries = []
    grad_keys = jnp.zeros(keys_all.shape, jnp.float32)
    grad_values = jnp.zeros(values.shape, jnp.float32)
    for start_row in range(0, length, block_rows):
        stop_row = start_row + block_rows
        scores = block_scores(queries, keys_all, start_row, block_rows, lengths)
        probability = jnp.exp(scores - log_sums[:, :, start_row:stop_row])
        grad_block = head_gradients[:, start_row:stop_row]
        grad_prob = jnp.einsum(
            "sqhc,skhc->shqk", grad_block, values[:, :stop_row], preferred_element_type=jnp.float32
        )
        grad_values = grad_values.at[:, :stop_row].add(
            jnp.einsum(
                "shqk,sqhc->skhc",
                probability.astype(jnp.bfloat16),
                grad_block,
                preferred_element_type=jnp.float32,
            )
        )
        centre = jnp.sum(grad_prob * probability, -1, keepdims=True)
        grad_scores = (probability * (grad_prob - centre)).astype(jnp.bfloat16)
        grad_queries.append(
            jnp.einsum(
                "shqk,skhc->sqhc",
                grad_scores,
                keys_all[:, :stop_row],
                preferred_element_type=jnp.float32,
            )
            * score_scale
        )
        grad_keys = grad_keys.at[:, :stop_row].add(
            jnp.einsum(
                "shqk,sqhc->skhc",
                grad_scores,
                queries[:, start_row:stop_row],
                preferred_element_type=jnp.float32,
            )
            * score_scale
        )
    stacked = jnp.stack([jnp.concatenate(grad_queries, 1), grad_keys, grad_values], 2)
    return stacked.reshape(query_key_value.shape)


def group_forward(inputs, lengths, dense_set):
    (
        first_gain,
        first_bias,
        query_key_value_weight,
        output_projection_weight,
        second_gain,
        second_bias,
    ) = dense_set
    first_normed, first_scale = norm_parts(inputs)
    block_input_rows = (
        first_normed * first_gain.astype(jnp.float32) + first_bias.astype(jnp.float32)
    ).astype(jnp.bfloat16)
    query_key_value = jnp.einsum(
        "onq,qm->onm", block_input_rows, query_key_value_weight, preferred_element_type=jnp.float32
    ).astype(jnp.bfloat16)
    expert_mixture, log_sums = attend(query_key_value, lengths)
    expert_mixture = expert_mixture.astype(jnp.bfloat16)
    hidden = inputs + jnp.einsum(
        "nap,pc->nac", expert_mixture, output_projection_weight, preferred_element_type=jnp.float32
    )
    second_normed, second_scale = norm_parts(hidden)
    normed_out = (
        second_normed * second_gain.astype(jnp.float32) + second_bias.astype(jnp.float32)
    ).astype(jnp.bfloat16)
    kept_state = (
        first_normed,
        first_scale,
        block_input_rows,
        query_key_value,
        expert_mixture,
        log_sums,
        second_normed,
        second_scale,
    )
    return (hidden, normed_out, kept_state)


def group_backward(kept_state, grad_out, grad_normed, lengths, dense_set):
    (
        first_gain,
        first_bias,
        query_key_value_weight,
        output_projection_weight,
        second_gain,
        second_bias,
    ) = dense_set
    (
        first_normed,
        first_scale,
        block_input_rows,
        query_key_value,
        expert_mixture,
        log_sums,
        second_normed,
        second_scale,
    ) = kept_state
    grad_hidden = grad_out + norm_back(
        grad_normed * second_gain.astype(jnp.float32), second_normed, second_scale
    )
    grad_gain2 = jnp.sum(grad_normed * second_normed, (0, 1))
    grad_bias2 = jnp.sum(grad_normed, (0, 1))
    branch_gradient = grad_hidden.astype(jnp.bfloat16)
    grad_projection = jnp.einsum(
        "zwo,zwf->of", expert_mixture, branch_gradient, preferred_element_type=jnp.float32
    )
    grad_mixture = jnp.einsum(
        "qbf,zf->qbz", branch_gradient, output_projection_weight, preferred_element_type=jnp.float32
    ).astype(jnp.bfloat16)
    head_gradients = attend_back(query_key_value, log_sums, grad_mixture, lengths).astype(
        jnp.bfloat16
    )
    grad_weight_qkv = jnp.einsum(
        "qwh,qwb->hb", block_input_rows, head_gradients, preferred_element_type=jnp.float32
    )
    grad_entered = jnp.einsum(
        "iuk,gk->iug", head_gradients, query_key_value_weight, preferred_element_type=jnp.float32
    )
    grad_gain1 = jnp.sum(grad_entered * first_normed, (0, 1))
    grad_bias1 = jnp.sum(grad_entered, (0, 1))
    grad_inputs = grad_hidden + norm_back(
        grad_entered * first_gain.astype(jnp.float32), first_normed, first_scale
    )
    return (
        grad_inputs,
        (grad_gain1, grad_bias1, grad_weight_qkv, grad_projection, grad_gain2, grad_bias2),
    )


def on_device(
    long_x,
    short_x,
    long_len,
    short_len,
    expert_ids,
    ln1_gain,
    ln1_bias,
    w_qkv,
    w_proj,
    ln2_gain,
    ln2_bias,
    w_up,
    w_down,
    long_cot,
    short_cot,
):
    dense_set = (
        lax.all_gather(ln1_gain, ("dp", "fsdp"), axis=0, tiled=True),
        lax.all_gather(ln1_bias, ("dp", "fsdp"), axis=0, tiled=True),
        lax.all_gather(w_qkv, ("dp", "fsdp"), axis=0, tiled=True),
        lax.all_gather(w_proj, ("dp", "fsdp"), axis=1, tiled=True),
        lax.all_gather(ln2_gain, ("dp", "fsdp"), axis=0, tiled=True),
        lax.all_gather(ln2_bias, ("dp", "fsdp"), axis=0, tiled=True),
    )
    long_hidden, long_normed, long_kept = group_forward(long_x, long_len, dense_set)
    short_hidden, short_normed, short_kept = group_forward(short_x, short_len, dense_set)
    model_width = long_x.shape[2]
    long_count = long_x.shape[0] * long_x.shape[1]
    hidden = jnp.concatenate(
        [long_hidden.reshape(long_count, model_width), short_hidden.reshape(-1, model_width)], 0
    )
    normed = jnp.concatenate(
        [long_normed.reshape(long_count, model_width), short_normed.reshape(-1, model_width)], 0
    )
    groups = lax.axis_size("fsdp")
    owned_count = w_up.shape[0]
    experts = owned_count * groups
    row_count = hidden.shape[0]
    capacity = 4 * row_count // (3 * experts)
    received_rows = groups * capacity
    chosen = expert_ids[:, 0]
    onehot = (chosen[:, None] == jnp.arange(experts, dtype=jnp.int32)[None, :]).astype(jnp.int32)
    slot_rank = jnp.sum(jnp.cumsum(onehot, 0) * onehot, 1) - 1
    flat_slot = chosen * capacity + slot_rank
    source = (
        jnp.full((experts * capacity,), row_count, jnp.int32)
        .at[flat_slot]
        .set(jnp.arange(row_count, dtype=jnp.int32))
    )

    def to_slots(token_rows):
        padded = jnp.concatenate([token_rows, jnp.zeros((1, model_width), token_rows.dtype)], 0)
        return padded[source].reshape(groups, owned_count, capacity, model_width)

    def from_slots(slot_rows):
        return slot_rows.reshape(experts * capacity, model_width)[flat_slot]

    arrived = lax.all_to_all(
        to_slots(normed), "fsdp", split_axis=0, concat_axis=2, tiled=True
    ).reshape(owned_count, received_rows, model_width)
    up_full, down_full = (
        lax.all_gather(w_up, "dp", axis=2, tiled=True),
        lax.all_gather(w_down, "dp", axis=1, tiled=True),
    )
    pre_act = jnp.einsum("erd,edf->erf", arrived, up_full, preferred_element_type=jnp.float32)
    activated = jax.nn.gelu(pre_act).astype(jnp.bfloat16)
    result = jnp.einsum(
        "erf,efd->erd", activated, down_full, preferred_element_type=jnp.float32
    ).astype(jnp.bfloat16)
    returned = lax.all_to_all(
        result.reshape(1, owned_count, received_rows, model_width),
        "fsdp",
        split_axis=2,
        concat_axis=0,
        tiled=True,
    )
    mixed_out = hidden + from_slots(returned).astype(jnp.float32)
    long_out = mixed_out[:long_count].reshape(long_x.shape)
    short_out = mixed_out[long_count:].reshape(short_x.shape)
    grad_out = jnp.concatenate(
        [long_cot.reshape(long_count, model_width), short_cot.reshape(-1, model_width)], 0
    )
    grad_arrived = lax.all_to_all(
        to_slots(grad_out.astype(jnp.bfloat16)), "fsdp", split_axis=0, concat_axis=2, tiled=True
    ).reshape(owned_count, received_rows, model_width)
    grad_act = jnp.einsum(
        "erd,efd->erf", grad_arrived, down_full, preferred_element_type=jnp.float32
    )
    grad_pre = gelu_back(pre_act, grad_act).astype(jnp.bfloat16)
    grad_slots = jnp.einsum(
        "erf,edf->erd", grad_pre, up_full, preferred_element_type=jnp.float32
    ).astype(jnp.bfloat16)
    grad_up_all = jnp.einsum("erd,erf->edf", arrived, grad_pre, preferred_element_type=jnp.float32)
    grad_down_all = jnp.einsum(
        "erf,erd->efd", activated, grad_arrived, preferred_element_type=jnp.float32
    )
    grad_up, grad_down = (
        lax.psum_scatter(
            grad_up_all.astype(jnp.bfloat16), "dp", scatter_dimension=2, tiled=True
        ).astype(jnp.float32),
        lax.psum_scatter(
            grad_down_all.astype(jnp.bfloat16), "dp", scatter_dimension=1, tiled=True
        ).astype(jnp.float32),
    )
    grad_back = lax.all_to_all(
        grad_slots.reshape(1, owned_count, received_rows, model_width),
        "fsdp",
        split_axis=2,
        concat_axis=0,
        tiled=True,
    )
    grad_normed = from_slots(grad_back).astype(jnp.float32)
    back_set = (
        lax.all_gather(ln1_gain, ("dp", "fsdp"), axis=0, tiled=True),
        lax.all_gather(ln1_bias, ("dp", "fsdp"), axis=0, tiled=True),
        lax.all_gather(w_qkv, ("dp", "fsdp"), axis=0, tiled=True),
        lax.all_gather(w_proj, ("dp", "fsdp"), axis=1, tiled=True),
        lax.all_gather(ln2_gain, ("dp", "fsdp"), axis=0, tiled=True),
        lax.all_gather(ln2_bias, ("dp", "fsdp"), axis=0, tiled=True),
    )
    long_grad, long_terms = group_backward(
        long_kept, long_cot, grad_normed[:long_count].reshape(long_x.shape), long_len, back_set
    )
    short_grad, short_terms = group_backward(
        short_kept, short_cot, grad_normed[long_count:].reshape(short_x.shape), short_len, back_set
    )
    summed = tuple(
        (long_term + short_term for long_term, short_term in zip(long_terms, short_terms))
    )
    owned_grads = (
        lax.psum_scatter(summed[0], ("dp", "fsdp"), scatter_dimension=0, tiled=True),
        lax.psum_scatter(summed[1], ("dp", "fsdp"), scatter_dimension=0, tiled=True),
        lax.psum_scatter(summed[2], ("dp", "fsdp"), scatter_dimension=0, tiled=True),
        lax.psum_scatter(summed[3], ("dp", "fsdp"), scatter_dimension=1, tiled=True),
        lax.psum_scatter(summed[4], ("dp", "fsdp"), scatter_dimension=0, tiled=True),
        lax.psum_scatter(summed[5], ("dp", "fsdp"), scatter_dimension=0, tiled=True),
    )
    return (
        long_out,
        short_out,
        long_grad,
        short_grad,
        owned_grads[0],
        owned_grads[1],
        owned_grads[2],
        owned_grads[3],
        owned_grads[4],
        owned_grads[5],
        grad_up,
        grad_down,
    )


def solution(mesh):
    return jax.shard_map(
        on_device,
        mesh=mesh,
        in_specs=(
            P(("dp", "fsdp"), None, None),
            P(("dp", "fsdp"), None, None),
            P(("dp", "fsdp")),
            P(("dp", "fsdp")),
            P(("dp", "fsdp"), None),
            P(("dp", "fsdp")),
            P(("dp", "fsdp")),
            P(("dp", "fsdp"), None),
            P(None, ("dp", "fsdp")),
            P(("dp", "fsdp")),
            P(("dp", "fsdp")),
            P("fsdp", None, "dp"),
            P("fsdp", "dp", None),
            P(("dp", "fsdp"), None, None),
            P(("dp", "fsdp"), None, None),
        ),
        out_specs=(
            P(("dp", "fsdp"), None, None),
            P(("dp", "fsdp"), None, None),
            P(("dp", "fsdp"), None, None),
            P(("dp", "fsdp"), None, None),
            P(("dp", "fsdp")),
            P(("dp", "fsdp")),
            P(("dp", "fsdp"), None),
            P(None, ("dp", "fsdp")),
            P(("dp", "fsdp")),
            P(("dp", "fsdp")),
            P("fsdp", None, "dp"),
            P("fsdp", "dp", None),
        ),
        check_vma=False,
    )
```

profile of v0, /device:TPU:12, one launch (start us, length us, event | category | flops | bytes accessed | tf_op | source)
XLA Modules:
  0.0 896.0 jit_solution(244129087365759414)
XLA Ops:
  13.7 41.4 %all-reduce.12 = (bf16[768]{0:T(1024)(128)(2,1)S(1)}, bf16[768]{0:T(1024)(128)(2,1)S(1)}, bf16[768]{0:T(1024)(128)(2,1)S(1)}, bf16[768]{0:T(1024)(128)(2,1)S(1)}) all-reduce(bf16[768]{0:T(1024)(128)(2,1)S(1)} %dynamic-update-slice.15, bf16[768]{0:T(1024)(128)(2,1)S(1)} %dynamic-update-slice.14, ...), channel_id=1, replica_groups=mesh['dp'=4,'fsdp'=8] {'dp','fsdp'}, use_global_device_ids=true, to_apply=%add.4 | all-reduce | flops 3072 | bytes 12288
  82.1 7.9 convolution_convert_fusion
  101.5 11.0 %fusion.17 = (f32[12,512]{1,0:T(8,128)S(1)}, f32[12,512,1024]{2,1,0:T(8,128)}) fusion(pred[512,1024]{1,0:T(8,128)(4,1)S(1)} %copy-done.28, bf16[1,1024,3,12,64]{1,4,3,2,0:T(8,128)(2,1)S(1)} %bitcast.363, bf16[1,1024,12,64]{1,3,2,0:T(8,128)(2,1)S(1)} %get-tuple-element.142), kind=kOutput, calls=%fused_computation.43 | convolution fusion | flops 824174592 | bytes 28073984 | tf_op jit(solution)/shard_map/sqhc,skhc->shqk/dot_general | solution.py:40
  112.5 12.3 %fusion.7 = f32[12,512]{1,0:T(8,128)S(1)} fusion(f32[12,512]{1,0:T(8,128)S(1)} %get-tuple-element.145, f32[12,512,1024]{2,1,0:T(8,128)} %get-tuple-element.146, pred[512,1024]{1,0:T(8,128)(4,1)S(1)} %copy-done.28), kind=kLoop, calls=%fused_computation.21 | loop fusion | flops 25159680 | bytes 25739264 | tf_op jit(solution)/shard_map/reduce_sum | solution.py:65
  128.2 9.2 %fusion.102 = bf16[12,64,512]{2,1,0:T(8,128)(2,1)} fusion(f32[12,512]{1,0:T(8,128)S(1)} %fusion.7, f32[12,512]{1,0:T(8,128)S(1)} %get-tuple-element.145, f32[12,512,1024]{2,1,0:T(8,128)S(1)} %copy-done, pred[512,1024]{1,0:T(8,128)(4,1)S(1)} %copy-done.28, bf16[1,1024,3,12,64]{1,4,3,2,0:T(8,128)(2,1)S(1)} %bitcast.364), kind=kOutput, calls=%fused_computation.165 | convolution fusion | flops 837156864 | bytes 28114944 | tf_op jit(solution)/shard_map/shqk,skhc->sqhc/dot_general | solution.py:68
  171.9 9.4 %gather_fusion = bf16[2048,768]{1,0:T(8,128)(2,1)} fusion(bf16[1537,768]{1,0:T(8,128)(2,1)S(1)} %maximum_maximum_fusion, s32[2048]{0:T(1024)S(1)} %fusion.127), kind=kCustom, calls=%fused_computation | custom fusion | bytes 6299648 | tf_op jit(solution)/shard_map/gather | solution.py:271
  188.9 9.4 %gather_fusion.2 = bf16[2048,768]{1,0:T(8,128)(2,1)} fusion(bf16[1537,768]{1,0:T(8,128)(2,1)S(1)} %fusion.65, s32[2048]{0:T(1024)S(1)} %fusion.127), kind=kCustom, calls=%fused_computation.2 | custom fusion | bytes 6299648 | tf_op jit(solution)/shard_map/gather | solution.py:271
  198.3 24.4 %all-to-all-done = bf16[8,1,256,768]{3,2,1,0:T(8,128)(2,1)} async-done(((bf16[8,1,256,768]{3,2,1,0:T(8,128)(2,1)}), bf16[8,1,256,768]{3,2,1,0:T(8,128)(2,1)}, u32[]{:S(2)}, u32[]{:S(2)}) %all-to-all-start) | async-done | bytes 3145760 | tf_op jit(solution)/shard_map/all_to_all | solution.py:276
  228.6 24.3 %multiply_convert_fusion.1 = (bf16[2048,3072]{1,0:T(8,128)(2,1)}, f32[2048,3072]{1,0:T(8,128)}) fusion(bf16[2048,768]{1,0:T(8,128)(2,1)} %bitcast.35, bf16[1,768,3072]{2,1,0:T(8,128)(2,1)} %all-gather.9.cloned.1.call-done), kind=kOutput, calls=%fused_computation.17 | convolution fusion | flops 9720299520 | bytes 45613056 | tf_op jit(solution)/shard_map/erd,edf->erf/dot_general | solution.py:283
  252.8 11.5 %all-to-all-done.2 = bf16[8,1,256,768]{3,2,1,0:T(8,128)(2,1)S(1)} async-done(((bf16[8,1,256,768]{3,2,1,0:T(8,128)(2,1)}), bf16[8,1,256,768]{3,2,1,0:T(8,128)(2,1)S(1)}, u32[]{:S(2)}, u32[]{:S(2)}) %all-to-all-start.2) | async-done | bytes 3145760 | tf_op jit(solution)/shard_map/all_to_all | solution.py:301
  264.4 14.5 %fusion.39 = bf16[1,3072,768]{2,1,0:T(8,128)(2,1)} fusion(bf16[2048,3072]{1,0:T(8,128)(2,1)} %get-tuple-element.153, bf16[2048,768]{1,0:T(8,128)(2,1)S(1)} %bitcast.384), kind=kOutput, calls=%fused_computation.68 | convolution fusion | flops 9666035712 | bytes 20447232 | tf_op jit(solution)/shard_map/erf,erd->efd/dot_general | solution.py:312
  278.9 26.0 %all-gather.11.cloned.1.call-done = bf16[1,3072,768]{2,1,0:T(8,128)(2,1)} async-done(((bf16[1,768,768]{2,1,0:T(8,128)(2,1)}), bf16[1,3072,768]{2,1,0:T(8,128)(2,1)}) %all-gather.11.cloned.1.call-update) | async-done | bytes 4718608 | tf_op jit(solution)/shard_map/all_gather | solution.py:281
  304.9 27.6 %fusion.6 = bf16[2048,3072]{1,0:T(8,128)(2,1)} fusion(f32[2048,3072]{1,0:T(8,128)} %get-tuple-element.154, bf16[2048,768]{1,0:T(8,128)(2,1)S(1)} %bitcast.385, bf16[1,3072,768]{2,1,0:T(8,128)(2,1)} %all-gather.11.cloned.1.call-done), kind=kOutput, calls=%fused_computation.13 | convolution fusion | flops 9789505536 | bytes 45613056 | tf_op jit(solution)/shard_map/erd,efd->erf/dot_general | solution.py:304
  332.5 14.3 %fusion.61 = bf16[1,1,2048,768]{3,2,1,0:T(8,128)(2,1)S(1)} fusion(bf16[2048,3072]{1,0:T(8,128)(2,1)} %fusion.6, bf16[1,768,3072]{2,1,0:T(8,128)(2,1)} %all-gather.9.cloned.1.call-done), kind=kOutput, calls=%fused_computation.102 | convolution fusion | flops 9665249280 | bytes 20447232 | tf_op jit(solution)/shard_map/erf,edf->erd/dot_general | solution.py:308
  346.8 44.7 %copy.102 = bf16[1,1,2048,768]{3,1,0,2:T(2,128)(2,1)} copy(bf16[1,1,2048,768]{3,2,1,0:T(8,128)(2,1)S(1)} %fusion.61) | data formatting | bytes 6291456 | tf_op jit(solution)/shard_map/reshape | solution.py:324
  392.1 31.8 %reduce.61 = bf16[2048,768]{1,0:T(8,128)(2,1)S(1)} reduce(bf16[2048,1,1,768]{3,2,1,0:T(2,128)(2,1)} %bitcast.365, bf16[]{:T(256)} %broadcast.771), dimensions={1,2}, to_apply=%bitcast.343.reduce_sub_computation | reduce | bytes 6291458
  432.5 15.4 %fusion.38 = bf16[1,768,3072]{2,1,0:T(8,128)(2,1)} fusion(bf16[2048,768]{1,0:T(8,128)(2,1)} %bitcast.35, bf16[2048,3072]{1,0:T(8,128)(2,1)} %fusion.6), kind=kOutput, calls=%fused_computation.67 | convolution fusion | flops 9666035712 | bytes 20447232 | tf_op jit(solution)/shard_map/erd,erf->edf/dot_general | solution.py:311
  448.0 20.2 %all-to-all-done.3 = bf16[8,2,98304]{2,1,0:T(2,128)(2,1)S(1)} async-done(((bf16[8,2,98304]{2,1,0:T(2,128)(2,1)}), bf16[8,2,98304]{2,1,0:T(2,128)(2,1)S(1)}, u32[]{:S(2)}, u32[]{:S(2)}) %all-to-all-start.3) | async-done | bytes 3145760 | tf_op jit(solution)/shard_map/all_to_all | solution.py:323
  503.3 7.5 multiply_convert_fusion.3
  521.8 11.4 %multiply_reduce_fusion.1 = (f32[12,512]{1,0:T(8,128)S(1)}, f32[12,512,512]{1,2,0:T(8,128)}) fusion(f32[12,512]{1,0:T(8,128)S(1)} %copy-done.73, f32[12,512,512]{1,2,0:T(8,128)} %copy-done.2, pred[512,512]{0,1:T(8,128)(4,1)S(1)} %copy-done.42, bf16[512,12,64]{0,2,1:T(8,128)(2,1)} %bitcast.380, bf16[1,512,3,12,64]{1,4,3,2,0:T(8,128)(2,1)S(1)} %bitcast.371), kind=kOutput, calls=%fused_computation.25 | convolution fusion | flops 418375680 | bytes 27058176 | tf_op jit(solution)/shard_map/sqhc,skhc->shqk/dot_general | solution.py:94
  555.3 18.3 %multiply_reduce_fusion = (f32[12,512]{1,0:T(8,128)S(1)}, f32[12,512,1024]{2,1,0:T(8,128)}) fusion(f32[12,512]{1,0:T(8,128)S(1)} %log_add_fusion.1, f32[12,512,1024]{2,1,0:T(8,128)} %get-tuple-element.146, pred[512,1024]{1,0:T(8,128)(4,1)S(1)} %copy-done.29, bf16[1,1024,3,12,64]{1,4,3,2,0:T(8,128)(2,1)} %bitcast.361, bf16[1,1024,12,64]{1,3,2,0:T(8,128)(2,1)} %bitcast.387), kind=kOutput, calls=%fused_computation.15 | convolution fusion | flops 836757504 | bytes 53264384 | tf_op jit(solution)/shard_map/sqhc,skhc->shqk/dot_general | solution.py:94
  573.6 21.2 %multiply_convert_fusion = bf16[12,512,1024]{2,1,0:T(8,128)(2,1)} fusion(f32[12,512,1024]{2,1,0:T(8,128)} %get-tuple-element.158, f32[12,512]{1,0:T(8,128)S(1)} %get-tuple-element.157, f32[12,512]{1,0:T(8,128)S(1)} %log_add_fusion.1, f32[12,512,1024]{2,1,0:T(8,128)} %get-tuple-element.146, pred[512,1024]{1,0:T(8,128)(4,1)S(1)} %copy-done.29), kind=kLoop, calls=%fused_computation.14 | loop fusion | flops 37748736 | bytes 63488000 | tf_op jit(solution)/shard_map/convert_element_type | solution.py:106
  594.8 10.0 %multiply_bitcast_fusion.3 = bf16[1,512,12,64]{1,3,2,0:T(8,128)(2,1)} fusion(bf16[12,512,1024]{2,1,0:T(8,128)(2,1)} %multiply_convert_fusion, bf16[1,1024,3,12,64]{1,4,3,2,0:T(8,128)(2,1)} %bitcast.362), kind=kOutput, calls=%fused_computation.151 | convolution fusion | flops 806092800 | bytes 14942208 | tf_op jit(solution)/shard_map/shqk,skhc->sqhc/dot_general | solution.py:108
  604.8 7.4 fusion.97
  616.6 13.4 %fusion.48 = bf16[1,1024,1,12,64]{1,4,3,2,0:T(8,128)(2,1)} fusion(f32[1,512,12,64]{1,3,2,0:T(8,128)} %fusion.94, f32[12,512]{1,0:T(8,128)S(1)} %log_add_fusion.1, f32[12,512,1024]{2,1,0:T(8,128)} %get-tuple-element.146, pred[512,1024]{1,0:T(8,128)(4,1)S(1)} %copy-done.29, bf16[1,1024,12,64]{1,3,2,0:T(8,128)(2,1)S(1)} %bitcast.389), kind=kOutput, calls=%fused_computation.79 | convolution fusion | flops 832045056 | bytes 29655040 | tf_op jit(solution)/shard_map/shqk,sqhc->skhc/dot_general | solution.py:98
  633.8 7.9 fusion.49
  654.3 14.4 %fusion.58 = bf16[1,1,2048,768]{3,2,1,0:T(8,128)(2,1)S(1)} fusion(bf16[2048,3072]{1,0:T(8,128)(2,1)} %get-tuple-element.153, bf16[1,3072,768]{2,1,0:T(8,128)(2,1)} %all-gather.11.cloned.1.call-done), kind=kOutput, calls=%fused_computation.101 | convolution fusion | flops 9665249280 | bytes 20447232 | tf_op jit(solution)/shard_map/erf,efd->erd/dot_general | solution.py:285
  668.7 45.1 %copy.103 = bf16[1,1,2048,768]{3,1,0,2:T(2,128)(2,1)} copy(bf16[1,1,2048,768]{3,2,1,0:T(8,128)(2,1)S(1)} %fusion.58) | data formatting | bytes 6291456 | tf_op jit(solution)/shard_map/reshape | solution.py:289
  713.8 31.6 %reduce.60 = bf16[2048,768]{1,0:T(8,128)(2,1)S(1)} reduce(bf16[2048,1,1,768]{3,2,1,0:T(2,128)(2,1)} %bitcast.366, bf16[]{:T(256)} %broadcast.771), dimensions={1,2}, to_apply=%bitcast.344.reduce_sub_computation | reduce | bytes 6291458
  754.3 38.1 %all-to-all-done.1 = bf16[8,2,98304]{2,1,0:T(2,128)(2,1)S(1)} async-done(((bf16[8,2,98304]{2,1,0:T(2,128)(2,1)}), bf16[8,2,98304]{2,1,0:T(2,128)(2,1)S(1)}, u32[]{:S(2)}, u32[]{:S(2)}) %all-to-all-start.1) | async-done | bytes 3145760 | tf_op jit(solution)/shard_map/all_to_all | solution.py:288
  812.7 7.2 fusion.51
  822.0 46.0 %all-reduce.11 = (f32[768]{0:T(1024)S(1)}, f32[768]{0:T(1024)S(1)}, f32[768]{0:T(1024)S(1)}, f32[768]{0:T(1024)S(1)}) all-reduce(f32[768]{0:T(1024)S(1)} %add.263, f32[768]{0:T(1024)S(1)} %add.264, f32[768]{0:T(1024)S(1)} %add.267, f32[768]{0:T(1024)S(1)} %add.268), channel_id=2, replica_groups=mesh['dp'=4,'fsdp'=8] {'dp','fsdp'}, use_global_device_ids=true, to_apply=%region_31.32.clone | all-reduce | flops 3072 | bytes 24576
  (402 shorter events, 243.8 us)
Async XLA Ops:
  7.2 64.7 %all-gather.5.cloned.1.call-start = ((), (), s32[]{:S(2)}) async-start(), calls=%async_computation.8 | async-start | bytes 3649536 | tf_op jit(solution)/shard_map/all_gather | solution.py:238
  8.0 156.2 %all-gather.7.cloned.1.call-start = ((), (), s32[]{:S(2)}) async-start(), calls=%async_computation.9 | async-start | bytes 1216512 | tf_op jit(solution)/shard_map/all_gather | solution.py:239
  8.7 219.8 %all-gather.9.cloned.1.call-start = ((), (), s32[]{:S(2)}) async-start(), calls=%async_computation.10 | async-start | bytes 5898240 | tf_op jit(solution)/shard_map/all_gather | solution.py:280
  12.4 59.5 %copy-start.92 = (f32[512]{0:T(512)}, f32[512]{0:T(512)S(1)}, u32[]{:S(2)}) copy-start(f32[512]{0:T(512)S(1)} %broadcast_multiply_fusion.11) | copy-start | bytes 6148
  12.7 59.2 %copy-start.99 = (f32[512]{0:T(512)}, f32[512]{0:T(512)S(1)}, u32[]{:S(2)}) copy-start(f32[512]{0:T(512)S(1)} %add_rsqrt_fusion.3) | copy-start | bytes 6148
  55.1 27.0 %copy-start.106 = (f32[768]{0:T(1024)}, f32[768]{0:T(1024)S(1)}, u32[]{:S(2)}) copy-start(f32[768]{0:T(1024)S(1)} %convert_element_type.214) | copy-start | bytes 9220
  55.1 27.0 %copy-start.74 = (f32[768]{0:T(1024)}, f32[768]{0:T(1024)S(1)}, u32[]{:S(2)}) copy-start(f32[768]{0:T(1024)S(1)} %convert_element_type.213) | copy-start | bytes 9220
  55.1 114.9 %copy-start.65 = (f32[768]{0:T(1024)}, f32[768]{0:T(1024)S(1)}, u32[]{:S(2)}) copy-start(f32[768]{0:T(1024)S(1)} %convert_element_type.227) | copy-start | bytes 9220
  57.3 24.8 %copy-start.90 = (f32[1024]{0:T(1024)}, f32[1024]{0:T(1024)S(1)}, u32[]{:S(2)}) copy-start(f32[1024]{0:T(1024)S(1)} %broadcast_multiply_fusion.5) | copy-start | bytes 12292
  59.7 22.4 %copy-start.104 = (f32[1024]{0:T(1024)}, f32[1024]{0:T(1024)S(1)}, u32[]{:S(2)}) copy-start(f32[1024]{0:T(1024)S(1)} %add_rsqrt_fusion.1) | copy-start | bytes 12292
  62.7 14.7 %copy-start.94 = (s32[1536]{0:T(1024)}, s32[1536]{0:T(1024)S(1)}, u32[]{:S(2)}) copy-start(s32[1536]{0:T(1024)S(1)} %fusion.128) | copy-start | bytes 18436
  101.5 11.0 %copy-start.22 = (bf16[1,1024,12,64]{1,3,2,0:T(8,128)(2,1)}, bf16[1,1024,12,64]{1,3,2,0:T(8,128)(2,1)S(1)}, u32[]{:S(2)}) copy-start(bf16[1,1024,12,64]{1,3,2,0:T(8,128)(2,1)S(1)} %get-tuple-element.142) | copy-start | bytes 4718596
  112.5 12.3 %copy-start.67 = (f32[12,512]{1,0:T(8,128)}, f32[12,512]{1,0:T(8,128)S(1)}, u32[]{:S(2)}) copy-start(f32[12,512]{1,0:T(8,128)S(1)} %get-tuple-element.145) | copy-start | bytes 73732
  112.5 15.7 %copy-start = (f32[12,512,1024]{2,1,0:T(8,128)S(1)}, f32[12,512,1024]{2,1,0:T(8,128)}, u32[]{:S(2)}) copy-start(f32[12,512,1024]{2,1,0:T(8,128)} %get-tuple-element.146) | copy-start | bytes 75497472
  181.3 41.4 %all-to-all-start = ((bf16[8,1,256,768]{3,2,1,0:T(8,128)(2,1)}), bf16[8,1,256,768]{3,2,1,0:T(8,128)(2,1)}, u32[]{:S(2)}, u32[]{:S(2)}) async-start(bf16[8,1,256,768]{3,2,1,0:T(8,128)(2,1)} %bitcast.374), calls=%async_computation | async-start | bytes 6291456 | tf_op jit(solution)/shard_map/all_to_all | solution.py:276
  186.2 118.7 %all-gather.11.cloned.1.call-start = ((), (), s32[]{:S(2)}) async-start(), calls=%async_computation.11 | async-start | bytes 5898240 | tf_op jit(solution)/shard_map/all_gather | solution.py:281
  222.7 41.6 %all-to-all-start.2 = ((bf16[8,1,256,768]{3,2,1,0:T(8,128)(2,1)}), bf16[8,1,256,768]{3,2,1,0:T(8,128)(2,1)S(1)}, u32[]{:S(2)}, u32[]{:S(2)}) async-start(bf16[8,1,256,768]{3,2,1,0:T(8,128)(2,1)} %bitcast.375), calls=%async_computation.2 | async-start | bytes 6291456 | tf_op jit(solution)/shard_map/all_to_all | solution.py:301
  227.9 655.3 %reduce-scatter.11.cloned.1.call-start = ((), (), s32[]{:S(2)}) async-start(), calls=%async_computation.15 | async-start | bytes 5898240 | tf_op jit(solution)/shard_map/reduce_scatter | solution.py:319
  427.4 40.8 %all-to-all-start.3 = ((bf16[8,2,98304]{2,1,0:T(2,128)(2,1)}), bf16[8,2,98304]{2,1,0:T(2,128)(2,1)S(1)}, u32[]{:S(2)}, u32[]{:S(2)}) async-start(bf16[8,2,98304]{2,1,0:T(2,128)(2,1)} %reshape.1286), calls=%async_computation.3 | async-start | bytes 6291456 | tf_op jit(solution)/shard_map/all_to_all | solution.py:323
  431.8 454.3 %reduce-scatter.9.cloned.1.call-start = ((), (), s32[]{:S(2)}) async-start(), calls=%async_computation.14 | async-start | bytes 5898240 | tf_op jit(solution)/shard_map/reduce_scatter | solution.py:316
  447.9 441.0 %reduce-scatter.7.cloned.1.call-start = ((), (), s32[]{:S(2)}) async-start(), calls=%async_computation.13 | async-start | bytes 2433024 | tf_op jit(solution)/shard_map/reduce_scatter | solution.py:352
  493.3 10.0 %copy-start.53 = (bf16[1024,768]{0,1:T(8,128)(2,1)}, bf16[1024,768]{0,1:T(8,128)(2,1)S(1)}, u32[]{:S(2)}) copy-start(bf16[1024,768]{0,1:T(8,128)(2,1)S(1)} %convolution_convert_fusion.4) | copy-start | bytes 4718596
  521.8 11.5 %slice-start.6 = ((s8[12582912]{0:T(1024)(128)(4,1)}), s8[4194304]{0:T(1024)(128)(4,1)S(1)}, s32[]{:S(2)}) async-start(s8[12582912]{0:T(1024)(128)(4,1)} %bitcast.354), calls=%async_computation.22 | async-start | bytes 8388608
  521.8 11.5 %slice-start.7 = ((s8[12582912]{0:T(1024)(128)(4,1)}), s8[4194304]{0:T(1024)(128)(4,1)S(1)}, s32[]{:S(2)}) async-start(s8[12582912]{0:T(1024)(128)(4,1)} %bitcast.354), calls=%async_computation.23 | async-start | bytes 8388608
  521.8 12.9 %slice-start.8 = ((s8[12582912]{0:T(1024)(128)(4,1)}), s8[4194304]{0:T(1024)(128)(4,1)S(1)}, s32[]{:S(2)}) async-start(s8[12582912]{0:T(1024)(128)(4,1)} %bitcast.354), calls=%async_computation.24 | async-start | bytes 8388608
  594.8 10.0 %copy-start.50 = (bf16[512,768]{0,1:T(8,128)(2,1)S(1)}, bf16[512,768]{0,1:T(8,128)(2,1)}, u32[]{:S(2)}) copy-start(bf16[512,768]{0,1:T(8,128)(2,1)} %copy.80) | copy-start | bytes 2359300
  594.8 17.4 %slice-start.3 = ((s8[12582912]{0:T(1024)(128)(4,1)}), s8[4194304]{0:T(1024)(128)(4,1)S(1)}, s32[]{:S(2)}) async-start(s8[12582912]{0:T(1024)(128)(4,1)} %bitcast.352), calls=%async_computation.19 | async-start | bytes 8388608
  594.8 17.4 %slice-start.4 = ((s8[12582912]{0:T(1024)(128)(4,1)}), s8[4194304]{0:T(1024)(128)(4,1)S(1)}, s32[]{:S(2)}) async-start(s8[12582912]{0:T(1024)(128)(4,1)} %bitcast.352), calls=%async_computation.20 | async-start | bytes 8388608
  630.1 258.8 %reduce-scatter.5.cloned.1.call-start = ((), (), s32[]{:S(2)}) async-start(), calls=%async_computation.12 | async-start | bytes 7299072 | tf_op jit(solution)/shard_map/reduce_scatter | solution.py:351
  633.7 15.3 %copy-start.37 = (bf16[1,512,3,12,64]{1,4,3,2,0:T(8,128)(2,1)}, bf16[1,512,3,12,64]{1,4,3,2,0:T(8,128)(2,1)S(1)}, u32[]{:S(2)}) copy-start(bf16[1,512,3,12,64]{1,4,3,2,0:T(8,128)(2,1)S(1)} %maximum_convert_fusion.1) | copy-start | bytes 7077892
  749.0 43.4 %all-to-all-start.1 = ((bf16[8,2,98304]{2,1,0:T(2,128)(2,1)}), bf16[8,2,98304]{2,1,0:T(2,128)(2,1)S(1)}, u32[]{:S(2)}, u32[]{:S(2)}) async-start(bf16[8,2,98304]{2,1,0:T(2,128)(2,1)} %reshape.1284), calls=%async_computation.1 | async-start | bytes 6291456 | tf_op jit(solution)/shard_map/all_to_all | solution.py:288
  819.9 50.5 %copy-start.6 = (f32[1,1024,768]{2,1,0:T(8,128)S(1)}, f32[1,1024,768]{2,1,0:T(8,128)}, u32[]{:S(2)}) copy-start(f32[1,1024,768]{2,1,0:T(8,128)} %copy-done.4) | copy-start | bytes 9437188
  (103 other events, 404.0 us)
Sparse Core Ops, SparseCore 0:
  11.0 60.9 all-gather.4
  74.8 52.4 all-gather.6
  128.8 86.7 all-gather.8
  217.1 87.8 all-gather.10
  307.1 86.2 reduce-scatter.10
  448.0 86.3 reduce-scatter.8
  630.2 99.3 reduce-scatter.6
  736.8 121.1 reduce-scatter.4
where the time goes:
time: 903 us; the launch traced here: 896 us
  matrix products  285 us (32%)
  local copies, waits for them, and re-layouts  203 us (22%)
  other arithmetic  161 us (18%)
  waiting for transfers between devices  123 us (14%)
  blocking collectives  87.5 us (10%)
  starting transfers between devices  20 us (2%)
  between operations  17.2 us (2%)
    unnamed x2, blocking collectives  87.5 us
    unnamed x7, other arithmetic  63.5 us
    unnamed x265, local copies, waits for them, and re-layouts  54.9 us
    reshape x1, local copies, waits for them, and re-layouts, on_device(): result.reshape(1, owned_count, received_rows, model_width)  45.1 us
    reshape x1, local copies, waits for them, and re-layouts, on_device(): grad_slots.reshape(1, owned_count, received_rows, model_width)  44.7 us
    all_to_all x1, waiting for transfers between devices, on_device(): lax.all_to_all(result.reshape(1, owned_count, received_rows, model_width)...  38.1 us
    dot_general x3, matrix products, attend_back(): jnp.einsum('sqhc,skhc->shqk', grad_block, values[:, :stop_row], preferred...  36.6 us
    convert_element_type x3, other arithmetic, attend_back(): grad_scores = (probability * (grad_prob - centre)).astype(jnp.bfloat16)  35.7 us
  transfers between devices with their start and end apart: 12, of which 6 were waited for; matrix products, arithmetic and copies ran while one was open for 69% of the time, Pallas kernels for 0%

commit v1 on v0

v1 whole, which is shorter than its diff:
```python
import functools

import jax
import jax.numpy as jnp
from jax import lax
from jax.experimental import pallas as pl
from jax.experimental.pallas import tpu as pltpu
from jax.sharding import PartitionSpec as P

MESH = pl.DeviceIdType.MESH
HEAD_DIM = 64
EPSILON = 1e-05
MASKED = -1e30
BF16 = jnp.bfloat16
F32 = jnp.float32
LANES = 128
ROWS = 512
BLOCK = 256
VMEM_LIMIT = 60 * 2**20

NN = (((1,), (0,)), ((), ()))
NT = (((1,), (1,)), ((), ()))
TN = (((0,), (0,)), ((), ()))


def dot(a, b, dims=NN, precision=None):
    return lax.dot_general(a, b, dims, preferred_element_type=F32, precision=precision)


def params(**extra):
    return pltpu.CompilerParams(vmem_limit_bytes=VMEM_LIMIT, **extra)


def cost(flops, moved, exps=0):
    return pl.CostEstimate(flops=int(flops), bytes_accessed=int(moved), transcendentals=int(exps))


def constant(shape):
    return pl.BlockSpec(shape, lambda *_: (0,) * len(shape), pipeline_mode=pl.Buffered(1))


def norm_parts(inputs):
    average = jnp.mean(inputs, -1, keepdims=True)
    centred = inputs - average
    inv_scale = lax.rsqrt(jnp.mean(centred * centred, -1, keepdims=True) + EPSILON)
    return centred * inv_scale, inv_scale


def norm_back(grad_normed, normed, inv_scale):
    centre_term = jnp.mean(grad_normed, -1, keepdims=True)
    slope_term = jnp.mean(grad_normed * normed, -1, keepdims=True)
    return inv_scale * (grad_normed - centre_term - normed * slope_term)


def vectors(vec_ref):
    return jnp.transpose(vec_ref[...].astype(F32))[:8]


def long_short(width, n_long):
    return [
        pl.BlockSpec((ROWS, width), lambda i: (jnp.minimum(i, n_long - 1), 0)),
        pl.BlockSpec((ROWS, width), lambda i: (jnp.maximum(i - n_long, 0), 0)),
    ]


def gather_kernel(n_dp, n_f, own_ref, out_ref, z_send, z_recv, p_send, p_recv, c_send, c_recv, l_sem):
    z = lax.axis_index("dp")
    f = lax.axis_index("fsdp")
    half = n_f // 2
    partner = f + 1 - 2 * lax.rem(f, 2)
    barrier = pltpu.get_barrier_semaphore()
    for k in range(1, n_dp):
        pl.semaphore_signal(barrier, 1, device_id=(lax.rem(z + k, n_dp), f), device_id_type=MESH)
    for k in range(1, half):
        pl.semaphore_signal(barrier, 1, device_id=(z, lax.rem(f + 2 * k, n_f)), device_id_type=MESH)
    pl.semaphore_signal(barrier, 1, device_id=(z, partner), device_id_type=MESH)
    local = pltpu.make_async_copy(own_ref, out_ref.at[z, f], l_sem)
    local.start()
    pl.semaphore_wait(barrier, n_dp - 1 + half)

    z_copies = []
    for k in range(1, n_dp):
        copy = pltpu.make_async_remote_copy(
            own_ref, out_ref.at[z, f], z_send.at[k], z_recv.at[k],
            device_id=(lax.rem(z + k, n_dp), f), device_id_type=MESH,
        )
        copy.start()
        z_copies.append(copy)
    local.wait()
    for copy in z_copies:
        copy.wait_recv()
    p_copies = []
    for k in range(1, half):
        copy = pltpu.make_async_remote_copy(
            out_ref.at[:, f], out_ref.at[:, f], p_send.at[k], p_recv.at[k],
            device_id=(z, lax.rem(f + 2 * k, n_f)), device_id_type=MESH,
        )
        copy.start()
        p_copies.append(copy)
    c_copies = []
    for k in range(half):
        if k:
            p_copies[k - 1].wait_recv()
        column = lax.rem(f + n_f - 2 * k, n_f)
        copy = pltpu.make_async_remote_copy(
            out_ref.at[:, column], out_ref.at[:, column], c_send.at[k], c_recv.at[k],
            device_id=(z, partner), device_id_type=MESH,
        )
        copy.start()
        c_copies.append(copy)
    for copy in c_copies:
        copy.wait_recv()
    for copy in z_copies + p_copies + c_copies:
        copy.wait_send()


def gather_dense(own, n_dp, n_f):
    return pl.pallas_call(
        functools.partial(gather_kernel, n_dp, n_f),
        out_shape=jax.ShapeDtypeStruct((n_dp, n_f) + own.shape, own.dtype),
        in_specs=[pl.BlockSpec(memory_space=pl.ANY)],
        out_specs=pl.BlockSpec(memory_space=pl.ANY),
        scratch_shapes=[
            pltpu.SemaphoreType.DMA((n_dp,)),
            pltpu.SemaphoreType.DMA((n_dp,)),
            pltpu.SemaphoreType.DMA((n_f // 2,)),
            pltpu.SemaphoreType.DMA((n_f // 2,)),
            pltpu.SemaphoreType.DMA((n_f // 2,)),
            pltpu.SemaphoreType.DMA((n_f // 2,)),
            pltpu.SemaphoreType.DMA,
        ],
        compiler_params=pltpu.CompilerParams(collective_id=0, has_side_effects=True),
        cost_estimate=cost(0, 100e6),
        name="gather_dense",
    )(own)


def scatter_kernel(
    n_dp, n_f, in_ref, out_ref, got1, sum1, got2, sum2, got3,
    c_send, c_recv, p_send, p_recv, z_send, z_recv,
):
    z = lax.axis_index("dp")
    f = lax.axis_index("fsdp")
    half = n_f // 2
    parity = lax.rem(f, 2)
    mine = f // 2
    partner = f + 1 - 2 * parity
    barrier = pltpu.get_barrier_semaphore()
    for k in range(1, n_dp):
        pl.semaphore_signal(barrier, 1, device_id=(lax.rem(z + k, n_dp), f), device_id_type=MESH)
    for k in range(1, half):
        pl.semaphore_signal(barrier, 1, device_id=(z, lax.rem(f + 2 * k, n_f)), device_id_type=MESH)
    pl.semaphore_signal(barrier, 1, device_id=(z, partner), device_id_type=MESH)
    pl.semaphore_wait(barrier, n_dp - 1 + half)

    c_copies = []
    order = list(range(1, half)) + [0]
    for k in order:
        slot = lax.rem(mine + k, half)
        copy = pltpu.make_async_remote_copy(
            in_ref.at[:, 2 * slot + 1 - parity], got1.at[slot], c_send.at[k], c_recv.at[k],
            device_id=(z, partner), device_id_type=MESH,
        )
        copy.start()
        c_copies.append(copy)
    p_copies = []
    for k, c_copy in zip(order, c_copies):
        c_copy.wait_recv()
        slot = lax.rem(mine + k, half)
        sum1[slot] = (in_ref[:, 2 * slot + parity].astype(F32) + got1[slot].astype(F32)).astype(BF16)
        if k:
            copy = pltpu.make_async_remote_copy(
                sum1.at[slot], got2.at[k], p_send.at[k], p_recv.at[k],
                device_id=(z, lax.rem(f + 2 * k, n_f)), device_id_type=MESH,
            )
            copy.start()
            p_copies.append(copy)
    for copy in p_copies:
        copy.wait_recv()
    total = sum1[mine].astype(F32)
    for k in range(1, half):
        total = total + got2[k].astype(F32)
    sum2[...] = total.astype(BF16)
    z_copies = []
    for k in range(1, n_dp):
        there = lax.rem(z + k, n_dp)
        copy = pltpu.make_async_remote_copy(
            sum2.at[there], got3.at[k], z_send.at[k], z_recv.at[k],
            device_id=(there, f), device_id_type=MESH,
        )
        copy.start()
        z_copies.append(copy)
    for copy in z_copies:
        copy.wait_recv()
    total = sum2[z].astype(F32)
    for k in range(1, n_dp):
        total = total + got3[k].astype(F32)
    out_ref[...] = total
    for copy in c_copies + p_copies + z_copies:
        copy.wait_send()


def scatter_dense(grads, n_dp, n_f):
    block = grads.shape[2:]
    half = n_f // 2
    return pl.pallas_call(
        functools.partial(scatter_kernel, n_dp, n_f),
        out_shape=jax.ShapeDtypeStruct(block, F32),
        in_specs=[pl.BlockSpec(memory_space=pltpu.VMEM)],
        out_specs=pl.BlockSpec(memory_space=pltpu.VMEM),
        scratch_shapes=[
            pltpu.VMEM((half, n_dp) + block, BF16),
            pltpu.VMEM((half, n_dp) + block, BF16),
            pltpu.VMEM((half, n_dp) + block, BF16),
            pltpu.VMEM((n_dp,) + block, BF16),
            pltpu.VMEM((n_dp,) + block, BF16),
            pltpu.SemaphoreType.DMA((half,)),
            pltpu.SemaphoreType.DMA((half,)),
            pltpu.SemaphoreType.DMA((half,)),
            pltpu.SemaphoreType.DMA((half,)),
            pltpu.SemaphoreType.DMA((n_dp,)),
            pltpu.SemaphoreType.DMA((n_dp,)),
        ],
        compiler_params=params(collective_id=1, has_side_effects=True),
        cost_estimate=cost(0, 100e6),
        name="scatter_dense",
    )(grads)


def dispatch_block(slot_row_ref, rows, block):
    first = block * BLOCK
    slot_id = first + lax.broadcasted_iota(jnp.int32, (BLOCK, 1), 0)
    chosen = (slot_row_ref[0:1, :] == slot_id).astype(F32).astype(BF16)
    return dot(chosen, rows).astype(BF16)


def cot_kernel(n_long, n_rows, cap, ids_ref, long_ref, short_ref, col_ref, row_ref, slots_ref, rows_ref):
    i = pl.program_id(0)

    @pl.when(i == 0)
    def _():
        count = ids_ref.shape[0]
        lane = lax.broadcasted_iota(jnp.int32, (1, LANES), 1)
        onehot = (ids_ref[...] == lane).astype(F32)
        onehot_low = onehot.astype(BF16)
        col = lax.broadcasted_iota(jnp.int32, (1, count), 1)
        base = (lane * cap).astype(F32)
        ones = jnp.ones((8, LANES), F32)
        for start in range(0, count, ROWS):
            row = start + lax.broadcasted_iota(jnp.int32, (ROWS, 1), 0)
            before = dot((col < row).astype(F32).astype(BF16), onehot_low)
            picked = (before + base) * onehot[start : start + ROWS]
            col_ref[start : start + ROWS, :] = jnp.sum(picked, 1, keepdims=True).astype(jnp.int32)
            row_ref[:, start : start + ROWS] = dot(
                ones, picked, NT, precision=lax.Precision.HIGHEST
            ).astype(jnp.int32)

    @pl.when(i < n_long)
    def _():
        rows_ref[pl.ds(pl.multiple_of(i * ROWS, ROWS), ROWS), :] = long_ref[...].astype(BF16)

    @pl.when((i >= n_long) & (i < n_rows))
    def _():
        rows_ref[pl.ds(pl.multiple_of(i * ROWS, ROWS), ROWS), :] = short_ref[...].astype(BF16)

    @pl.when(i >= n_rows)
    def _():
        slots_ref[...] = dispatch_block(row_ref, rows_ref[...], i - n_rows)


def route_cot(ids, long_cot, short_cot, slots, cap):
    width = long_cot.shape[1]
    n_long, n_short = long_cot.shape[0] // ROWS, short_cot.shape[0] // ROWS
    n_rows = n_long + n_short
    count = ids.shape[0]
    return pl.pallas_call(
        functools.partial(cot_kernel, n_long, n_rows, cap),
        grid=(n_rows + slots // BLOCK,),
        in_specs=[
            constant((count, 1)),
            pl.BlockSpec((ROWS, width), lambda i: (jnp.minimum(i, n_long - 1), 0)),
            pl.BlockSpec((ROWS, width), lambda i: (jnp.clip(i - n_long, 0, n_short - 1), 0)),
        ],
        out_specs=[
            pl.BlockSpec((count, 1), lambda i: (0, 0)),
            pl.BlockSpec((8, count), lambda i: (0, 0)),
            pl.BlockSpec((BLOCK, width), lambda i: (jnp.maximum(i - n_rows, 0), 0)),
        ],
        out_shape=[
            jax.ShapeDtypeStruct((count, 1), jnp.int32),
            jax.ShapeDtypeStruct((8, count), jnp.int32),
            jax.ShapeDtypeStruct((slots, width), BF16),
        ],
        scratch_shapes=[pltpu.VMEM((count, width), BF16)],
        compiler_params=params(),
        cost_estimate=cost(2 * slots * count * width, 4 * count * width + 2 * slots * width),
        name="route_cot",
    )(ids, long_cot, short_cot)


def qkv_kernel(n_long, width, long_ref, short_ref, w_ref, vec_ref, qkv_ref, vec_scr):
    i = pl.program_id(0)

    @pl.when(i == 0)
    def _():
        vec_scr[...] = vectors(vec_ref)

    def body(x_ref):
        normed, _ = norm_parts(x_ref[...])
        rows = (normed * vec_scr[0:1, :] + vec_scr[1:2, :]).astype(BF16)
        for part in range(3):
            cut = slice(part * width, (part + 1) * width)
            out = dot(rows, w_ref[:, cut])
            if part == 0:
                out = out * HEAD_DIM ** (-0.5)
            qkv_ref[:, cut] = out.astype(BF16)

    pl.when(i < n_long)(lambda: body(long_ref))
    pl.when(i >= n_long)(lambda: body(short_ref))


def make_qkv(long_x, short_x, dense):
    width = long_x.shape[1]
    n_long, n_short = long_x.shape[0] // ROWS, short_x.shape[0] // ROWS
    count = long_x.shape[0] + short_x.shape[0]
    return pl.pallas_call(
        functools.partial(qkv_kernel, n_long, width),
        grid=(n_long + n_short,),
        in_specs=long_short(width, n_long)
        + [
            constant((width, 3 * width)),
            pl.BlockSpec((width, LANES), lambda i: (0, 4 * width // LANES)),
        ],
        out_specs=pl.BlockSpec((ROWS, 3 * width), lambda i: (i, 0)),
        out_shape=jax.ShapeDtypeStruct((count, 3 * width), BF16),
        scratch_shapes=[pltpu.VMEM((8, width), F32)],
        compiler_params=params(),
        cost_estimate=cost(6 * count * width * width, count * width * 10 + 6 * width * width),
        name="make_qkv",
    )(long_x, short_x, dense, dense)


def sequences(long_shape, short_shape):
    found = []
    start = 0
    for which, (number, length) in enumerate((long_shape, short_shape)):
        for index in range(number):
            found.append((start, length, which, index))
            start += length
    return found


def head_masks():
    lane = lax.broadcasted_iota(jnp.int32, (1, LANES), 1)
    return (lane < HEAD_DIM, lane >= HEAD_DIM)


def attend_kernel(seqs, long_len, short_len, q_ref, k_ref, v_ref, o_ref, lse_ref):
    pair = pl.program_id(0)
    masks = head_masks()
    lane = lax.broadcasted_iota(jnp.int32, (1, LANES), 1)

    @pl.when(pair == 0)
    def _():
        lse_ref[...] = jnp.zeros_like(lse_ref)

    causal = lax.broadcasted_iota(jnp.int32, (BLOCK, BLOCK), 1) <= lax.broadcasted_iota(
        jnp.int32, (BLOCK, BLOCK), 0
    )
    for start, length, which, index in seqs:
        valid = (short_len if which else long_len)[index]
        key_pos = lax.broadcasted_iota(jnp.int32, (1, length), 1)
        bias = jnp.where(key_pos < valid, 0.0, MASKED)
        for first in range(0, length, BLOCK):
            here = slice(start + first, start + first + BLOCK)
            past = slice(start, start + first)
            q = q_ref[here, :]
            outs = []
            stats = jnp.zeros((BLOCK, LANES), F32)
            for head in range(2):
                qh = jnp.where(masks[head], q, jnp.zeros_like(q))
                near = dot(qh, k_ref[here, :], NT) + bias[:, first : first + BLOCK]
                near = jnp.where(causal, near, MASKED)
                top = jnp.max(near, 1, keepdims=True)
                if first:
                    far = dot(qh, k_ref[past, :], NT) + bias[:, :first]
                    top = jnp.maximum(top, jnp.max(far, 1, keepdims=True))
                near = jnp.exp(near - top)
                total = jnp.sum(near, 1, keepdims=True)
                out = dot(near.astype(BF16), v_ref[here, :])
                if first:
                    far = jnp.exp(far - top)
                    total = total + jnp.sum(far, 1, keepdims=True)
                    out = out + dot(far.astype(BF16), v_ref[past, :])
                outs.append(out * (1.0 / total))
                stats = jnp.where(lane == 2 * pair + head, top + jnp.log(total), stats)
            o_ref[here, :] = jnp.where(masks[0], outs[0], outs[1]).astype(BF16)
            lse_ref[here, :] = lse_ref[here, :] + stats


def attend(qkv, long_len, short_len, seqs):
    count, width = qkv.shape[0], qkv.shape[1] // 3
    pairs = width // LANES
    return pl.pallas_call(
        functools.partial(attend_kernel, seqs),
        grid=(pairs,),
        in_specs=[pl.BlockSpec(memory_space=pltpu.SMEM)] * 2
        + [
            pl.BlockSpec((count, LANES), lambda i: (0, i)),
            pl.BlockSpec((count, LANES), lambda i: (0, i + pairs)),
            pl.BlockSpec((count, LANES), lambda i: (0, i + 2 * pairs)),
        ],
        out_specs=[
            pl.BlockSpec((count, LANES), lambda i: (0, i)),
            pl.BlockSpec((count, LANES), lambda i: (0, 0)),
        ],
        out_shape=[
            jax.ShapeDtypeStruct((count, width), BF16),
            jax.ShapeDtypeStruct((count, LANES), F32),
        ],
        compiler_params=params(),
        cost_estimate=cost(16e9, 8 * count * width, 10e6),
        name="attend",
    )(long_len, short_len, qkv, qkv, qkv)


def attend_back_kernel(
    seqs, long_len, short_len, q_ref, k_ref, v_ref, o_ref, do_ref, lse_ref,
    dq_ref, dk_ref, dv_ref, acc_ref, row_ref,
):
    pair = pl.program_id(0)
    masks = head_masks()
    lane = lax.broadcasted_iota(jnp.int32, (8, LANES), 1)
    which_row = lax.broadcasted_iota(jnp.int32, (8, LANES), 0)
    pick = (lane == 2 * pair + which_row).astype(F32) * (which_row < 2).astype(F32)
    split = (lane // HEAD_DIM == which_row).astype(F32)
    row_ref[0:8, :] = dot(pick, lse_ref[...], NT, precision=lax.Precision.HIGHEST)
    row_ref[8:16, :] = dot(
        split, do_ref[...].astype(F32) * o_ref[...].astype(F32), NT,
        precision=lax.Precision.HIGHEST,
    )
    acc_ref[...] = jnp.zeros_like(acc_ref)
    causal = lax.broadcasted_iota(jnp.int32, (BLOCK, BLOCK), 0) <= lax.broadcasted_iota(
        jnp.int32, (BLOCK, BLOCK), 1
    )
    for start, length, which, index in seqs:
        valid = (short_len if which else long_len)[index]
        for first in range(0, length, BLOCK):
            here = slice(start + first, start + first + BLOCK)
            k, v = k_ref[here, :], v_ref[here, :]
            key_pos = first + lax.broadcasted_iota(jnp.int32, (BLOCK, 1), 0)
            inside = key_pos < valid
            dk = jnp.zeros((BLOCK, LANES), F32)
            dv = jnp.zeros((BLOCK, LANES), F32)
            for head in range(2):
                kh = jnp.where(masks[head], k, jnp.zeros_like(k))
                for rows, allowed in (
                    (here, inside & causal),
                    (slice(here.stop, start + length), inside),
                ):
                    if rows.start == rows.stop:
                        continue
                    q, do = q_ref[rows, :], do_ref[rows, :]
                    qh = jnp.where(masks[head], q, jnp.zeros_like(q))
                    doh = jnp.where(masks[head], do, jnp.zeros_like(do))
                    scores = dot(k, qh, NT)
                    p = jnp.where(allowed, jnp.exp(scores - row_ref[head : head + 1, rows]), 0.0)
                    dp = dot(v, doh, NT)
                    ds = (p * (dp - row_ref[8 + head : 9 + head, rows])).astype(BF16)
                    dv = dv + dot(p.astype(BF16), doh)
                    dk = dk + dot(ds, qh)
                    acc_ref[rows, :] = acc_ref[rows, :] + dot(ds, kh, TN)
            dk_ref[here, :] = dk.astype(BF16)
            dv_ref[here, :] = dv.astype(BF16)
    dq_ref[...] = (acc_ref[...] * HEAD_DIM ** (-0.5)).astype(BF16)


def attend_back(qkv, o, d_o, lse, long_len, short_len, seqs):
    count, width = o.shape
    pairs = width // LANES
    one = pl.BlockSpec((count, LANES), lambda i: (0, i))
    return pl.pallas_call(
        functools.partial(attend_back_kernel, seqs),
        grid=(pairs,),
        in_specs=[pl.BlockSpec(memory_space=pltpu.SMEM)] * 2
        + [
            one,
            pl.BlockSpec((count, LANES), lambda i: (0, i + pairs)),
            pl.BlockSpec((count, LANES), lambda i: (0, i + 2 * pairs)),
            one,
            one,
            constant((count, LANES)),
        ],
        out_specs=[one, one, one],
        out_shape=[jax.ShapeDtypeStruct((count, width), BF16)] * 3,
        scratch_shapes=[pltpu.VMEM((count, LANES), F32), pltpu.VMEM((16, count), F32)],
        compiler_params=params(),
        cost_estimate=cost(40e9, 16 * count * width, 10e6),
        name="attend_back",
    )(long_len, short_len, qkv, qkv, qkv, o, d_o, lse)


def project_kernel(
    n_long, n_rows, long_ref, short_ref, o_ref, w_ref, vec_ref, row_ref,
    h_ref, slots_ref, rows_ref, vec_scr,
):
    i = pl.program_id(0)

    @pl.when(i == 0)
    def _():
        vec_scr[...] = vectors(vec_ref)

    def body(x_ref):
        hidden = x_ref[...] + dot(o_ref[...], w_ref[...], NT)
        h_ref[...] = hidden
        normed, _ = norm_parts(hidden)
        rows_ref[pl.ds(pl.multiple_of(i * ROWS, ROWS), ROWS), :] = (
            normed * vec_scr[2:3, :] + vec_scr[3:4, :]
        ).astype(BF16)

    pl.when(i < n_long)(lambda: body(long_ref))
    pl.when((i >= n_long) & (i < n_rows))(lambda: body(short_ref))

    @pl.when(i >= n_rows)
    def _():
        slots_ref[...] = dispatch_block(row_ref, rows_ref[...], i - n_rows)


def project(long_x, short_x, o, dense, slot_row, slots):
    width = long_x.shape[1]
    n_long, n_short = long_x.shape[0] // ROWS, short_x.shape[0] // ROWS
    n_rows = n_long + n_short
    count = o.shape[0]
    return pl.pallas_call(
        functools.partial(project_kernel, n_long, n_rows),
        grid=(n_rows + slots // BLOCK,),
        in_specs=[
            pl.BlockSpec((ROWS, width), lambda i: (jnp.minimum(i, n_long - 1), 0)),
            pl.BlockSpec((ROWS, width), lambda i: (jnp.clip(i - n_long, 0, n_short - 1), 0)),
            pl.BlockSpec((ROWS, width), lambda i: (jnp.minimum(i, n_rows - 1), 0)),
            pl.BlockSpec((width, width), lambda i: (0, 3)),
            pl.BlockSpec((width, LANES), lambda i: (0, 4 * width // LANES)),
            constant((8, count)),
        ],
        out_specs=[
            pl.BlockSpec((ROWS, width), lambda i: (jnp.minimum(i, n_rows - 1), 0)),
            pl.BlockSpec((BLOCK, width), lambda i: (jnp.maximum(i - n_rows, 0), 0)),
        ],
        out_shape=[
            jax.ShapeDtypeStruct((count, width), F32),
            jax.ShapeDtypeStruct((slots, width), BF16),
        ],
        scratch_shapes=[pltpu.VMEM((count, width), BF16), pltpu.VMEM((8, width), F32)],
        compiler_params=params(),
        cost_estimate=cost(2 * (slots + width) * count * width, 12 * count * width),
        name="project",
    )(long_x, short_x, o, dense, dense, slot_row)


def gelu_parts(pre):
    scale = 0.7978845608028654
    square = pre * pre
    flat = jnp.tanh(scale * pre * (1.0 + 0.044715 * square))
    half = 0.5 * (1.0 + flat)
    slope = half + (0.5 * scale) * pre * (1.0 - flat * flat) * (1.0 + 0.134145 * square)
    return half * pre, slope


def experts_kernel(n_r, b_ref, g_ref, up_ref, act_ref, slope_ref, gd_ref, all_ref):
    r = pl.program_id(1)
    pre = dot(b_ref[...], up_ref[...])
    act, slope = gelu_parts(pre)
    act = act.astype(BF16)
    act_ref[...] = act
    slope_ref[...] = slope.astype(BF16)
    all_ref[pl.ds(pl.multiple_of(r * ROWS, ROWS), ROWS), :] = act

    @pl.when(r == n_r - 1)
    def _():
        gd_ref[...] = dot(all_ref[...], g_ref[...], TN).astype(BF16)


def experts_up(b_slots, g_slots, up):
    rows, width = b_slots.shape
    hidden = up.shape[1]
    n_r, n_f = rows // ROWS, hidden // width
    tile = pl.BlockSpec((ROWS, width), lambda f, r: (r, f))
    return pl.pallas_call(
        functools.partial(experts_kernel, n_r),
        grid=(n_f, n_r),
        in_specs=[
            pl.BlockSpec((ROWS, width), lambda f, r: (r, 0)),
            constant((rows, width)),
            pl.BlockSpec((width, width), lambda f, r: (0, f)),
        ],
        out_specs=[tile, tile, pl.BlockSpec((width, width), lambda f, r: (f, 0))],
        out_shape=[
            jax.ShapeDtypeStruct((rows, hidden), BF16),
            jax.ShapeDtypeStruct((rows, hidden), BF16),
            jax.ShapeDtypeStruct((hidden, width), BF16),
        ],
        scratch_shapes=[pltpu.VMEM((rows, width), BF16)],
        compiler_params=params(),
        cost_estimate=cost(4 * rows * width * hidden, 6 * rows * hidden, rows * hidden),
        name="experts_up",
    )(b_slots, g_slots, up)


def experts_back_kernel(
    n_f, n_r, b_ref, g_ref, act_ref, slope_ref, up_ref, down_ref,
    y_ref, db_ref, gu_ref, y_acc, db_acc, all_ref,
):
    f, r = pl.program_id(0), pl.program_id(1)
    rows = pl.ds(pl.multiple_of(r * ROWS, ROWS), ROWS)
    d_act = dot(g_ref[rows, :], down_ref[...], NT)
    d_pre = (d_act * slope_ref[...].astype(F32)).astype(BF16)
    all_ref[rows, :] = d_pre
    y = dot(act_ref[...], down_ref[...])
    db = dot(d_pre, up_ref[...], NT)

    @pl.when(f == 0)
    def _():
        y_acc[rows, :] = y
        db_acc[rows, :] = db

    @pl.when((f > 0) & (f < n_f - 1))
    def _():
        y_acc[rows, :] = y_acc[rows, :] + y
        db_acc[rows, :] = db_acc[rows, :] + db

    @pl.when(f == n_f - 1)
    def _():
        y_ref[rows, :] = (y_acc[rows, :] + y).astype(BF16)
        db_ref[rows, :] = (db_acc[rows, :] + db).astype(BF16)

    @pl.when(r == n_r - 1)
    def _():
        gu_ref[...] = dot(b_ref[...], all_ref[...], TN).astype(BF16)


def experts_back(b_slots, g_slots, act, slope, up, down):
    rows, width = b_slots.shape
    hidden = up.shape[1]
    n_r, n_f = rows // ROWS, hidden // width
    tile = pl.BlockSpec((ROWS, width), lambda f, r: (r, f))
    whole = pl.BlockSpec((rows, width), lambda f, r: (0, 0))
    return pl.pallas_call(
        functools.partial(experts_back_kernel, n_f, n_r),
        grid=(n_f, n_r),
        in_specs=[
            constant((rows, width)),
            constant((rows, width)),
            tile,
            tile,
            pl.BlockSpec((width, width), lambda f, r: (0, f)),
            pl.BlockSpec((width, width), lambda f, r: (f, 0)),
        ],
        out_specs=[whole, whole, pl.BlockSpec((width, width), lambda f, r: (0, f))],
        out_shape=[
            jax.ShapeDtypeStruct((rows, width), BF16),
            jax.ShapeDtypeStruct((rows, width), BF16),
            jax.ShapeDtypeStruct((width, hidden), BF16),
        ],
        scratch_shapes=[
            pltpu.VMEM((rows, width), F32),
            pltpu.VMEM((rows, width), F32),
            pltpu.VMEM((rows, width), BF16),
        ],
        compiler_params=params(),
        cost_estimate=cost(8 * rows * width * hidden, 8 * rows * hidden),
        name="experts_back",
    )(b_slots, g_slots, act, slope, up, down)


def combine_rows(col_ref, slots_ref):
    slot_id = lax.broadcasted_iota(jnp.int32, (1, slots_ref.shape[0]), 1)
    chosen = (col_ref[...] == slot_id).astype(F32).astype(BF16)
    return dot(chosen, slots_ref[...])


def finish_kernel(n_long, h_ref, col_ref, y_ref, long_ref, short_ref):
    i = pl.program_id(0)
    out = h_ref[...] + combine_rows(col_ref, y_ref)

    @pl.when(i < n_long)
    def _():
        long_ref[...] = out

    @pl.when(i >= n_long)
    def _():
        short_ref[...] = out


def finish(h, slot_col, y_back, n_long, n_short):
    count, width = h.shape
    slots = y_back.shape[0]
    return pl.pallas_call(
        functools.partial(finish_kernel, n_long),
        grid=(n_long + n_short,),
        in_specs=[
            pl.BlockSpec((ROWS, width), lambda i: (i, 0)),
            pl.BlockSpec((ROWS, 1), lambda i: (i, 0)),
            constant((slots, width)),
        ],
        out_specs=long_short(width, n_long),
        out_shape=[
            jax.ShapeDtypeStruct((n_long * ROWS, width), F32),
            jax.ShapeDtypeStruct((n_short * ROWS, width), F32),
        ],
        compiler_params=params(),
        cost_estimate=cost(2 * slots * count * width, 8 * count * width + 2 * slots * width),
        name="finish",
    )(h, slot_col, y_back)


def hidden_back_kernel(
    n_long, n_rows, h_ref, col_ref, db_ref, long_ref, short_ref, o_ref, w_ref, vec_ref,
    dh_ref, do_ref, gp_ref, gv_ref, acc_ref, vec_scr,
):
    i = pl.program_id(0)

    @pl.when(i == 0)
    def _():
        vec_scr[...] = vectors(vec_ref)
        acc_ref[...] = jnp.zeros_like(acc_ref)
        gv_ref[...] = jnp.zeros_like(gv_ref)

    def body(cot_ref):
        d_b = combine_rows(col_ref, db_ref)
        normed, inv_scale = norm_parts(h_ref[...])
        gv_ref[0:1, :] = gv_ref[0:1, :] + jnp.sum(d_b * normed, 0, keepdims=True)
        gv_ref[1:2, :] = gv_ref[1:2, :] + jnp.sum(d_b, 0, keepdims=True)
        d_h = cot_ref[...] + norm_back(d_b * vec_scr[2:3, :], normed, inv_scale)
        dh_ref[...] = d_h
        d_attn = d_h.astype(BF16)
        do_ref[...] = dot(d_attn, w_ref[...]).astype(BF16)
        acc_ref[...] = acc_ref[...] + dot(d_attn, o_ref[...], TN)

    pl.when(i < n_long)(lambda: body(long_ref))
    pl.when(i >= n_long)(lambda: body(short_ref))

    @pl.when(i == n_rows - 1)
    def _():
        gp_ref[...] = acc_ref[...].astype(BF16)


def hidden_back(h, slot_col, db_back, long_cot, short_cot, o, dense):
    count, width = h.shape
    slots = db_back.shape[0]
    n_long, n_short = long_cot.shape[0] // ROWS, short_cot.shape[0] // ROWS
    n_rows = n_long + n_short
    row = pl.BlockSpec((ROWS, width), lambda i: (i, 0))
    return pl.pallas_call(
        functools.partial(hidden_back_kernel, n_long, n_rows),
        grid=(n_rows,),
        in_specs=[row, pl.BlockSpec((ROWS, 1), lambda i: (i, 0)), constant((slots, width))]
        + long_short(width, n_long)
        + [
            row,
            pl.BlockSpec((width, width), lambda i: (0, 3)),
            pl.BlockSpec((width, LANES), lambda i: (0, 4 * width // LANES)),
        ],
        out_specs=[
            row,
            row,
            pl.BlockSpec((width, width), lambda i: (0, 0)),
            pl.BlockSpec((8, width), lambda i: (0, 0)),
        ],
        out_shape=[
            jax.ShapeDtypeStruct((count, width), F32),
            jax.ShapeDtypeStruct((count, width), BF16),
            jax.ShapeDtypeStruct((width, width), BF16),
            jax.ShapeDtypeStruct((8, width), F32),
        ],
        scratch_shapes=[pltpu.VMEM((width, width), F32), pltpu.VMEM((8, width), F32)],
        compiler_params=params(),
        cost_estimate=cost(2 * (slots + 2 * width) * count * width, 16 * count * width),
        name="hidden_back",
    )(h, slot_col, db_back, long_cot, short_cot, o, dense, dense)


def input_back_kernel(
    n_long, n_rows, width, long_ref, short_ref, dh_ref, dq_ref, dk_ref, dv_ref, w_ref, vec_ref,
    gp_ref, gv_ref, lg_ref, sg_ref, out_ref, acc_ref, vec_scr, gv_scr,
):
    i = pl.program_id(0)

    @pl.when(i == 0)
    def _():
        vec_scr[...] = vectors(vec_ref)
        acc_ref[...] = jnp.zeros_like(acc_ref)
        gv_scr[...] = jnp.zeros_like(gv_scr)
        gv_scr[2:4, :] = gv_ref[0:2, :]

    def body(x_ref, grad_ref):
        normed, inv_scale = norm_parts(x_ref[...])
        rows = (normed * vec_scr[0:1, :] + vec_scr[1:2, :]).astype(BF16)
        entered = jnp.zeros_like(normed)
        for part, d_ref in enumerate((dq_ref, dk_ref, dv_ref)):
            cut = slice(part * width, (part + 1) * width)
            entered = entered + dot(d_ref[...], w_ref[:, cut], NT)
            acc_ref[:, cut] = acc_ref[:, cut] + dot(rows, d_ref[...], TN)
        gv_scr[0:1, :] = gv_scr[0:1, :] + jnp.sum(entered * normed, 0, keepdims=True)
        gv_scr[1:2, :] = gv_scr[1:2, :] + jnp.sum(entered, 0, keepdims=True)
        grad_ref[...] = dh_ref[...] + norm_back(entered * vec_scr[0:1, :], normed, inv_scale)

    pl.when(i < n_long)(lambda: body(long_ref, lg_ref))
    pl.when(i >= n_long)(lambda: body(short_ref, sg_ref))

    @pl.when(i == n_rows - 1)
    def _():
        out_ref[:, : 3 * width] = acc_ref[...].astype(BF16)
        out_ref[:, 3 * width : 4 * width] = gp_ref[...]
        out_ref[:, 4 * width :] = jnp.transpose(gv_scr[...]).astype(BF16)


def input_back(long_x, short_x, d_h, dq, dk, dv, dense, grad_proj, grad_vec):
    count, width = d_h.shape
    n_long, n_short = long_x.shape[0] // ROWS, short_x.shape[0] // ROWS
    n_rows = n_long + n_short
    row = pl.BlockSpec((ROWS, width), lambda i: (i, 0))
    return pl.pallas_call(
        functools.partial(input_back_kernel, n_long, n_rows, width),
        grid=(n_rows,),
        in_specs=long_short(width, n_long)
        + [
            row,
            row,
            row,
            row,
            constant((width, 3 * width)),
            pl.BlockSpec((width, LANES), lambda i: (0, 4 * width // LANES)),
            constant((width, width)),
            constant((8, width)),
        ],
        out_specs=long_short(width, n_long)
        + [pl.BlockSpec((width, 4 * width + LANES), lambda i: (0, 0))],
        out_shape=[
            jax.ShapeDtypeStruct(long_x.shape, F32),
            jax.ShapeDtypeStruct(short_x.shape, F32),
            jax.ShapeDtypeStruct((width, 4 * width + LANES), BF16),
        ],
        scratch_shapes=[
            pltpu.VMEM((width, 3 * width), F32),
            pltpu.VMEM((8, width), F32),
            pltpu.VMEM((LANES, width), F32),
        ],
        compiler_params=params(),
        cost_estimate=cost(12 * count * width * width, 20 * count * width),
        name="input_back",
    )(long_x, short_x, d_h, dq, dk, dv, dense, dense, grad_proj, grad_vec)


def on_device(
    n_dp, n_f, long_x, short_x, long_len, short_len, expert_ids, ln1_gain, ln1_bias,
    w_qkv, w_proj, ln2_gain, ln2_bias, w_up, w_down, long_cot, short_cot,
):
    width = long_x.shape[2]
    share = w_qkv.shape[0]
    seqs = sequences(long_x.shape[:2], short_x.shape[:2])
    flat = lambda a: a.reshape(-1, width)
    xl, xs, gl, gs = flat(long_x), flat(short_x), flat(long_cot), flat(short_cot)
    n_long, n_short = xl.shape[0] // ROWS, xs.shape[0] // ROWS
    experts = n_f * w_up.shape[0]
    cap = 4 * expert_ids.shape[0] // (3 * experts)
    slots = experts * cap

    up = lax.all_gather(w_up, "dp", axis=2, tiled=True)[0]
    down = lax.all_gather(w_down, "dp", axis=1, tiled=True)[0]

    vec = jnp.stack([ln1_gain, ln1_bias, ln2_gain, ln2_bias], 1)
    own = jnp.concatenate(
        [w_qkv, w_proj.T, jnp.pad(vec, ((0, 0), (0, LANES - vec.shape[1])))], 1
    )
    dense = gather_dense(own, n_dp, n_f).reshape(n_dp * n_f * share, own.shape[1])

    def exchange(rows):
        sent = lax.all_to_all(
            rows.reshape(n_f, slots // n_f, width), "fsdp", split_axis=0, concat_axis=0, tiled=True
        )
        return sent.reshape(slots, width)

    slot_col, slot_row, g_slots = route_cot(expert_ids, gl, gs, slots, cap)
    qkv = make_qkv(xl, xs, dense)
    g_there = exchange(g_slots)
    o, lse = attend(qkv, long_len, short_len, seqs)
    h, b_slots = project(xl, xs, o, dense, slot_row, slots)
    b_there = exchange(b_slots)
    act, slope, grad_down = experts_up(b_there, g_there, up)
    grad_down = lax.psum_scatter(grad_down, "dp", scatter_dimension=0, tiled=True).astype(F32)
    y, d_b, grad_up = experts_back(b_there, g_there, act, slope, up, down)
    grad_up = lax.psum_scatter(grad_up, "dp", scatter_dimension=1, tiled=True).astype(F32)
    db_back = exchange(d_b)
    y_back = exchange(y)
    d_h, d_o, grad_proj, grad_vec = hidden_back(h, slot_col, db_back, gl, gs, o, dense)
    long_out, short_out = finish(h, slot_col, y_back, n_long, n_short)
    dq, dk, dv = attend_back(qkv, o, d_o, lse, long_len, short_len, seqs)
    long_grad, short_grad, grads = input_back(xl, xs, d_h, dq, dk, dv, dense, grad_proj, grad_vec)
    owned = scatter_dense(grads.reshape(n_dp, n_f, share, own.shape[1]), n_dp, n_f)
    return (
        long_out.reshape(long_x.shape),
        short_out.reshape(short_x.shape),
        long_grad.reshape(long_x.shape),
        short_grad.reshape(short_x.shape),
        owned[:, 4 * width],
        owned[:, 4 * width + 1],
        owned[:, : 3 * width],
        owned[:, 3 * width : 4 * width].T,
        owned[:, 4 * width + 2],
        owned[:, 4 * width + 3],
        grad_up[None],
        grad_down[None],
    )


def solution(mesh):
    both = ("dp", "fsdp")
    return jax.shard_map(
        functools.partial(on_device, mesh.shape["dp"], mesh.shape["fsdp"]),
        mesh=mesh,
        in_specs=(
            P(both, None, None),
            P(both, None, None),
            P(both),
            P(both),
            P(both, None),
            P(both),
            P(both),
            P(both, None),
            P(None, both),
            P(both),
            P(both),
            P("fsdp", None, "dp"),
            P("fsdp", "dp", None),
            P(both, None, None),
            P(both, None, None),
        ),
        out_specs=(
            P(both, None, None),
            P(both, None, None),
            P(both, None, None),
            P(both, None, None),
            P(both),
            P(both),
            P(both, None),
            P(None, both),
            P(both),
            P(both),
            P("fsdp", None, "dp"),
            P("fsdp", "dp", None),
        ),
        check_vma=False,
    )
```

time: 903 us -> 519 us (0.57)
  Pallas kernels: 0 us -> 388 us
  matrix products: 285 us -> 0 us
  local copies, waits for them, and re-layouts: 203 us -> 10.3 us
  other arithmetic: 161 us -> 6.38 us
  waiting for transfers between devices: 123 us -> 1.47 us
  starting transfers between devices: 20 us -> 10.2 us
    pallas_call x0 -> x12, Pallas kernels: none -> 388 us  [the longest x1 67.7 us: gather_dense(): pl.pallas_call(functools.partial(gather_kernel, n_dp, n_f), out_shape=jax...]
    dot_general x36 -> x0, matrix products: 285 us -> none  [the longest x3 36.6 us: attend_back(): jnp.einsum('sqhc,skhc->shqk', grad_block, values[:, :stop_row], preferred...]
    all_to_all x4 -> x2, waiting for transfers between devices: 94.2 us -> 0.01 us  [exchange(): lax.all_to_all(rows.reshape(n_f, slots // n_f, width), 'fsdp', split_axis...]
    reshape x4 -> x0, local copies, waits for them, and re-layouts: 93 us -> none  [the longest x1 45.1 us: on_device(): result.reshape(1, owned_count, received_rows, model_width)]
    unnamed x2 -> x0, blocking collectives: 87.5 us -> none
    all_to_all x0 -> x2, blocking collectives: none -> 82 us  [exchange(): lax.all_to_all(rows.reshape(n_f, slots // n_f, width), 'fsdp', split_axis...]
    unnamed x7 -> x0, other arithmetic: 63.5 us -> none
    unnamed x265 -> x19, local copies, waits for them, and re-layouts: 54.9 us -> 5.49 us
  transfers between devices with their start and end apart: 12 -> 6, of which waited for: 6 -> 0; matrix products, arithmetic and copies ran while one was open for 69% -> 2% of each run, Pallas kernels for 0% -> 75%
where the time goes in v1:
time: 519 us; the launch traced here: 514 us
  Pallas kernels  388 us (75%)
  blocking collectives  82 us (16%)
  between operations  15.4 us (3%)
  local copies, waits for them, and re-layouts  10.3 us (2%)
  starting transfers between devices  10.2 us (2%)
  other arithmetic  6.38 us (1%)
    all_to_all x2, blocking collectives, exchange(): lax.all_to_all(rows.reshape(n_f, slots // n_f, width), 'fsdp', split_axis...  82 us
    pallas_call x1, Pallas kernels, gather_dense(): pl.pallas_call(functools.partial(gather_kernel, n_dp, n_f), out_shape=jax...  67.7 us
    pallas_call x1, Pallas kernels, experts_back(): pl.pallas_call(functools.partial(experts_back_kernel, n_f, n_r), grid=(n_...  56.1 us
    pallas_call x1, Pallas kernels, attend_back(): pl.pallas_call(functools.partial(attend_back_kernel, seqs), grid=(pairs,)...  52 us
    pallas_call x1, Pallas kernels, scatter_dense(): pl.pallas_call(functools.partial(scatter_kernel, n_dp, n_f), out_shape=ja...  51.9 us
    pallas_call x1, Pallas kernels, experts_up(): pl.pallas_call(functools.partial(experts_kernel, n_r), grid=(n_f, n_r), i...  39.6 us
    pallas_call x1, Pallas kernels, attend(): pl.pallas_call(functools.partial(attend_kernel, seqs), grid=(pairs,), in_...  27.8 us
    pallas_call x1, Pallas kernels, input_back(): pl.pallas_call(functools.partial(input_back_kernel, n_long, n_rows, width...  22.8 us
  transfers between devices with their start and end apart: 6, of which 0 were waited for; matrix products, arithmetic and copies ran while one was open for 2% of the time, Pallas kernels for 75%

profile of v1, /device:TPU:12, one launch (start us, length us, event | category | flops | bytes accessed | tf_op | source)
XLA Modules:
  0.0 513.6 jit_solution(15291015765835871604)
XLA Ops:
  7.2 0.0 all-gather.3.cloned.1.call-start
  7.2 0.7 all-gather.3.cloned.1.call-update
  7.9 1.9 copy.38.ids_ref
  9.8 14.0 %route_cot.1 = (s32[1536,1]{1,0:T(8,128)}, s32[8,1536]{1,0:T(8,128)}, bf16[2048,768]{1,0:T(8,128)(2,1)}) custom-call(s32[1536,1]{1,0:T(8,128)} %copy.38.ids_ref, f32[1024,768]{1,0:T(8,128)} %bitcast.65, f32[512,768]{1,0:T(8,128)} %bitcast.67), custom_call_target="tpu_custom_call" | custom-call | flops 4831838208 | bytes 7864320 | tf_op jit(solution)/shard_map/route_cot/pallas_call | solution.py:276
  23.8 4.4 all-to-all-start.1
  28.2 0.7 all-gather.5.cloned.1.call-update
  28.9 0.3 reduce-scatter.5.cloned.1.call-start
  29.3 0.1 copy.37
  29.4 0.7 fusion.1.own_ref
  31.3 67.7 %gather_dense.1 = bf16[4,8,24,3200]{3,2,1,0:T(8,128)(2,1)} custom-call(bf16[24,3200]{1,0:T(8,128)(2,1)} %fusion.1.own_ref), custom_call_target="tpu_custom_call" | custom-call | bytes 100000000 | tf_op jit(solution)/shard_map/gather_dense/pallas_call | solution.py:118
  99.0 11.5 %make_qkv.1.q_ref.k_ref.v_ref = bf16[1536,2304]{1,0:T(8,128)(2,1)} custom-call(f32[1024,768]{1,0:T(8,128)} %bitcast.51, f32[512,768]{1,0:T(8,128)} %bitcast.54, bf16[768,3200]{1,0:T(8,128)(2,1)} %bitcast.33, bf16[768,3200]{1,0:T(8,128)(2,1)} %bitcast.34), custom_call_target="tpu_custom_call" | custom-call | flops 5435817984 | bytes 15335424 | tf_op jit(solution)/shard_map/make_qkv/pallas_call | solution.py:326
  110.6 27.8 %attend.1 = (bf16[1536,768]{1,0:T(8,128)(2,1)}, f32[1536,128]{1,0:T(8,128)}) custom-call(s32[1]{0:T(128)S(6)} %copy.39.long_len, s32[1]{0:T(128)S(6)} %copy.40.short_len, bf16[1536,2304]{1,0:T(8,128)(2,1)} %make_qkv.1.q_ref.k_ref.v_ref, bf16[1536,2304]{1,0:T(8,128)(2,1)} %make_qkv.1.q_ref.k_ref.v_ref, bf16[1536,2304]{1,0:T(8,128)(2,1)} %make_qkv.1.q_ref.k_ref.v_ref), custom_call_target="tpu_custom_call" | custom-call | flops 16000000000 | bytes 9437184 | tf_op jit(solution)/shard_map/attend/pallas_call | solution.py:404
  138.4 14.9 %project.1 = (f32[1536,768]{1,0:T(8,128)}, bf16[2048,768]{1,0:T(8,128)(2,1)}) custom-call(f32[1024,768]{1,0:T(8,128)} %bitcast.52, f32[512,768]{1,0:T(8,128)} %bitcast.55, bf16[1536,768]{1,0:T(8,128)(2,1)} %get-tuple-element.37.o_ref, bf16[768,3200]{1,0:T(8,128)(2,1)} %bitcast.35, bf16[768,3200]{1,0:T(8,128)(2,1)} %bitcast.36, ...), custom_call_target="tpu_custom_call" | custom-call | flops 6643777536 | bytes 14155776 | tf_op jit(solution)/shard_map/project/pallas_call | solution.py:534
  153.3 42.2 %all_to_all.20 = bf16[8,256,768]{2,1,0:T(8,128)(2,1)} all-to-all(bf16[8,256,768]{2,1,0:T(8,128)(2,1)} %bitcast.50), channel_id=1, replica_groups=mesh['dp'=4,'fsdp'=8] {'fsdp'}, dimensions={0} | all-to-all | bytes 6291456 | tf_op jit(solution)/shard_map/all_to_all | solution.py:878
  195.5 39.6 %experts_up.1 = (bf16[2048,3072]{1,0:T(8,128)(2,1)}, bf16[2048,3072]{1,0:T(8,128)(2,1)}, bf16[3072,768]{1,0:T(8,128)(2,1)}) custom-call(bf16[2048,768]{1,0:T(8,128)(2,1)} %bitcast.46, bf16[2048,768]{1,0:T(8,128)(2,1)} %bitcast.42, bf16[768,3072]{1,0:T(8,128)(2,1)} %bitcast.62), custom_call_target="tpu_custom_call" | custom-call | flops 19327352832 | bytes 37748736 | tf_op jit(solution)/shard_map/experts_up/pallas_call | solution.py:588
  235.1 0.0 reduce-scatter.3.cloned.1.call-start
  235.1 0.0 all-gather.5.cloned.1.call-done
  235.2 56.1 %experts_back.1 = (bf16[2048,768]{1,0:T(8,128)(2,1)}, bf16[2048,768]{1,0:T(8,128)(2,1)}, bf16[768,3072]{1,0:T(8,128)(2,1)}) custom-call(bf16[2048,768]{1,0:T(8,128)(2,1)} %bitcast.47, bf16[2048,768]{1,0:T(8,128)(2,1)} %bitcast.43, bf16[2048,3072]{1,0:T(8,128)(2,1)} %get-tuple-element.43.act_ref, bf16[2048,3072]{1,0:T(8,128)(2,1)} %get-tuple-element.44.slope_ref, ...), custom_call_target="tpu_custom_call" | custom-call | flops 38654705664 | bytes 50331648 | tf_op jit(solution)/shard_map/experts_back/pallas_call | solution.py:647
  291.3 1.9 copy-done.2
  293.3 39.8 %all_to_all.21 = bf16[8,256,768]{2,1,0:T(8,128)(2,1)} all-to-all(bf16[8,256,768]{2,1,0:T(8,128)(2,1)S(1)} %bitcast.48), channel_id=1, replica_groups=mesh['dp'=4,'fsdp'=8] {'fsdp'}, dimensions={0} | all-to-all | bytes 6291456 | tf_op jit(solution)/shard_map/all_to_all | solution.py:878
  333.1 5.5 %all-to-all-start.2 = ((bf16[8,256,768]{2,1,0:T(8,128)(2,1)}), bf16[8,256,768]{2,1,0:T(8,128)(2,1)S(1)}, u32[]{:S(2)}, u32[]{:S(2)}) async-start(bf16[8,256,768]{2,1,0:T(8,128)(2,1)} %bitcast.16), calls=%async_computation.2 | async-start | bytes 6291456 | tf_op jit(solution)/shard_map/all_to_all | solution.py:878
  338.6 19.4 %hidden_back.1 = (f32[1536,768]{1,0:T(8,128)}, bf16[1536,768]{1,0:T(8,128)(2,1)}, bf16[768,768]{1,0:T(8,128)(2,1)}, f32[8,768]{1,0:T(8,128)}) custom-call(f32[1536,768]{1,0:T(8,128)} %get-tuple-element.39.h_ref, s32[1536,1]{1,0:T(8,128)} %get-tuple-element.40.col_ref, bf16[2048,768]{1,0:T(8,128)(2,1)} %bitcast.49, f32[1024,768]{1,0:T(8,128)} %bitcast.66, ...), custom_call_target="tpu_custom_call" | custom-call | flops 8455716864 | bytes 18874368 | tf_op jit(solution)/shard_map/hidden_back/pallas_call | solution.py:753
  358.0 52.0 %attend_back.1 = (bf16[1536,768]{1,0:T(8,128)(2,1)}, bf16[1536,768]{1,0:T(8,128)(2,1)}, bf16[1536,768]{1,0:T(8,128)(2,1)}) custom-call(s32[1]{0:T(128)S(6)} %copy.39.long_len, s32[1]{0:T(128)S(6)} %copy.40.short_len, bf16[1536,2304]{1,0:T(8,128)(2,1)} %make_qkv.1.q_ref.k_ref.v_ref, bf16[1536,2304]{1,0:T(8,128)(2,1)} %make_qkv.1.q_ref.k_ref.v_ref, ...), custom_call_target="tpu_custom_call" | custom-call | flops 40000000000 | bytes 18874368 | tf_op jit(solution)/shard_map/attend_back/pallas_call | solution.py:482
  410.0 22.8 %input_back.1 = (f32[1024,768]{1,0:T(8,128)}, f32[512,768]{1,0:T(8,128)}, bf16[768,3200]{1,0:T(8,128)(2,1)}) custom-call(f32[1024,768]{1,0:T(8,128)} %bitcast.53, f32[512,768]{1,0:T(8,128)} %bitcast.56, f32[1536,768]{1,0:T(8,128)} %get-tuple-element.49.dh_ref, bf16[1536,768]{1,0:T(8,128)(2,1)} %get-tuple-element.52.dq_ref, ...), custom_call_target="tpu_custom_call" | custom-call | flops 10871635968 | bytes 23592960 | tf_op jit(solution)/shard_map/input_back/pallas_call | solution.py:822
  432.8 51.9 %scatter_dense.1 = f32[24,3200]{1,0:T(8,128)} custom-call(bf16[4,8,24,3200]{3,2,1,0:T(8,128)(2,1)} %bitcast.41), custom_call_target="tpu_custom_call" | custom-call | bytes 100000000 | tf_op jit(solution)/shard_map/scatter_dense/pallas_call | solution.py:206
  484.8 1.6 slice.20
  486.4 1.6 slice_reduce_fusion
  488.0 1.5 slice_bitcast_fusion
  489.5 1.6 copy-done.1
  491.2 10.0 %finish.1 = (f32[1024,768]{1,0:T(8,128)}, f32[512,768]{1,0:T(8,128)}) custom-call(f32[1536,768]{1,0:T(8,128)} %get-tuple-element.39.h_ref, s32[1536,1]{1,0:T(8,128)} %get-tuple-element.40.col_ref, bf16[2048,768]{1,0:T(8,128)(2,1)} %bitcast.44), custom_call_target="tpu_custom_call" | custom-call | flops 4831838208 | bytes 12582912 | tf_op jit(solution)/shard_map/finish/pallas_call | solution.py:697
  501.2 2.8 bitcast_convert_fusion
  504.0 2.8 bitcast_convert_fusion.1
  (25 shorter events, 0.1 us)
Async XLA Ops:
  7.2 188.3 %all-gather.3.cloned.1.call-start = ((), (), s32[]{:S(2)}) async-start(), calls=%async_computation.6 | async-start | bytes 5898240 | tf_op jit(solution)/shard_map/all_gather | solution.py:868
  23.8 5.4 %copy-start.5 = (bf16[24]{0:T(256)(128)(2,1)S(1)}, bf16[24]{0:T(256)(128)(2,1)}, u32[]{:S(2)}) copy-start(bf16[24]{0:T(256)(128)(2,1)} %param.25) | copy-start | bytes 148
  23.8 5.4 %copy-start.6 = (bf16[24]{0:T(256)(128)(2,1)S(1)}, bf16[24]{0:T(256)(128)(2,1)}, u32[]{:S(2)}) copy-start(bf16[24]{0:T(256)(128)(2,1)} %param.24) | copy-start | bytes 148
  23.8 5.4 %copy-start.7 = (bf16[24]{0:T(256)(128)(2,1)S(1)}, bf16[24]{0:T(256)(128)(2,1)}, u32[]{:S(2)}) copy-start(bf16[24]{0:T(256)(128)(2,1)} %param.21) | copy-start | bytes 148
  23.8 5.4 %copy-start.8 = (bf16[24]{0:T(256)(128)(2,1)S(1)}, bf16[24]{0:T(256)(128)(2,1)}, u32[]{:S(2)}) copy-start(bf16[24]{0:T(256)(128)(2,1)} %param.20) | copy-start | bytes 148
  23.8 5.5 %copy-start.3 = (bf16[24,2304]{1,0:T(8,128)(2,1)S(1)}, bf16[24,2304]{1,0:T(8,128)(2,1)}, u32[]{:S(2)}) copy-start(bf16[24,2304]{1,0:T(8,128)(2,1)} %param.22) | copy-start | bytes 331780
  23.8 5.5 %copy-start.4 = (bf16[768,24]{0,1:T(8,128)(2,1)S(1)}, bf16[768,24]{0,1:T(8,128)(2,1)}, u32[]{:S(2)}) copy-start(bf16[768,24]{0,1:T(8,128)(2,1)} %param.23) | copy-start | bytes 110596
  23.8 129.4 %all-to-all-start.1 = ((bf16[8,256,768]{2,1,0:T(8,128)(2,1)}), bf16[8,256,768]{2,1,0:T(8,128)(2,1)S(1)}, u32[]{:S(2)}, u32[]{:S(2)}) async-start(bf16[8,256,768]{2,1,0:T(8,128)(2,1)} %bitcast.45), calls=%async_computation.1 | async-start | bytes 6291456 | tf_op jit(solution)/shard_map/all_to_all | solution.py:878
  28.2 207.0 %all-gather.5.cloned.1.call-start = ((), (), s32[]{:S(2)}) async-start(), calls=%async_computation.7 | async-start | bytes 5898240 | tf_op jit(solution)/shard_map/all_gather | solution.py:869
  28.9 472.2 %reduce-scatter.5.cloned.1.call-start = ((), (), s32[]{:S(2)}) async-start(), calls=%async_computation.9 | async-start | bytes 5898240 | tf_op jit(solution)/shard_map/reduce_scatter | solution.py:890
  153.3 42.2 %copy-start = (bf16[8,256,768]{2,1,0:T(8,128)(2,1)}, bf16[8,256,768]{2,1,0:T(8,128)(2,1)S(1)}, u32[]{:S(2)}) copy-start(bf16[8,256,768]{2,1,0:T(8,128)(2,1)S(1)} %all-to-all-done.1) | copy-start | bytes 9437188
  235.1 268.9 %reduce-scatter.3.cloned.1.call-start = ((), (), s32[]{:S(2)}) async-start(), calls=%async_computation.8 | async-start | bytes 5898240 | tf_op jit(solution)/shard_map/reduce_scatter | solution.py:892
  291.3 2.0 copy-start.2
  333.1 156.5 %all-to-all-start.2 = ((bf16[8,256,768]{2,1,0:T(8,128)(2,1)}), bf16[8,256,768]{2,1,0:T(8,128)(2,1)S(1)}, u32[]{:S(2)}, u32[]{:S(2)}) async-start(bf16[8,256,768]{2,1,0:T(8,128)(2,1)} %bitcast.16), calls=%async_computation.2 | async-start | bytes 6291456 | tf_op jit(solution)/shard_map/all_to_all | solution.py:878
  489.5 1.7 copy-start.1
Sparse Core Ops, SparseCore 0:
  9.6 99.8 all-gather.2
  111.0 89.0 all-gather.4
  235.2 84.1 reduce-scatter.4
  321.6 85.7 reduce-scatter.2

commit v2 on v1

--- a/solution.py
+++ b/solution.py
@@ -63,7 +63,10 @@
     ]
 
 
-def gather_kernel(n_dp, n_f, own_ref, out_ref, z_send, z_recv, p_send, p_recv, c_send, c_recv, l_sem):
+def gather_kernel(
+    n_dp, n_f, cap, own_ref, ids_ref, long_ref, short_ref, out_ref, col_ref, row_ref, slots_ref,
+    rows_ref, z_send, z_recv, p_send, p_recv, c_send, c_recv, l_sem,
+):
     z = lax.axis_index("dp")
     f = lax.axis_index("fsdp")
     half = n_f // 2
@@ -86,6 +89,10 @@
         )
         copy.start()
         z_copies.append(copy)
+    number_slots(cap, ids_ref, col_ref, row_ref)
+    n_long = long_ref.shape[0]
+    rows_ref[:n_long, :] = long_ref[...].astype(BF16)
+    rows_ref[n_long:, :] = short_ref[...].astype(BF16)
     local.wait()
     for copy in z_copies:
         copy.wait_recv()
@@ -97,6 +104,13 @@
         )
         copy.start()
         p_copies.append(copy)
+
+    def fill(block, carry):
+        start = pl.multiple_of(block * BLOCK, BLOCK)
+        slots_ref[pl.ds(start, BLOCK), :] = dispatch_block(row_ref, rows_ref[...], start, BLOCK)
+        return carry
+
+    lax.fori_loop(0, slots_ref.shape[0] // BLOCK, fill, 0)
     c_copies = []
     for k in range(half):
         if k:
@@ -114,13 +128,21 @@
         copy.wait_send()
 
 
-def gather_dense(own, n_dp, n_f):
+def gather_dense(own, ids, long_cot, short_cot, n_dp, n_f, cap, slots):
+    count, width = ids.shape[0], long_cot.shape[1]
+    vmem = pl.BlockSpec(memory_space=pltpu.VMEM)
     return pl.pallas_call(
-        functools.partial(gather_kernel, n_dp, n_f),
-        out_shape=jax.ShapeDtypeStruct((n_dp, n_f) + own.shape, own.dtype),
-        in_specs=[pl.BlockSpec(memory_space=pl.ANY)],
-        out_specs=pl.BlockSpec(memory_space=pl.ANY),
+        functools.partial(gather_kernel, n_dp, n_f, cap),
+        out_shape=[
+            jax.ShapeDtypeStruct((n_dp, n_f) + own.shape, own.dtype),
+            jax.ShapeDtypeStruct((count, 1), jnp.int32),
+            jax.ShapeDtypeStruct((8, count), jnp.int32),
+            jax.ShapeDtypeStruct((slots, width), BF16),
+        ],
+        in_specs=[pl.BlockSpec(memory_space=pl.ANY), vmem, vmem, vmem],
+        out_specs=[pl.BlockSpec(memory_space=pl.ANY), vmem, vmem, vmem],
         scratch_shapes=[
+            pltpu.VMEM((count, width), BF16),
             pltpu.SemaphoreType.DMA((n_dp,)),
             pltpu.SemaphoreType.DMA((n_dp,)),
             pltpu.SemaphoreType.DMA((n_f // 2,)),
@@ -129,10 +151,10 @@
             pltpu.SemaphoreType.DMA((n_f // 2,)),
             pltpu.SemaphoreType.DMA,
         ],
-        compiler_params=pltpu.CompilerParams(collective_id=0, has_side_effects=True),
+        compiler_params=params(collective_id=0, has_side_effects=True),
         cost_estimate=cost(0, 100e6),
         name="gather_dense",
-    )(own)
+    )(own, ids, long_cot, short_cot)
 
 
 def scatter_kernel(
@@ -227,75 +249,49 @@
     )(grads)
 
 
-def dispatch_block(slot_row_ref, rows, block):
-    first = block * BLOCK
-    slot_id = first + lax.broadcasted_iota(jnp.int32, (BLOCK, 1), 0)
+def dispatch_block(slot_row_ref, rows, first, size):
+    slot_id = first + lax.broadcasted_iota(jnp.int32, (size, 1), 0)
     chosen = (slot_row_ref[0:1, :] == slot_id).astype(F32).astype(BF16)
     return dot(chosen, rows).astype(BF16)
 
 
-def cot_kernel(n_long, n_rows, cap, ids_ref, long_ref, short_ref, col_ref, row_ref, slots_ref, rows_ref):
-    i = pl.program_id(0)
-
-    @pl.when(i == 0)
-    def _():
-        count = ids_ref.shape[0]
-        lane = lax.broadcasted_iota(jnp.int32, (1, LANES), 1)
-        onehot = (ids_ref[...] == lane).astype(F32)
-        onehot_low = onehot.astype(BF16)
-        col = lax.broadcasted_iota(jnp.int32, (1, count), 1)
-        base = (lane * cap).astype(F32)
-        ones = jnp.ones((8, LANES), F32)
-        for start in range(0, count, ROWS):
-            row = start + lax.broadcasted_iota(jnp.int32, (ROWS, 1), 0)
-            before = dot((col < row).astype(F32).astype(BF16), onehot_low)
-            picked = (before + base) * onehot[start : start + ROWS]
-            col_ref[start : start + ROWS, :] = jnp.sum(picked, 1, keepdims=True).astype(jnp.int32)
-            row_ref[:, start : start + ROWS] = dot(
-                ones, picked, NT, precision=lax.Precision.HIGHEST
-            ).astype(jnp.int32)
-
-    @pl.when(i < n_long)
-    def _():
-        rows_ref[pl.ds(pl.multiple_of(i * ROWS, ROWS), ROWS), :] = long_ref[...].astype(BF16)
-
-    @pl.when((i >= n_long) & (i < n_rows))
-    def _():
-        rows_ref[pl.ds(pl.multiple_of(i * ROWS, ROWS), ROWS), :] = short_ref[...].astype(BF16)
-
-    @pl.when(i >= n_rows)
-    def _():
-        slots_ref[...] = dispatch_block(row_ref, rows_ref[...], i - n_rows)
-
-
-def route_cot(ids, long_cot, short_cot, slots, cap):
-    width = long_cot.shape[1]
-    n_long, n_short = long_cot.shape[0] // ROWS, short_cot.shape[0] // ROWS
-    n_rows = n_long + n_short
-    count = ids.shape[0]
-    return pl.pallas_call(
-        functools.partial(cot_kernel, n_long, n_rows, cap),
-        grid=(n_rows + slots // BLOCK,),
-        in_specs=[
-            constant((count, 1)),
-            pl.BlockSpec((ROWS, width), lambda i: (jnp.minimum(i, n_long - 1), 0)),
-            pl.BlockSpec((ROWS, width), lambda i: (jnp.clip(i - n_long, 0, n_short - 1), 0)),
-        ],
-        out_specs=[
-            pl.BlockSpec((count, 1), lambda i: (0, 0)),
-            pl.BlockSpec((8, count), lambda i: (0, 0)),
-            pl.BlockSpec((BLOCK, width), lambda i: (jnp.maximum(i - n_rows, 0), 0)),
-        ],
-        out_shape=[
-            jax.ShapeDtypeStruct((count, 1), jnp.int32),
-            jax.ShapeDtypeStruct((8, count), jnp.int32),
-            jax.ShapeDtypeStruct((slots, width), BF16),
-        ],
-        scratch_shapes=[pltpu.VMEM((count, width), BF16)],
-        compiler_params=params(),
-        cost_estimate=cost(2 * slots * count * width, 4 * count * width + 2 * slots * width),
-        name="route_cot",
-    )(ids, long_cot, short_cot)
+def number_slots(cap, ids_ref, col_ref, row_ref):
+    count = ids_ref.shape[0]
+    lane = lax.broadcasted_iota(jnp.int32, (1, LANES), 1)
+    onehot = (ids_ref[...] == lane).astype(F32)
+    onehot_low = onehot.astype(BF16)
+    col = lax.broadcasted_iota(jnp.int32, (1, count), 1)
+    base = (lane * cap).astype(F32)
+    ones = jnp.ones((8, LANES), F32)
+    for start in range(0, count, ROWS):
+        row = start + lax.broadcasted_iota(jnp.int32, (ROWS, 1), 0)
+        before = dot((col < row).astype(F32).astype(BF16), onehot_low)
+        picked = (before + base) * onehot[start : start + ROWS]
+        col_ref[start : start + ROWS, :] = jnp.sum(picked, 1, keepdims=True).astype(jnp.int32)
+        row_ref[:, start : start + ROWS] = dot(
+            ones, picked, NT, precision=lax.Precision.HIGHEST
+        ).astype(jnp.int32)
+
+
+def peers(n_f):
+    f = lax.axis_index("fsdp")
+    half = n_f // 2
+    chip, core = f // 2, lax.rem(f, 2)
+
+    def to(k):
+        return lax.rem(chip + k // 2, half) * 2 + lax.rem(core + lax.rem(k, 2), 2)
+
+    def source(k):
+        return lax.rem(chip + half - k // 2, half) * 2 + lax.rem(core + lax.rem(k, 2), 2)
+
+    return f, to, source
+
+
+def greet(n_f, to):
+    z = lax.axis_index("dp")
+    barrier = pltpu.get_barrier_semaphore()
+    for k in range(1, n_f):
+        pl.semaphore_signal(barrier, 1, device_id=(z, to(k)), device_id_type=MESH)
 
 
 def qkv_kernel(n_long, width, long_ref, short_ref, w_ref, vec_ref, qkv_ref, vec_scr):
@@ -500,14 +496,37 @@
     )(long_len, short_len, qkv, qkv, qkv, o, d_o, lse)
 
 
-def project_kernel(
-    n_long, n_rows, long_ref, short_ref, o_ref, w_ref, vec_ref, row_ref,
-    h_ref, slots_ref, rows_ref, vec_scr,
+def gelu_parts(pre):
+    scale = 0.7978845608028654
+    square = pre * pre
+    flat = jnp.tanh(scale * pre * (1.0 + 0.044715 * square))
+    half = 0.5 * (1.0 + flat)
+    slope = half + (0.5 * scale) * pre * (1.0 - flat * flat) * (1.0 + 0.134145 * square)
+    return half * pre, slope
+
+
+def forward_kernel(
+    n_f, n_long, n_rows, long_ref, short_ref, o_ref, w_ref, vec_ref, row_ref, g_ref, up_ref,
+    h_ref, there_ref, act_ref, slope_ref, gd_ref,
+    rows_ref, vec_scr, out_buf, in_buf, all_ref, send, recv,
 ):
     i = pl.program_id(0)
+    z = lax.axis_index("dp")
+    f, to, source = peers(n_f)
+    cap, width = out_buf.shape[1:]
+    n_up = n_rows + n_f
+    n_down = n_up + n_f
+    barrier = pltpu.get_barrier_semaphore()
+
+    def transfer(k):
+        return pltpu.make_async_remote_copy(
+            out_buf.at[k], in_buf.at[f], send.at[k], recv.at[k],
+            device_id=(z, to(k)), device_id_type=MESH,
+        )
 
     @pl.when(i == 0)
     def _():
+        greet(n_f, to)
         vec_scr[...] = vectors(vec_ref)
 
     def body(x_ref):
@@ -521,155 +540,210 @@
     pl.when(i < n_long)(lambda: body(long_ref))
     pl.when((i >= n_long) & (i < n_rows))(lambda: body(short_ref))
 
-    @pl.when(i >= n_rows)
-    def _():
-        slots_ref[...] = dispatch_block(row_ref, rows_ref[...], i - n_rows)
-
-
-def project(long_x, short_x, o, dense, slot_row, slots):
+    @pl.when(i == n_rows)
+    def _():
+        pl.semaphore_wait(barrier, n_f - 1)
+
+    @pl.when((i >= n_rows) & (i < n_up - 1))
+    def _():
+        k = i - n_rows + 1
+        out_buf[k] = dispatch_block(row_ref, rows_ref[...], to(k) * cap, cap)
+        transfer(k).start()
+
+    @pl.when(i == n_up - 1)
+    def _():
+        in_buf[f] = dispatch_block(row_ref, rows_ref[...], f * cap, cap)
+
+    @pl.when((i > n_up) & (i < n_down))
+    def _():
+        transfer(i - n_up).wait_recv()
+
+    @pl.when((i >= n_up) & (i < n_down))
+    def _():
+        origin = source(i - n_up)
+        rows = in_buf[origin]
+        here = pl.ds(pl.multiple_of(origin * cap, cap), cap)
+        for first in range(0, up_ref.shape[1], width):
+            cut = slice(first, first + width)
+            act, slope = gelu_parts(dot(rows, up_ref[:, cut]))
+            act = act.astype(BF16)
+            act_ref[:, cut] = act
+            slope_ref[:, cut] = slope.astype(BF16)
+            all_ref[here, cut] = act
+        there_ref[here, :] = rows
+
+    @pl.when(i >= n_down)
+    def _():
+        cut = pl.ds(pl.multiple_of((i - n_down) * width, width), width)
+        gd_ref[...] = dot(all_ref[:, cut], g_ref[...], TN).astype(BF16)
+
+    @pl.when(i == pl.num_programs(0) - 1)
+    def _():
+        for k in range(1, n_f):
+            transfer(k).wait_send()
+
+
+def forward_experts(long_x, short_x, o, dense, slot_row, g_there, up, n_f, cap):
     width = long_x.shape[1]
+    hidden = up.shape[1]
     n_long, n_short = long_x.shape[0] // ROWS, short_x.shape[0] // ROWS
     n_rows = n_long + n_short
+    n_up = n_rows + n_f
+    n_down = n_up + n_f
+    n_hidden = hidden // width
+    slots = n_f * cap
     count = o.shape[0]
+    tile = pl.BlockSpec((cap, hidden), lambda i: (jnp.clip(i - n_up, 0, n_f - 1), 0))
     return pl.pallas_call(
-        functools.partial(project_kernel, n_long, n_rows),
-        grid=(n_rows + slots // BLOCK,),
+        functools.partial(forward_kernel, n_f, n_long, n_rows),
+        grid=(n_down + n_hidden,),
         in_specs=[
             pl.BlockSpec((ROWS, width), lambda i: (jnp.minimum(i, n_long - 1), 0)),
             pl.BlockSpec((ROWS, width), lambda i: (jnp.clip(i - n_long, 0, n_short - 1), 0)),
             pl.BlockSpec((ROWS, width), lambda i: (jnp.minimum(i, n_rows - 1), 0)),
-            pl.BlockSpec((width, width), lambda i: (0, 3)),
+            pl.BlockSpec((width, width), lambda i: (0, 3), pipeline_mode=pl.Buffered(1)),
             pl.BlockSpec((width, LANES), lambda i: (0, 4 * width // LANES)),
             constant((8, count)),
+            constant((slots, width)),
+            constant((width, hidden)),
         ],
         out_specs=[
             pl.BlockSpec((ROWS, width), lambda i: (jnp.minimum(i, n_rows - 1), 0)),
-            pl.BlockSpec((BLOCK, width), lambda i: (jnp.maximum(i - n_rows, 0), 0)),
+            pl.BlockSpec((slots, width), lambda i: (0, 0)),
+            tile,
+            tile,
+            pl.BlockSpec((width, width), lambda i: (jnp.clip(i - n_down, 0, n_hidden - 1), 0)),
         ],
         out_shape=[
             jax.ShapeDtypeStruct((count, width), F32),
             jax.ShapeDtypeStruct((slots, width), BF16),
-        ],
-        scratch_shapes=[pltpu.VMEM((count, width), BF16), pltpu.VMEM((8, width), F32)],
-        compiler_params=params(),
-        cost_estimate=cost(2 * (slots + width) * count * width, 12 * count * width),
-        name="project",
-    )(long_x, short_x, o, dense, dense, slot_row)
-
-
-def gelu_parts(pre):
-    scale = 0.7978845608028654
-    square = pre * pre
-    flat = jnp.tanh(scale * pre * (1.0 + 0.044715 * square))
-    half = 0.5 * (1.0 + flat)
-    slope = half + (0.5 * scale) * pre * (1.0 - flat * flat) * (1.0 + 0.134145 * square)
-    return half * pre, slope
-
-
-def experts_kernel(n_r, b_ref, g_ref, up_ref, act_ref, slope_ref, gd_ref, all_ref):
-    r = pl.program_id(1)
-    pre = dot(b_ref[...], up_ref[...])
-    act, slope = gelu_parts(pre)
-    act = act.astype(BF16)
-    act_ref[...] = act
-    slope_ref[...] = slope.astype(BF16)
-    all_ref[pl.ds(pl.multiple_of(r * ROWS, ROWS), ROWS), :] = act
-
-    @pl.when(r == n_r - 1)
-    def _():
-        gd_ref[...] = dot(all_ref[...], g_ref[...], TN).astype(BF16)
-
-
-def experts_up(b_slots, g_slots, up):
-    rows, width = b_slots.shape
+            jax.ShapeDtypeStruct((slots, hidden), BF16),
+            jax.ShapeDtypeStruct((slots, hidden), BF16),
+            jax.ShapeDtypeStruct((hidden, width), BF16),
+        ],
+        scratch_shapes=[
+            pltpu.VMEM((count, width), BF16),
+            pltpu.VMEM((8, width), F32),
+            pltpu.VMEM((n_f, cap, width), BF16),
+            pltpu.VMEM((n_f, cap, width), BF16),
+            pltpu.VMEM((slots, hidden), BF16),
+            pltpu.SemaphoreType.DMA((n_f,)),
+            pltpu.SemaphoreType.DMA((n_f,)),
+        ],
+        compiler_params=params(collective_id=2, has_side_effects=True),
+        cost_estimate=cost(
+            2 * slots * width * (count + 2 * hidden), 60e6, slots * hidden
+        ),
+        name="forward_experts",
+    )(long_x, short_x, o, dense, dense, slot_row, g_there, up)
+
+
+def back_kernel(
+    n_f, b_ref, g_ref, act_ref, slope_ref, up_ref, down_ref, y_ref, db_ref, gu_ref,
+    out_buf, all_ref, send, recv, l_sem,
+):
+    i = pl.program_id(0)
+    z = lax.axis_index("dp")
+    f, to, source = peers(n_f)
+    cap, width = out_buf.shape[1:]
+    barrier = pltpu.get_barrier_semaphore()
+
+    def transfer(k):
+        return pltpu.make_async_remote_copy(
+            out_buf.at[k], db_ref.at[f], send.at[k], recv.at[k],
+            device_id=(z, source(k)), device_id_type=MESH,
+        )
+
+    keep = pltpu.make_async_copy(out_buf.at[0], db_ref.at[f], l_sem)
+
+    @pl.when(i == 0)
+    def _():
+        z_ = lax.axis_index("dp")
+        for k in range(1, n_f):
+            pl.semaphore_signal(barrier, 1, device_id=(z_, source(k)), device_id_type=MESH)
+
+    @pl.when(i < n_f)
+    def _():
+        k = n_f - 1 - i
+        here = pl.ds(pl.multiple_of(source(k) * cap, cap), cap)
+        g = g_ref[here, :]
+        d_b = jnp.zeros((cap, width), F32)
+        for first in range(0, up_ref.shape[1], width):
+            cut = slice(first, first + width)
+            d_act = dot(g, down_ref[cut, :], NT)
+            d_pre = (d_act * slope_ref[:, cut].astype(F32)).astype(BF16)
+            all_ref[here, cut] = d_pre
+            d_b = d_b + dot(d_pre, up_ref[:, cut], NT)
+        out_buf[k] = d_b.astype(BF16)
+
+    @pl.when(i == 0)
+    def _():
+        pl.semaphore_wait(barrier, n_f - 1)
+
+    @pl.when(i < n_f - 1)
+    def _():
+        transfer(n_f - 1 - i).start()
+
+    @pl.when(i == n_f - 1)
+    def _():
+        keep.start()
+
+    @pl.when(i < n_f)
+    def _():
+        here = pl.ds(pl.multiple_of(source(n_f - 1 - i) * cap, cap), cap)
+        y_ref[here, :] = dot(act_ref[...], down_ref[...]).astype(BF16)
+
+    @pl.when(i >= n_f)
+    def _():
+        cut = pl.ds(pl.multiple_of((i - n_f) * width, width), width)
+        gu_ref[...] = dot(b_ref[...], all_ref[:, cut], TN).astype(BF16)
+
+    @pl.when(i == pl.num_programs(0) - 1)
+    def _():
+        keep.wait()
+        for k in range(1, n_f):
+            transfer(k).wait_recv()
+        for k in range(1, n_f):
+            transfer(k).wait_send()
+
+
+def back_experts(b_there, g_there, act, slope, up, down, n_f, cap):
+    slots, width = b_there.shape
     hidden = up.shape[1]
-    n_r, n_f = rows // ROWS, hidden // width
-    tile = pl.BlockSpec((ROWS, width), lambda f, r: (r, f))
+    n_hidden = hidden // width
+    tile = pl.BlockSpec((cap, hidden), lambda i: (jnp.maximum(n_f - 1 - i, 0), 0))
     return pl.pallas_call(
-        functools.partial(experts_kernel, n_r),
-        grid=(n_f, n_r),
+        functools.partial(back_kernel, n_f),
+        grid=(n_f + n_hidden,),
         in_specs=[
-            pl.BlockSpec((ROWS, width), lambda f, r: (r, 0)),
-            constant((rows, width)),
-            pl.BlockSpec((width, width), lambda f, r: (0, f)),
-        ],
-        out_specs=[tile, tile, pl.BlockSpec((width, width), lambda f, r: (f, 0))],
-        out_shape=[
-            jax.ShapeDtypeStruct((rows, hidden), BF16),
-            jax.ShapeDtypeStruct((rows, hidden), BF16),
-            jax.ShapeDtypeStruct((hidden, width), BF16),
-        ],
-        scratch_shapes=[pltpu.VMEM((rows, width), BF16)],
-        compiler_params=params(),
-        cost_estimate=cost(4 * rows * width * hidden, 6 * rows * hidden, rows * hidden),
-        name="experts_up",
-    )(b_slots, g_slots, up)
-
-
-def experts_back_kernel(
-    n_f, n_r, b_ref, g_ref, act_ref, slope_ref, up_ref, down_ref,
-    y_ref, db_ref, gu_ref, y_acc, db_acc, all_ref,
-):
-    f, r = pl.program_id(0), pl.program_id(1)
-    rows = pl.ds(pl.multiple_of(r * ROWS, ROWS), ROWS)
-    d_act = dot(g_ref[rows, :], down_ref[...], NT)
-    d_pre = (d_act * slope_ref[...].astype(F32)).astype(BF16)
-    all_ref[rows, :] = d_pre
-    y = dot(act_ref[...], down_ref[...])
-    db = dot(d_pre, up_ref[...], NT)
-
-    @pl.when(f == 0)
-    def _():
-        y_acc[rows, :] = y
-        db_acc[rows, :] = db
-
-    @pl.when((f > 0) & (f < n_f - 1))
-    def _():
-        y_acc[rows, :] = y_acc[rows, :] + y
-        db_acc[rows, :] = db_acc[rows, :] + db
-
-    @pl.when(f == n_f - 1)
-    def _():
-        y_ref[rows, :] = (y_acc[rows, :] + y).astype(BF16)
-        db_ref[rows, :] = (db_acc[rows, :] + db).astype(BF16)
-
-    @pl.when(r == n_r - 1)
-    def _():
-        gu_ref[...] = dot(b_ref[...], all_ref[...], TN).astype(BF16)
-
-
-def experts_back(b_slots, g_slots, act, slope, up, down):
-    rows, width = b_slots.shape
-    hidden = up.shape[1]
-    n_r, n_f = rows // ROWS, hidden // width
-    tile = pl.BlockSpec((ROWS, width), lambda f, r: (r, f))
-    whole = pl.BlockSpec((rows, width), lambda f, r: (0, 0))
-    return pl.pallas_call(
-        functools.partial(experts_back_kernel, n_f, n_r),
-        grid=(n_f, n_r),
-        in_specs=[
-            constant((rows, width)),
-            constant((rows, width)),
+            constant((slots, width)),
+            constant((slots, width)),
             tile,
             tile,
-            pl.BlockSpec((width, width), lambda f, r: (0, f)),
-            pl.BlockSpec((width, width), lambda f, r: (f, 0)),
-        ],
-        out_specs=[whole, whole, pl.BlockSpec((width, width), lambda f, r: (0, f))],
+            constant((width, hidden)),
+            constant((hidden, width)),
+        ],
+        out_specs=[
+            pl.BlockSpec((slots, width), lambda i: (0, 0)),
+            pl.BlockSpec(memory_space=pl.ANY),
+            pl.BlockSpec((width, width), lambda i: (0, jnp.maximum(i - n_f, 0))),
+        ],
         out_shape=[
-            jax.ShapeDtypeStruct((rows, width), BF16),
-            jax.ShapeDtypeStruct((rows, width), BF16),
+            jax.ShapeDtypeStruct((slots, width), BF16),
+            jax.ShapeDtypeStruct((n_f, cap, width), BF16),
             jax.ShapeDtypeStruct((width, hidden), BF16),
         ],
         scratch_shapes=[
-            pltpu.VMEM((rows, width), F32),
-            pltpu.VMEM((rows, width), F32),
-            pltpu.VMEM((rows, width), BF16),
-        ],
-        compiler_params=params(),
-        cost_estimate=cost(8 * rows * width * hidden, 8 * rows * hidden),
-        name="experts_back",
-    )(b_slots, g_slots, act, slope, up, down)
+            pltpu.VMEM((n_f, cap, width), BF16),
+            pltpu.VMEM((slots, hidden), BF16),
+            pltpu.SemaphoreType.DMA((n_f,)),
+            pltpu.SemaphoreType.DMA((n_f,)),
+            pltpu.SemaphoreType.DMA,
+        ],
+        compiler_params=params(collective_id=3, has_side_effects=True),
+        cost_estimate=cost(8 * slots * width * hidden, 60e6),
+        name="back_experts",
+    )(b_there, g_there, act, slope, up, down)
 
 
 def combine_rows(col_ref, slots_ref):
@@ -872,25 +946,27 @@
     own = jnp.concatenate(
         [w_qkv, w_proj.T, jnp.pad(vec, ((0, 0), (0, LANES - vec.shape[1])))], 1
     )
-    dense = gather_dense(own, n_dp, n_f).reshape(n_dp * n_f * share, own.shape[1])
+    dense, slot_col, slot_row, g_slots = gather_dense(
+        own, expert_ids, gl, gs, n_dp, n_f, cap, slots
+    )
+    dense = dense.reshape(n_dp * n_f * share, own.shape[1])
 
     def exchange(rows):
         sent = lax.all_to_all(
-            rows.reshape(n_f, slots // n_f, width), "fsdp", split_axis=0, concat_axis=0, tiled=True
+            rows.reshape(n_f, cap, width), "fsdp", split_axis=0, concat_axis=0, tiled=True
         )
         return sent.reshape(slots, width)
 
-    slot_col, slot_row, g_slots = route_cot(expert_ids, gl, gs, slots, cap)
+    g_there = exchange(g_slots)
     qkv = make_qkv(xl, xs, dense)
-    g_there = exchange(g_slots)
     o, lse = attend(qkv, long_len, short_len, seqs)
-    h, b_slots = project(xl, xs, o, dense, slot_row, slots)
-    b_there = exchange(b_slots)
-    act, slope, grad_down = experts_up(b_there, g_there, up)
+    h, b_there, act, slope, grad_down = forward_experts(
+        xl, xs, o, dense, slot_row, g_there, up, n_f, cap
+    )
     grad_down = lax.psum_scatter(grad_down, "dp", scatter_dimension=0, tiled=True).astype(F32)
-    y, d_b, grad_up = experts_back(b_there, g_there, act, slope, up, down)
+    y, db_back, grad_up = back_experts(b_there, g_there, act, slope, up, down, n_f, cap)
+    db_back = db_back.reshape(slots, width)
     grad_up = lax.psum_scatter(grad_up, "dp", scatter_dimension=1, tiled=True).astype(F32)
-    db_back = exchange(d_b)
     y_back = exchange(y)
     d_h, d_o, grad_proj, grad_vec = hidden_back(h, slot_col, db_back, gl, gs, o, dense)
     long_out, short_out = finish(h, slot_col, y_back, n_long, n_short)

time: 519 us -> 450 us (0.87)
  blocking collectives: 82 us -> 0 us
  Pallas kernels: 388 us -> 400 us
    all_to_all x2 -> x0, blocking collectives: 82 us -> none  [exchange(): lax.all_to_all(rows.reshape(n_f, slots // n_f, width), 'fsdp', split_axis...]
    pallas_call x5 -> x3, Pallas kernels: 192 us -> 206 us  [the longest x1 82.1 us: forward_experts(): pl.pallas_call(functools.partial(forward_kernel, n_f, n_long, n_rows), gr...]
  transfers between devices with their start and end apart: 6 -> 6, of which waited for: 0 -> 0; matrix products, arithmetic and copies ran while one was open for 2% -> 2% of each run, Pallas kernels for 75% -> 90%
where the time goes in v2:
time: 450 us; the launch traced here: 445 us
  Pallas kernels  400 us (89%)
  between operations  15.3 us (3%)
  starting transfers between devices  10.8 us (2%)
  local copies, waits for them, and re-layouts  9.99 us (2%)
  other arithmetic  7.08 us (2%)
    pallas_call x1, Pallas kernels, forward_experts(): pl.pallas_call(functools.partial(forward_kernel, n_f, n_long, n_rows), gr...  82.1 us
    pallas_call x1, Pallas kernels, gather_dense(): pl.pallas_call(functools.partial(gather_kernel, n_dp, n_f, cap), out_shap...  67.6 us
    pallas_call x1, Pallas kernels, back_experts(): pl.pallas_call(functools.partial(back_kernel, n_f), grid=(n_f + n_hidden,...  56 us
    pallas_call x1, Pallas kernels, attend_back(): pl.pallas_call(functools.partial(attend_back_kernel, seqs), grid=(pairs,)...  52.2 us
    pallas_call x1, Pallas kernels, scatter_dense(): pl.pallas_call(functools.partial(scatter_kernel, n_dp, n_f), out_shape=ja...  50.7 us
    pallas_call x1, Pallas kernels, attend(): pl.pallas_call(functools.partial(attend_kernel, seqs), grid=(pairs,), in_...  27.8 us
    pallas_call x1, Pallas kernels, input_back(): pl.pallas_call(functools.partial(input_back_kernel, n_long, n_rows, width...  23 us
    pallas_call x1, Pallas kernels, hidden_back(): pl.pallas_call(functools.partial(hidden_back_kernel, n_long, n_rows), gri...  19.4 us
  transfers between devices with their start and end apart: 6, of which 0 were waited for; matrix products, arithmetic and copies ran while one was open for 2% of the time, Pallas kernels for 90%

profile of v2, /device:TPU:12, one launch (start us, length us, event | category | flops | bytes accessed | tf_op | source)
XLA Modules:
  0.0 445.1 jit_solution(16999297588960072224)
XLA Ops:
  7.2 0.0 all-gather.3.cloned.1.call-start
  7.2 0.7 all-gather.3.cloned.1.call-update
  7.9 0.0 all-gather.5.cloned.1.call-start
  8.0 0.7 all-gather.5.cloned.1.call-update
  8.7 0.7 pad_maximum_fusion
  9.4 0.1 copy.37
  9.5 1.9 copy.38.ids_ref
  11.4 0.7 fusion.1.own_ref
  12.1 67.6 %gather_dense.1 = (bf16[4,8,24,3200]{3,2,1,0:T(8,128)(2,1)}, s32[1536,1]{1,0:T(8,128)}, s32[8,1536]{1,0:T(8,128)}, bf16[2048,768]{1,0:T(8,128)(2,1)}) custom-call(bf16[24,3200]{1,0:T(8,128)(2,1)} %fusion.1.own_ref, s32[1536,1]{1,0:T(8,128)} %copy.38.ids_ref, f32[1024,768]{1,0:T(8,128)} %bitcast.39, f32[512,768]{1,0:T(8,128)} %bitcast.48), custom_call_target="tpu_custom_call" | custom-call | bytes 100000000 | tf_op jit(solution)/shard_map/gather_dense/pallas_call | solution.py:134
  79.7 4.2 all-to-all-start
  85.2 11.5 %make_qkv.1.q_ref.k_ref.v_ref = bf16[1536,2304]{1,0:T(8,128)(2,1)} custom-call(f32[1024,768]{1,0:T(8,128)} %bitcast.45, f32[512,768]{1,0:T(8,128)} %bitcast.50, bf16[768,3200]{1,0:T(8,128)(2,1)} %bitcast.30, bf16[768,3200]{1,0:T(8,128)(2,1)} %bitcast.31), custom_call_target="tpu_custom_call" | custom-call | flops 5435817984 | bytes 15335424 | tf_op jit(solution)/shard_map/make_qkv/pallas_call | solution.py:322
  96.8 27.8 %attend.1 = (bf16[1536,768]{1,0:T(8,128)(2,1)}, f32[1536,128]{1,0:T(8,128)}) custom-call(s32[1]{0:T(128)S(6)} %copy.39.long_len, s32[1]{0:T(128)S(6)} %copy.40.short_len, bf16[1536,2304]{1,0:T(8,128)(2,1)} %make_qkv.1.q_ref.k_ref.v_ref, bf16[1536,2304]{1,0:T(8,128)(2,1)} %make_qkv.1.q_ref.k_ref.v_ref, bf16[1536,2304]{1,0:T(8,128)(2,1)} %make_qkv.1.q_ref.k_ref.v_ref), custom_call_target="tpu_custom_call" | custom-call | flops 16000000000 | bytes 9437184 | tf_op jit(solution)/shard_map/attend/pallas_call | solution.py:400
  124.6 0.0 all-gather.3.cloned.1.call-done
  124.6 1.6 copy-done.1
  126.2 82.1 %forward_experts.1 = (f32[1536,768]{1,0:T(8,128)}, bf16[2048,768]{1,0:T(8,128)(2,1)}, bf16[2048,3072]{1,0:T(8,128)(2,1)}, bf16[2048,3072]{1,0:T(8,128)(2,1)}, bf16[3072,768]{1,0:T(8,128)(2,1)}) custom-call(f32[1024,768]{1,0:T(8,128)} %bitcast.46, f32[512,768]{1,0:T(8,128)} %bitcast.51, bf16[1536,768]{1,0:T(8,128)(2,1)} %get-tuple-element.39.o_ref, ...), custom_call_target="tpu_custom_call" | custom-call | flops 24159191040 | bytes 60000000 | tf_op jit(solution)/shard_map/forward_experts/pallas_call | solution.py:597
  208.3 0.0 reduce-scatter.5.cloned.1.call-update
  208.3 0.0 reduce-scatter.3.cloned.1.call-start
  208.4 0.0 all-gather.5.cloned.1.call-done
  208.4 56.0 %back_experts.1 = (bf16[2048,768]{1,0:T(8,128)(2,1)}, bf16[8,256,768]{2,1,0:T(8,128)(2,1)}, bf16[768,3072]{1,0:T(8,128)(2,1)}) custom-call(bf16[2048,768]{1,0:T(8,128)(2,1)} %get-tuple-element.44.b_ref, bf16[2048,768]{1,0:T(8,128)(2,1)} %bitcast.43, bf16[2048,3072]{1,0:T(8,128)(2,1)} %get-tuple-element.45.act_ref, ...), custom_call_target="tpu_custom_call" | custom-call | flops 38654705664 | bytes 60000000 | tf_op jit(solution)/shard_map/back_experts/pallas_call | solution.py:715
  264.4 0.0 reduce-scatter.3.cloned.1.call-update
  264.4 6.5 %all-to-all-start.1 = ((bf16[8,256,768]{2,1,0:T(8,128)(2,1)}), bf16[8,256,768]{2,1,0:T(8,128)(2,1)S(1)}, u32[]{:S(2)}, u32[]{:S(2)}) async-start(bf16[8,256,768]{2,1,0:T(8,128)(2,1)} %bitcast.14), calls=%async_computation.1 | async-start | bytes 6291456 | tf_op jit(solution)/shard_map/all_to_all | solution.py:955
  271.0 19.4 %hidden_back.1 = (f32[1536,768]{1,0:T(8,128)}, bf16[1536,768]{1,0:T(8,128)(2,1)}, bf16[768,768]{1,0:T(8,128)(2,1)}, f32[8,768]{1,0:T(8,128)}) custom-call(f32[1536,768]{1,0:T(8,128)} %get-tuple-element.42.h_ref, s32[1536,1]{1,0:T(8,128)} %get-tuple-element.43.col_ref, bf16[2048,768]{1,0:T(8,128)(2,1)} %bitcast.63, f32[1024,768]{1,0:T(8,128)} %bitcast.40, ...), custom_call_target="tpu_custom_call" | custom-call | flops 8455716864 | bytes 18874368 | tf_op jit(solution)/shard_map/hidden_back/pallas_call | solution.py:827
  290.4 52.2 %attend_back.1 = (bf16[1536,768]{1,0:T(8,128)(2,1)}, bf16[1536,768]{1,0:T(8,128)(2,1)}, bf16[1536,768]{1,0:T(8,128)(2,1)}) custom-call(s32[1]{0:T(128)S(6)} %copy.39.long_len, s32[1]{0:T(128)S(6)} %copy.40.short_len, bf16[1536,2304]{1,0:T(8,128)(2,1)} %make_qkv.1.q_ref.k_ref.v_ref, bf16[1536,2304]{1,0:T(8,128)(2,1)} %make_qkv.1.q_ref.k_ref.v_ref, ...), custom_call_target="tpu_custom_call" | custom-call | flops 40000000000 | bytes 18874368 | tf_op jit(solution)/shard_map/attend_back/pallas_call | solution.py:478
  342.6 23.0 %input_back.1 = (f32[1024,768]{1,0:T(8,128)}, f32[512,768]{1,0:T(8,128)}, bf16[768,3200]{1,0:T(8,128)(2,1)}) custom-call(f32[1024,768]{1,0:T(8,128)} %bitcast.47, f32[512,768]{1,0:T(8,128)} %bitcast.52, f32[1536,768]{1,0:T(8,128)} %get-tuple-element.51.dh_ref, bf16[1536,768]{1,0:T(8,128)(2,1)} %get-tuple-element.54.dq_ref, ...), custom_call_target="tpu_custom_call" | custom-call | flops 10871635968 | bytes 23592960 | tf_op jit(solution)/shard_map/input_back/pallas_call | solution.py:896
  365.6 50.7 %scatter_dense.1 = f32[24,3200]{1,0:T(8,128)} custom-call(bf16[4,8,24,3200]{3,2,1,0:T(8,128)(2,1)} %bitcast.38), custom_call_target="tpu_custom_call" | custom-call | bytes 100000000 | tf_op jit(solution)/shard_map/scatter_dense/pallas_call | solution.py:228
  416.3 1.6 slice.20
  417.9 1.6 slice_reduce_fusion
  419.5 1.5 slice_bitcast_fusion
  421.0 1.6 copy-done
  422.7 10.0 %finish.1 = (f32[1024,768]{1,0:T(8,128)}, f32[512,768]{1,0:T(8,128)}) custom-call(f32[1536,768]{1,0:T(8,128)} %get-tuple-element.42.h_ref, s32[1536,1]{1,0:T(8,128)} %get-tuple-element.43.col_ref, bf16[2048,768]{1,0:T(8,128)(2,1)} %bitcast.41), custom_call_target="tpu_custom_call" | custom-call | flops 4831838208 | bytes 12582912 | tf_op jit(solution)/shard_map/finish/pallas_call | solution.py:771
  432.7 2.8 bitcast_convert_fusion
  435.5 2.8 bitcast_convert_fusion.1
  (11 shorter events, 0.0 us)
Async XLA Ops:
  7.2 4.2 copy-start.3
  7.2 4.2 copy-start.2
  7.2 117.4 %all-gather.3.cloned.1.call-start = ((), (), s32[]{:S(2)}) async-start(), calls=%async_computation.4 | async-start | bytes 5898240 | tf_op jit(solution)/shard_map/all_gather | solution.py:942
  7.9 200.5 %all-gather.5.cloned.1.call-start = ((), (), s32[]{:S(2)}) async-start(), calls=%async_computation.5 | async-start | bytes 5898240 | tf_op jit(solution)/shard_map/all_gather | solution.py:943
  79.7 44.8 %all-to-all-start = ((bf16[8,256,768]{2,1,0:T(8,128)(2,1)}), bf16[8,256,768]{2,1,0:T(8,128)(2,1)S(1)}, u32[]{:S(2)}, u32[]{:S(2)}) async-start(bf16[8,256,768]{2,1,0:T(8,128)(2,1)} %bitcast.44), calls=%async_computation | async-start | bytes 6291456 | tf_op jit(solution)/shard_map/all_to_all | solution.py:955
  83.9 348.7 %reduce-scatter.5.cloned.1.call-start = ((), (), s32[]{:S(2)}) async-start(), calls=%async_computation.7 | async-start | bytes 5898240 | tf_op jit(solution)/shard_map/reduce_scatter | solution.py:966
  124.5 1.7 copy-start.1
  208.3 227.2 %reduce-scatter.3.cloned.1.call-start = ((), (), s32[]{:S(2)}) async-start(), calls=%async_computation.6 | async-start | bytes 5898240 | tf_op jit(solution)/shard_map/reduce_scatter | solution.py:969
  264.4 156.6 %all-to-all-start.1 = ((bf16[8,256,768]{2,1,0:T(8,128)(2,1)}), bf16[8,256,768]{2,1,0:T(8,128)(2,1)S(1)}, u32[]{:S(2)}, u32[]{:S(2)}) async-start(bf16[8,256,768]{2,1,0:T(8,128)(2,1)} %bitcast.14), calls=%async_computation.1 | async-start | bytes 6291456 | tf_op jit(solution)/shard_map/all_to_all | solution.py:955
  421.0 1.6 copy-start
Sparse Core Ops, SparseCore 0:
  9.6 97.2 all-gather.2
  108.4 89.0 all-gather.4
  208.5 85.0 reduce-scatter.4
  295.7 85.7 reduce-scatter.2

commit v3 on v2

--- a/solution.py
+++ b/solution.py
@@ -16,7 +16,10 @@
 LANES = 128
 ROWS = 512
 BLOCK = 256
+ATTEND = 512
+ATTEND_BACK = 512
 VMEM_LIMIT = 60 * 2**20
+N_CHUNKS = 3
 
 NN = (((1,), (0,)), ((), ()))
 NT = (((1,), (1,)), ((), ()))
@@ -61,6 +64,12 @@
         pl.BlockSpec((ROWS, width), lambda i: (jnp.minimum(i, n_long - 1), 0)),
         pl.BlockSpec((ROWS, width), lambda i: (jnp.maximum(i - n_long, 0), 0)),
     ]
+
+
+def column_chunks(columns):
+    tiles = columns // LANES
+    edges = [LANES * (tiles * c // N_CHUNKS) for c in range(N_CHUNKS + 1)]
+    return [slice(lo, hi) for lo, hi in zip(edges, edges[1:])]
 
 
 def gather_kernel(
@@ -81,47 +90,62 @@
     local.start()
     pl.semaphore_wait(barrier, n_dp - 1 + half)
 
-    z_copies = []
-    for k in range(1, n_dp):
-        copy = pltpu.make_async_remote_copy(
-            own_ref, out_ref.at[z, f], z_send.at[k], z_recv.at[k],
-            device_id=(lax.rem(z + k, n_dp), f), device_id_type=MESH,
-        )
-        copy.start()
-        z_copies.append(copy)
+    chunks = column_chunks(own_ref.shape[1])
+    z_copies, p_copies, c_copies = [], [], []
+
+    def send_z(c):
+        for k in range(1, n_dp):
+            copy = pltpu.make_async_remote_copy(
+                own_ref.at[:, chunks[c]], out_ref.at[z, f, :, chunks[c]],
+                z_send.at[c, k], z_recv.at[c, k],
+                device_id=(lax.rem(z + k, n_dp), f), device_id_type=MESH,
+            )
+            copy.start()
+            z_copies.append(copy)
+
+    def send_p(c):
+        for k in range(1, n_dp):
+            z_copies[c * (n_dp - 1) + k - 1].wait_recv()
+        for k in range(1, half):
+            copy = pltpu.make_async_remote_copy(
+                out_ref.at[:, f, :, chunks[c]], out_ref.at[:, f, :, chunks[c]],
+                p_send.at[c, k], p_recv.at[c, k],
+                device_id=(z, lax.rem(f + 2 * k, n_f)), device_id_type=MESH,
+            )
+            copy.start()
+            p_copies.append(copy)
+
+    def send_c(c):
+        for k in range(half):
+            if k:
+                p_copies[c * (half - 1) + k - 1].wait_recv()
+            column = lax.rem(f + n_f - 2 * k, n_f)
+            copy = pltpu.make_async_remote_copy(
+                out_ref.at[:, column, :, chunks[c]], out_ref.at[:, column, :, chunks[c]],
+                c_send.at[c, k], c_recv.at[c, k],
+                device_id=(z, partner), device_id_type=MESH,
+            )
+            copy.start()
+            c_copies.append(copy)
+
+    def fill(block, carry):
+        start = pl.multiple_of(block * BLOCK, BLOCK)
+        slots_ref[pl.ds(start, BLOCK), :] = dispatch_block(row_ref, rows_ref[...], start, BLOCK)
+        return carry
+
+    n_blocks = slots_ref.shape[0] // BLOCK
+    for c in range(len(chunks)):
+        send_z(c)
     number_slots(cap, ids_ref, col_ref, row_ref)
     n_long = long_ref.shape[0]
     rows_ref[:n_long, :] = long_ref[...].astype(BF16)
     rows_ref[n_long:, :] = short_ref[...].astype(BF16)
     local.wait()
-    for copy in z_copies:
-        copy.wait_recv()
-    p_copies = []
-    for k in range(1, half):
-        copy = pltpu.make_async_remote_copy(
-            out_ref.at[:, f], out_ref.at[:, f], p_send.at[k], p_recv.at[k],
-            device_id=(z, lax.rem(f + 2 * k, n_f)), device_id_type=MESH,
-        )
-        copy.start()
-        p_copies.append(copy)
-
-    def fill(block, carry):
-        start = pl.multiple_of(block * BLOCK, BLOCK)
-        slots_ref[pl.ds(start, BLOCK), :] = dispatch_block(row_ref, rows_ref[...], start, BLOCK)
-        return carry
-
-    lax.fori_loop(0, slots_ref.shape[0] // BLOCK, fill, 0)
-    c_copies = []
-    for k in range(half):
-        if k:
-            p_copies[k - 1].wait_recv()
-        column = lax.rem(f + n_f - 2 * k, n_f)
-        copy = pltpu.make_async_remote_copy(
-            out_ref.at[:, column], out_ref.at[:, column], c_send.at[k], c_recv.at[k],
-            device_id=(z, partner), device_id_type=MESH,
-        )
-        copy.start()
-        c_copies.append(copy)
+    for c in range(len(chunks)):
+        send_p(c)
+        lax.fori_loop(c * n_blocks // len(chunks), (c + 1) * n_blocks // len(chunks), fill, 0)
+    for c in range(len(chunks)):
+        send_c(c)
     for copy in c_copies:
         copy.wait_recv()
     for copy in z_copies + p_copies + c_copies:
@@ -143,110 +167,18 @@
         out_specs=[pl.BlockSpec(memory_space=pl.ANY), vmem, vmem, vmem],
         scratch_shapes=[
             pltpu.VMEM((count, width), BF16),
-            pltpu.SemaphoreType.DMA((n_dp,)),
-            pltpu.SemaphoreType.DMA((n_dp,)),
-            pltpu.SemaphoreType.DMA((n_f // 2,)),
-            pltpu.SemaphoreType.DMA((n_f // 2,)),
-            pltpu.SemaphoreType.DMA((n_f // 2,)),
-            pltpu.SemaphoreType.DMA((n_f // 2,)),
+            pltpu.SemaphoreType.DMA((N_CHUNKS, n_dp)),
+            pltpu.SemaphoreType.DMA((N_CHUNKS, n_dp)),
+            pltpu.SemaphoreType.DMA((N_CHUNKS, n_f // 2)),
+            pltpu.SemaphoreType.DMA((N_CHUNKS, n_f // 2)),
+            pltpu.SemaphoreType.DMA((N_CHUNKS, n_f // 2)),
+            pltpu.SemaphoreType.DMA((N_CHUNKS, n_f // 2)),
             pltpu.SemaphoreType.DMA,
         ],
         compiler_params=params(collective_id=0, has_side_effects=True),
         cost_estimate=cost(0, 100e6),
         name="gather_dense",
     )(own, ids, long_cot, short_cot)
-
-
-def scatter_kernel(
-    n_dp, n_f, in_ref, out_ref, got1, sum1, got2, sum2, got3,
-    c_send, c_recv, p_send, p_recv, z_send, z_recv,
-):
-    z = lax.axis_index("dp")
-    f = lax.axis_index("fsdp")
-    half = n_f // 2
-    parity = lax.rem(f, 2)
-    mine = f // 2
-    partner = f + 1 - 2 * parity
-    barrier = pltpu.get_barrier_semaphore()
-    for k in range(1, n_dp):
-        pl.semaphore_signal(barrier, 1, device_id=(lax.rem(z + k, n_dp), f), device_id_type=MESH)
-    for k in range(1, half):
-        pl.semaphore_signal(barrier, 1, device_id=(z, lax.rem(f + 2 * k, n_f)), device_id_type=MESH)
-    pl.semaphore_signal(barrier, 1, device_id=(z, partner), device_id_type=MESH)
-    pl.semaphore_wait(barrier, n_dp - 1 + half)
-
-    c_copies = []
-    order = list(range(1, half)) + [0]
-    for k in order:
-        slot = lax.rem(mine + k, half)
-        copy = pltpu.make_async_remote_copy(
-            in_ref.at[:, 2 * slot + 1 - parity], got1.at[slot], c_send.at[k], c_recv.at[k],
-            device_id=(z, partner), device_id_type=MESH,
-        )
-        copy.start()
-        c_copies.append(copy)
-    p_copies = []
-    for k, c_copy in zip(order, c_copies):
-        c_copy.wait_recv()
-        slot = lax.rem(mine + k, half)
-        sum1[slot] = (in_ref[:, 2 * slot + parity].astype(F32) + got1[slot].astype(F32)).astype(BF16)
-        if k:
-            copy = pltpu.make_async_remote_copy(
-                sum1.at[slot], got2.at[k], p_send.at[k], p_recv.at[k],
-                device_id=(z, lax.rem(f + 2 * k, n_f)), device_id_type=MESH,
-            )
-            copy.start()
-            p_copies.append(copy)
-    for copy in p_copies:
-        copy.wait_recv()
-    total = sum1[mine].astype(F32)
-    for k in range(1, half):
-        total = total + got2[k].astype(F32)
-    sum2[...] = total.astype(BF16)
-    z_copies = []
-    for k in range(1, n_dp):
-        there = lax.rem(z + k, n_dp)
-        copy = pltpu.make_async_remote_copy(
-            sum2.at[there], got3.at[k], z_send.at[k], z_recv.at[k],
-            device_id=(there, f), device_id_type=MESH,
-        )
-        copy.start()
-        z_copies.append(copy)
-    for copy in z_copies:
-        copy.wait_recv()
-    total = sum2[z].astype(F32)
-    for k in range(1, n_dp):
-        total = total + got3[k].astype(F32)
-    out_ref[...] = total
-    for copy in c_copies + p_copies + z_copies:
-        copy.wait_send()
-
-
-def scatter_dense(grads, n_dp, n_f):
-    block = grads.shape[2:]
-    half = n_f // 2
-    return pl.pallas_call(
-        functools.partial(scatter_kernel, n_dp, n_f),
-        out_shape=jax.ShapeDtypeStruct(block, F32),
-        in_specs=[pl.BlockSpec(memory_space=pltpu.VMEM)],
-        out_specs=pl.BlockSpec(memory_space=pltpu.VMEM),
-        scratch_shapes=[
-            pltpu.VMEM((half, n_dp) + block, BF16),
-            pltpu.VMEM((half, n_dp) + block, BF16),
-            pltpu.VMEM((half, n_dp) + block, BF16),
-            pltpu.VMEM((n_dp,) + block, BF16),
-            pltpu.VMEM((n_dp,) + block, BF16),
-            pltpu.SemaphoreType.DMA((half,)),
-            pltpu.SemaphoreType.DMA((half,)),
-            pltpu.SemaphoreType.DMA((half,)),
-            pltpu.SemaphoreType.DMA((half,)),
-            pltpu.SemaphoreType.DMA((n_dp,)),
-            pltpu.SemaphoreType.DMA((n_dp,)),
-        ],
-        compiler_params=params(collective_id=1, has_side_effects=True),
-        cost_estimate=cost(0, 100e6),
-        name="scatter_dense",
-    )(grads)
 
 
 def dispatch_block(slot_row_ref, rows, first, size):
@@ -351,6 +283,18 @@
     return (lane < HEAD_DIM, lane >= HEAD_DIM)
 
 
+def marked(q, k, valid, first, masks, lane):
+    key_pos = first + lax.broadcasted_iota(jnp.int32, (k.shape[0], 1), 0)
+    bias = jnp.where(key_pos < valid, 0.0, MASKED).astype(BF16)
+    found = []
+    for head in range(2):
+        spare = HEAD_DIM * (1 - head)
+        qh = jnp.where(masks[head], q, jnp.where(lane == spare, 1.0, 0.0).astype(BF16))
+        kh = jnp.where(masks[head], k, jnp.where(lane == spare, bias, jnp.zeros_like(bias)))
+        found.append((qh, kh))
+    return found
+
+
 def attend_kernel(seqs, long_len, short_len, q_ref, k_ref, v_ref, o_ref, lse_ref):
     pair = pl.program_id(0)
     masks = head_masks()
@@ -360,38 +304,41 @@
     def _():
         lse_ref[...] = jnp.zeros_like(lse_ref)
 
-    causal = lax.broadcasted_iota(jnp.int32, (BLOCK, BLOCK), 1) <= lax.broadcasted_iota(
-        jnp.int32, (BLOCK, BLOCK), 0
+    causal = lax.broadcasted_iota(jnp.int32, (ATTEND, ATTEND), 0) <= lax.broadcasted_iota(
+        jnp.int32, (ATTEND, ATTEND), 1
     )
+    upper = lax.broadcasted_iota(jnp.int32, (LANES, 1), 0) < HEAD_DIM
     for start, length, which, index in seqs:
         valid = (short_len if which else long_len)[index]
-        key_pos = lax.broadcasted_iota(jnp.int32, (1, length), 1)
-        bias = jnp.where(key_pos < valid, 0.0, MASKED)
-        for first in range(0, length, BLOCK):
-            here = slice(start + first, start + first + BLOCK)
-            past = slice(start, start + first)
-            q = q_ref[here, :]
+        rows = slice(start, start + length)
+        heads = marked(q_ref[rows, :], k_ref[rows, :], valid, 0, masks, lane)
+        v = jnp.transpose(v_ref[rows, :].astype(F32))
+        values = [
+            jnp.where(upper, v, 1.0).astype(BF16),
+            jnp.where(upper, 1.0, v).astype(BF16),
+        ]
+        for first in range(0, length, ATTEND):
+            last = first + ATTEND
             outs = []
-            stats = jnp.zeros((BLOCK, LANES), F32)
-            for head in range(2):
-                qh = jnp.where(masks[head], q, jnp.zeros_like(q))
-                near = dot(qh, k_ref[here, :], NT) + bias[:, first : first + BLOCK]
+            for head, (qh, kh) in enumerate(heads):
+                qb = qh[first:last]
+                near = dot(kh[first:last], qb, NT)
                 near = jnp.where(causal, near, MASKED)
-                top = jnp.max(near, 1, keepdims=True)
+                top = jnp.max(near, 0, keepdims=True)
                 if first:
-                    far = dot(qh, k_ref[past, :], NT) + bias[:, :first]
-                    top = jnp.maximum(top, jnp.max(far, 1, keepdims=True))
-                near = jnp.exp(near - top)
-                total = jnp.sum(near, 1, keepdims=True)
-                out = dot(near.astype(BF16), v_ref[here, :])
+                    far = dot(kh[:first], qb, NT)
+                    top = jnp.maximum(top, jnp.max(far, 0, keepdims=True))
+                out = dot(values[head][:, first:last], jnp.exp(near - top).astype(BF16))
                 if first:
-                    far = jnp.exp(far - top)
-                    total = total + jnp.sum(far, 1, keepdims=True)
-                    out = out + dot(far.astype(BF16), v_ref[past, :])
+                    out = out + dot(values[head][:, :first], jnp.exp(far - top).astype(BF16))
+                total = out[LANES - 1 : LANES] if head == 0 else out[0:1]
                 outs.append(out * (1.0 / total))
-                stats = jnp.where(lane == 2 * pair + head, top + jnp.log(total), stats)
-            o_ref[here, :] = jnp.where(masks[0], outs[0], outs[1]).astype(BF16)
-            lse_ref[here, :] = lse_ref[here, :] + stats
+                lse_ref[pl.ds(2 * pair + head, 1), start + first : start + last] = top + jnp.log(
+                    total
+                )
+            o_ref[start + first : start + last, :] = jnp.transpose(
+                jnp.where(upper, outs[0], outs[1])
+            ).astype(BF16)
 
 
 def attend(qkv, long_len, short_len, seqs):
@@ -408,11 +355,11 @@
         ],
         out_specs=[
             pl.BlockSpec((count, LANES), lambda i: (0, i)),
-            pl.BlockSpec((count, LANES), lambda i: (0, 0)),
+            pl.BlockSpec((LANES, count), lambda i: (0, 0)),
         ],
         out_shape=[
             jax.ShapeDtypeStruct((count, width), BF16),
-            jax.ShapeDtypeStruct((count, LANES), F32),
+            jax.ShapeDtypeStruct((LANES, count), F32),
         ],
         compiler_params=params(),
         cost_estimate=cost(16e9, 8 * count * width, 10e6),
@@ -422,58 +369,66 @@
 
 def attend_back_kernel(
     seqs, long_len, short_len, q_ref, k_ref, v_ref, o_ref, do_ref, lse_ref,
-    dq_ref, dk_ref, dv_ref, acc_ref, row_ref,
+    d_ref, dkt_ref, dvt_ref, lse_scr,
 ):
     pair = pl.program_id(0)
     masks = head_masks()
-    lane = lax.broadcasted_iota(jnp.int32, (8, LANES), 1)
-    which_row = lax.broadcasted_iota(jnp.int32, (8, LANES), 0)
-    pick = (lane == 2 * pair + which_row).astype(F32) * (which_row < 2).astype(F32)
-    split = (lane // HEAD_DIM == which_row).astype(F32)
-    row_ref[0:8, :] = dot(pick, lse_ref[...], NT, precision=lax.Precision.HIGHEST)
-    row_ref[8:16, :] = dot(
-        split, do_ref[...].astype(F32) * o_ref[...].astype(F32), NT,
-        precision=lax.Precision.HIGHEST,
-    )
-    acc_ref[...] = jnp.zeros_like(acc_ref)
-    causal = lax.broadcasted_iota(jnp.int32, (BLOCK, BLOCK), 0) <= lax.broadcasted_iota(
-        jnp.int32, (BLOCK, BLOCK), 1
+    lane = lax.broadcasted_iota(jnp.int32, (1, LANES), 1)
+
+    @pl.when(pair == 0)
+    def _():
+        lse_scr[...] = jnp.transpose(lse_ref[...])
+
+    causal = lax.broadcasted_iota(jnp.int32, (ATTEND_BACK, ATTEND_BACK), 1) <= (
+        lax.broadcasted_iota(jnp.int32, (ATTEND_BACK, ATTEND_BACK), 0)
     )
     for start, length, which, index in seqs:
         valid = (short_len if which else long_len)[index]
-        for first in range(0, length, BLOCK):
-            here = slice(start + first, start + first + BLOCK)
-            k, v = k_ref[here, :], v_ref[here, :]
-            key_pos = first + lax.broadcasted_iota(jnp.int32, (BLOCK, 1), 0)
-            inside = key_pos < valid
-            dk = jnp.zeros((BLOCK, LANES), F32)
-            dv = jnp.zeros((BLOCK, LANES), F32)
-            for head in range(2):
-                kh = jnp.where(masks[head], k, jnp.zeros_like(k))
-                for rows, allowed in (
-                    (here, inside & causal),
-                    (slice(here.stop, start + length), inside),
-                ):
-                    if rows.start == rows.stop:
+        rows = slice(start, start + length)
+        q, k, v, do = q_ref[rows, :], k_ref[rows, :], v_ref[rows, :], do_ref[rows, :]
+        heads = marked(q, k, valid, 0, masks, lane)
+        q_t = jnp.transpose(q.astype(F32)).astype(BF16)
+        do_t = jnp.transpose(do.astype(F32)).astype(BF16)
+        both = do.astype(F32) * o_ref[rows, :].astype(F32)
+        lse_all = lse_scr[rows, :]
+        dkt_ref[...] = jnp.zeros_like(dkt_ref)
+        dvt_ref[...] = jnp.zeros_like(dvt_ref)
+        for first in range(0, length, ATTEND_BACK):
+            last = first + ATTEND_BACK
+            dqs = []
+            for head, (qh, kh) in enumerate(heads):
+                part = slice(HEAD_DIM * head, HEAD_DIM * (head + 1))
+                doh = jnp.where(masks[head], do[first:last], jnp.zeros_like(do[first:last]))
+                lse = jnp.sum(
+                    jnp.where(lane == 2 * pair + head, lse_all[first:last], 0.0), 1, keepdims=True
+                )
+                delta = jnp.sum(jnp.where(masks[head], both[first:last], 0.0), 1, keepdims=True)
+                dq = jnp.zeros((ATTEND_BACK, LANES), F32)
+                for keys in (slice(0, first), slice(first, last)):
+                    if keys.stop == keys.start:
                         continue
-                    q, do = q_ref[rows, :], do_ref[rows, :]
-                    qh = jnp.where(masks[head], q, jnp.zeros_like(q))
-                    doh = jnp.where(masks[head], do, jnp.zeros_like(do))
-                    scores = dot(k, qh, NT)
-                    p = jnp.where(allowed, jnp.exp(scores - row_ref[head : head + 1, rows]), 0.0)
-                    dp = dot(v, doh, NT)
-                    ds = (p * (dp - row_ref[8 + head : 9 + head, rows])).astype(BF16)
-                    dv = dv + dot(p.astype(BF16), doh)
-                    dk = dk + dot(ds, qh)
-                    acc_ref[rows, :] = acc_ref[rows, :] + dot(ds, kh, TN)
-            dk_ref[here, :] = dk.astype(BF16)
-            dv_ref[here, :] = dv.astype(BF16)
-    dq_ref[...] = (acc_ref[...] * HEAD_DIM ** (-0.5)).astype(BF16)
+                    p = jnp.exp(dot(qh[first:last], kh[keys], NT) - lse)
+                    if keys.start == first:
+                        p = jnp.where(causal, p, 0.0)
+                    dp = dot(doh, v[keys], NT)
+                    ds = (p * (dp - delta)).astype(BF16)
+                    dvt_ref[part, keys] = dvt_ref[part, keys] + dot(
+                        do_t[part, first:last], p.astype(BF16)
+                    )
+                    dkt_ref[part, keys] = dkt_ref[part, keys] + dot(q_t[part, first:last], ds)
+                    dq = dq + dot(ds, k[keys])
+                dqs.append(dq)
+            d_ref[0, start + first : start + last, :] = (
+                jnp.where(masks[0], dqs[0], dqs[1]) * HEAD_DIM ** (-0.5)
+            ).astype(BF16)
+        d_ref[1, rows, :] = jnp.transpose(dkt_ref[:, :length]).astype(BF16)
+        d_ref[2, rows, :] = jnp.transpose(dvt_ref[:, :length]).astype(BF16)
 
 
 def attend_back(qkv, o, d_o, lse, long_len, short_len, seqs):
     count, width = o.shape
     pairs = width // LANES
+    longest = max(length for _, length, _, _ in seqs)
     one = pl.BlockSpec((count, LANES), lambda i: (0, i))
     return pl.pallas_call(
         functools.partial(attend_back_kernel, seqs),
@@ -485,11 +440,15 @@
             pl.BlockSpec((count, LANES), lambda i: (0, i + 2 * pairs)),
             one,
             one,
-            constant((count, LANES)),
-        ],
-        out_specs=[one, one, one],
-        out_shape=[jax.ShapeDtypeStruct((count, width), BF16)] * 3,
-        scratch_shapes=[pltpu.VMEM((count, LANES), F32), pltpu.VMEM((16, count), F32)],
+            constant((LANES, count)),
+        ],
+        out_specs=pl.BlockSpec((3, count, LANES), lambda i: (0, 0, i)),
+        out_shape=jax.ShapeDtypeStruct((3, count, width), BF16),
+        scratch_shapes=[
+            pltpu.VMEM((LANES, longest), F32),
+            pltpu.VMEM((LANES, longest), F32),
+            pltpu.VMEM((count, LANES), F32),
+        ],
         compiler_params=params(),
         cost_estimate=cost(40e9, 16 * count * width, 10e6),
         name="attend_back",
@@ -638,14 +597,68 @@
     )(long_x, short_x, o, dense, dense, slot_row, g_there, up)
 
 
+def own_kernel(
+    n_f, z_ref, b_ref, g_ref, act_ref, slope_ref, up_ref, down_ref, y_ref, db_ref, gu_ref, all_ref
+):
+    i = pl.program_id(0)
+    _, _, source = peers(n_f)
+    cap = y_ref.shape[0]
+
+    @pl.when(i < n_f)
+    def _():
+        here = pl.ds(pl.multiple_of(source(i) * cap, cap), cap)
+        d_act = dot(g_ref[here, :], down_ref[...], NT)
+        d_pre = (d_act * slope_ref[...].astype(F32)).astype(BF16)
+        all_ref[here, :] = d_pre
+        db_ref[...] = dot(d_pre, up_ref[...], NT)
+        y_ref[...] = dot(act_ref[...], down_ref[...])
+
+    @pl.when(i >= n_f)
+    def _():
+        gu_ref[...] = dot(b_ref[...], all_ref[...], TN).astype(BF16)
+
+
+def own_experts(z, b_there, g_there, act, slope, up, own_down, n_f, cap):
+    slots, width = b_there.shape
+    piece = own_down.shape[0]
+    tile = pl.BlockSpec((cap, piece), lambda i, z: (jnp.minimum(i, n_f - 1), z[0]))
+    out = pl.BlockSpec((cap, width), lambda i, z: (jnp.minimum(i, n_f - 1), 0))
+    return pl.pallas_call(
+        functools.partial(own_kernel, n_f),
+        grid_spec=pltpu.PrefetchScalarGridSpec(
+            num_scalar_prefetch=1,
+            grid=(n_f + 1,),
+            in_specs=[
+                constant((slots, width)),
+                constant((slots, width)),
+                tile,
+                tile,
+                pl.BlockSpec((width, piece), lambda i, z: (0, z[0])),
+                constant((piece, width)),
+            ],
+            out_specs=[out, out, pl.BlockSpec((width, piece), lambda i, z: (0, 0))],
+            scratch_shapes=[pltpu.VMEM((slots, piece), BF16)],
+        ),
+        out_shape=[
+            jax.ShapeDtypeStruct((slots, width), F32),
+            jax.ShapeDtypeStruct((slots, width), F32),
+            jax.ShapeDtypeStruct((width, piece), BF16),
+        ],
+        compiler_params=params(),
+        cost_estimate=cost(8 * slots * width * piece, 30e6),
+        name="own_experts",
+    )(z, b_there, g_there, act, slope, up, own_down)
+
+
 def back_kernel(
-    n_f, b_ref, g_ref, act_ref, slope_ref, up_ref, down_ref, y_ref, db_ref, gu_ref,
-    out_buf, all_ref, send, recv, l_sem,
+    n_dp, n_f, b_ref, g_ref, act_ref, slope_ref, up_ref, down_ref, y0_ref, db0_ref, gu0_ref,
+    y_ref, db_ref, gu_ref, out_buf, all_ref, send, recv, l_sem,
 ):
     i = pl.program_id(0)
     z = lax.axis_index("dp")
     f, to, source = peers(n_f)
     cap, width = out_buf.shape[1:]
+    piece = gu_ref.shape[1]
     barrier = pltpu.get_barrier_semaphore()
 
     def transfer(k):
@@ -654,26 +667,26 @@
             device_id=(z, source(k)), device_id_type=MESH,
         )
 
+    def other(m):
+        return pl.ds(pl.multiple_of(lax.rem(z + m, n_dp) * piece, piece), piece)
+
     keep = pltpu.make_async_copy(out_buf.at[0], db_ref.at[f], l_sem)
 
     @pl.when(i == 0)
     def _():
-        z_ = lax.axis_index("dp")
-        for k in range(1, n_f):
-            pl.semaphore_signal(barrier, 1, device_id=(z_, source(k)), device_id_type=MESH)
+        greet(n_f, to)
 
     @pl.when(i < n_f)
     def _():
         k = n_f - 1 - i
         here = pl.ds(pl.multiple_of(source(k) * cap, cap), cap)
         g = g_ref[here, :]
-        d_b = jnp.zeros((cap, width), F32)
-        for first in range(0, up_ref.shape[1], width):
-            cut = slice(first, first + width)
-            d_act = dot(g, down_ref[cut, :], NT)
-            d_pre = (d_act * slope_ref[:, cut].astype(F32)).astype(BF16)
-            all_ref[here, cut] = d_pre
-            d_b = d_b + dot(d_pre, up_ref[:, cut], NT)
+        d_b = db0_ref[...]
+        for m in range(1, n_dp):
+            d_act = dot(g, down_ref[other(m), :], NT)
+            d_pre = (d_act * slope_ref[:, other(m)].astype(F32)).astype(BF16)
+            all_ref[here, other(m)] = d_pre
+            d_b = d_b + dot(d_pre, up_ref[:, other(m)], NT)
         out_buf[k] = d_b.astype(BF16)
 
     @pl.when(i == 0)
@@ -691,11 +704,18 @@
     @pl.when(i < n_f)
     def _():
         here = pl.ds(pl.multiple_of(source(n_f - 1 - i) * cap, cap), cap)
-        y_ref[here, :] = dot(act_ref[...], down_ref[...]).astype(BF16)
-
-    @pl.when(i >= n_f)
-    def _():
-        cut = pl.ds(pl.multiple_of((i - n_f) * width, width), width)
+        y = y0_ref[...]
+        for m in range(1, n_dp):
+            y = y + dot(act_ref[:, other(m)], down_ref[other(m), :])
+        y_ref[here, :] = y.astype(BF16)
+
+    @pl.when((i >= n_f) & (i - n_f == z))
+    def _():
+        gu_ref[...] = gu0_ref[...]
+
+    @pl.when((i >= n_f) & (i - n_f != z))
+    def _():
+        cut = pl.ds(pl.multiple_of((i - n_f) * piece, piece), piece)
         gu_ref[...] = dot(b_ref[...], all_ref[:, cut], TN).astype(BF16)
 
     @pl.when(i == pl.num_programs(0) - 1)
@@ -707,14 +727,15 @@
             transfer(k).wait_send()
 
 
-def back_experts(b_there, g_there, act, slope, up, down, n_f, cap):
+def back_experts(b_there, g_there, act, slope, up, down, y0, db0, gu0, n_dp, n_f, cap):
     slots, width = b_there.shape
     hidden = up.shape[1]
-    n_hidden = hidden // width
+    piece = hidden // n_dp
     tile = pl.BlockSpec((cap, hidden), lambda i: (jnp.maximum(n_f - 1 - i, 0), 0))
+    begun = pl.BlockSpec((cap, width), lambda i: (jnp.maximum(n_f - 1 - i, 0), 0))
     return pl.pallas_call(
-        functools.partial(back_kernel, n_f),
-        grid=(n_f + n_hidden,),
+        functools.partial(back_kernel, n_dp, n_f),
+        grid=(n_f + n_dp,),
         in_specs=[
             constant((slots, width)),
             constant((slots, width)),
@@ -722,11 +743,14 @@
             tile,
             constant((width, hidden)),
             constant((hidden, width)),
+            begun,
+            begun,
+            constant((width, piece)),
         ],
         out_specs=[
             pl.BlockSpec((slots, width), lambda i: (0, 0)),
             pl.BlockSpec(memory_space=pl.ANY),
-            pl.BlockSpec((width, width), lambda i: (0, jnp.maximum(i - n_f, 0))),
+            pl.BlockSpec((width, piece), lambda i: (0, jnp.maximum(i - n_f, 0))),
         ],
         out_shape=[
             jax.ShapeDtypeStruct((slots, width), BF16),
@@ -741,50 +765,15 @@
             pltpu.SemaphoreType.DMA,
         ],
         compiler_params=params(collective_id=3, has_side_effects=True),
-        cost_estimate=cost(8 * slots * width * hidden, 60e6),
+        cost_estimate=cost(6 * slots * width * hidden, 60e6),
         name="back_experts",
-    )(b_there, g_there, act, slope, up, down)
+    )(b_there, g_there, act, slope, up, down, y0, db0, gu0)
 
 
 def combine_rows(col_ref, slots_ref):
     slot_id = lax.broadcasted_iota(jnp.int32, (1, slots_ref.shape[0]), 1)
     chosen = (col_ref[...] == slot_id).astype(F32).astype(BF16)
     return dot(chosen, slots_ref[...])
-
-
-def finish_kernel(n_long, h_ref, col_ref, y_ref, long_ref, short_ref):
-    i = pl.program_id(0)
-    out = h_ref[...] + combine_rows(col_ref, y_ref)
-
-    @pl.when(i < n_long)
-    def _():
-        long_ref[...] = out
-
-    @pl.when(i >= n_long)
-    def _():
-        short_ref[...] = out
-
-
-def finish(h, slot_col, y_back, n_long, n_short):
-    count, width = h.shape
-    slots = y_back.shape[0]
-    return pl.pallas_call(
-        functools.partial(finish_kernel, n_long),
-        grid=(n_long + n_short,),
-        in_specs=[
-            pl.BlockSpec((ROWS, width), lambda i: (i, 0)),
-            pl.BlockSpec((ROWS, 1), lambda i: (i, 0)),
-            constant((slots, width)),
-        ],
-        out_specs=long_short(width, n_long),
-        out_shape=[
-            jax.ShapeDtypeStruct((n_long * ROWS, width), F32),
-            jax.ShapeDtypeStruct((n_short * ROWS, width), F32),
-        ],
-        compiler_params=params(),
-        cost_estimate=cost(2 * slots * count * width, 8 * count * width + 2 * slots * width),
-        name="finish",
-    )(h, slot_col, y_back)
 
 
 def hidden_back_kernel(
@@ -802,8 +791,8 @@
     def body(cot_ref):
         d_b = combine_rows(col_ref, db_ref)
         normed, inv_scale = norm_parts(h_ref[...])
-        gv_ref[0:1, :] = gv_ref[0:1, :] + jnp.sum(d_b * normed, 0, keepdims=True)
-        gv_ref[1:2, :] = gv_ref[1:2, :] + jnp.sum(d_b, 0, keepdims=True)
+        gv_ref[2:3, :] = gv_ref[2:3, :] + jnp.sum(d_b * normed, 0, keepdims=True)
+        gv_ref[3:4, :] = gv_ref[3:4, :] + jnp.sum(d_b, 0, keepdims=True)
         d_h = cot_ref[...] + norm_back(d_b * vec_scr[2:3, :], normed, inv_scale)
         dh_ref[...] = d_h
         d_attn = d_h.astype(BF16)
@@ -838,13 +827,13 @@
             row,
             row,
             pl.BlockSpec((width, width), lambda i: (0, 0)),
-            pl.BlockSpec((8, width), lambda i: (0, 0)),
+            pl.BlockSpec((LANES, width), lambda i: (0, 0)),
         ],
         out_shape=[
             jax.ShapeDtypeStruct((count, width), F32),
             jax.ShapeDtypeStruct((count, width), BF16),
             jax.ShapeDtypeStruct((width, width), BF16),
-            jax.ShapeDtypeStruct((8, width), F32),
+            jax.ShapeDtypeStruct((LANES, width), F32),
         ],
         scratch_shapes=[pltpu.VMEM((width, width), F32), pltpu.VMEM((8, width), F32)],
         compiler_params=params(),
@@ -853,9 +842,9 @@
     )(h, slot_col, db_back, long_cot, short_cot, o, dense, dense)
 
 
-def input_back_kernel(
-    n_long, n_rows, width, long_ref, short_ref, dh_ref, dq_ref, dk_ref, dv_ref, w_ref, vec_ref,
-    gp_ref, gv_ref, lg_ref, sg_ref, out_ref, acc_ref, vec_scr, gv_scr,
+def grads_kernel(
+    n_long, n_rows, width, long_ref, short_ref, d_ref, w_ref, vec_ref, gp_ref, gv_ref,
+    out_ref, acc_ref, vec_scr, sum_scr,
 ):
     i = pl.program_id(0)
 
@@ -863,66 +852,424 @@
     def _():
         vec_scr[...] = vectors(vec_ref)
         acc_ref[...] = jnp.zeros_like(acc_ref)
-        gv_scr[...] = jnp.zeros_like(gv_scr)
-        gv_scr[2:4, :] = gv_ref[0:2, :]
-
-    def body(x_ref, grad_ref):
-        normed, inv_scale = norm_parts(x_ref[...])
+        sum_scr[...] = jnp.zeros_like(sum_scr)
+
+    def body(x_ref):
+        normed, _ = norm_parts(x_ref[...])
         rows = (normed * vec_scr[0:1, :] + vec_scr[1:2, :]).astype(BF16)
-        entered = jnp.zeros_like(normed)
-        for part, d_ref in enumerate((dq_ref, dk_ref, dv_ref)):
+        for part in range(3):
             cut = slice(part * width, (part + 1) * width)
-            entered = entered + dot(d_ref[...], w_ref[:, cut], NT)
-            acc_ref[:, cut] = acc_ref[:, cut] + dot(rows, d_ref[...], TN)
-        gv_scr[0:1, :] = gv_scr[0:1, :] + jnp.sum(entered * normed, 0, keepdims=True)
-        gv_scr[1:2, :] = gv_scr[1:2, :] + jnp.sum(entered, 0, keepdims=True)
-        grad_ref[...] = dh_ref[...] + norm_back(entered * vec_scr[0:1, :], normed, inv_scale)
-
-    pl.when(i < n_long)(lambda: body(long_ref, lg_ref))
-    pl.when(i >= n_long)(lambda: body(short_ref, sg_ref))
+            acc_ref[:, cut] = acc_ref[:, cut] + dot(rows, d_ref[part], TN)
+            sum_scr[:, cut] = sum_scr[:, cut] + jnp.sum(
+                d_ref[part].astype(F32), 0, keepdims=True
+            )
+
+    pl.when(i < n_long)(lambda: body(long_ref))
+    pl.when(i >= n_long)(lambda: body(short_ref))
 
     @pl.when(i == n_rows - 1)
     def _():
-        out_ref[:, : 3 * width] = acc_ref[...].astype(BF16)
-        out_ref[:, 3 * width : 4 * width] = gp_ref[...]
-        out_ref[:, 4 * width :] = jnp.transpose(gv_scr[...]).astype(BF16)
-
-
-def input_back(long_x, short_x, d_h, dq, dk, dv, dense, grad_proj, grad_vec):
+        out_ref[:, :width] = gp_ref[...]
+        out_ref[:, width : 4 * width] = acc_ref[...].astype(BF16)
+        weighted = jnp.zeros((width, 1), F32)
+        bias_grad = jnp.zeros((width, 1), F32)
+        for part in range(3):
+            cut = slice(part * width, (part + 1) * width)
+            weight = w_ref[:, cut].astype(F32)
+            weighted = weighted + jnp.sum(weight * acc_ref[:, cut], 1, keepdims=True)
+            bias_grad = bias_grad + jnp.sum(weight * sum_scr[:, cut], 1, keepdims=True)
+        out_ref[:, 4 * width :] = norm1_grads(weighted, bias_grad, vec_ref, gv_ref)
+
+
+def dense_grads(long_x, short_x, d_qkv, dense, grad_proj, grad_vec):
+    count, width = d_qkv.shape[1:]
+    n_long, n_short = long_x.shape[0] // ROWS, short_x.shape[0] // ROWS
+    n_rows = n_long + n_short
+    return pl.pallas_call(
+        functools.partial(grads_kernel, n_long, n_rows, width),
+        grid=(n_rows,),
+        in_specs=long_short(width, n_long)
+        + [
+            pl.BlockSpec((3, ROWS, width), lambda i: (0, i, 0)),
+            constant((width, 3 * width)),
+            pl.BlockSpec((width, LANES), lambda i: (0, 4 * width // LANES)),
+            constant((width, width)),
+            constant((LANES, width)),
+        ],
+        out_specs=pl.BlockSpec((width, 4 * width + LANES), lambda i: (0, 0)),
+        out_shape=jax.ShapeDtypeStruct((width, 4 * width + LANES), BF16),
+        scratch_shapes=[
+            pltpu.VMEM((width, 3 * width), F32),
+            pltpu.VMEM((8, width), F32),
+            pltpu.VMEM((1, 3 * width), F32),
+        ],
+        compiler_params=params(),
+        cost_estimate=cost(6 * count * width * width, 16 * count * width),
+        name="dense_grads",
+    )(long_x, short_x, d_qkv, dense, dense, grad_proj, grad_vec)
+
+
+class Reducer:
+    def __init__(self, part_ref, out_ref, chunks, scratch):
+        self.part, self.out, self.chunks = part_ref, out_ref, chunks
+        self.got1, self.sum1, self.got2, self.sum2, self.got3 = scratch[:5]
+        self.sems = scratch[5:]
+        self.n_dp, self.n_f = part_ref.shape[:2]
+        self.z = lax.axis_index("dp")
+        self.f = lax.axis_index("fsdp")
+        self.half = self.n_f // 2
+        self.parity = lax.rem(self.f, 2)
+        self.mine = self.f // 2
+        self.partner = self.f + 1 - 2 * self.parity
+        self.order = list(range(1, self.half)) + [0]
+        self.barrier = pltpu.get_barrier_semaphore()
+
+    def greet(self):
+        z, f = self.z, self.f
+        for k in range(1, self.n_dp):
+            pl.semaphore_signal(
+                self.barrier, 1, device_id=(lax.rem(z + k, self.n_dp), f), device_id_type=MESH
+            )
+        for k in range(1, self.half):
+            pl.semaphore_signal(
+                self.barrier, 1, device_id=(z, lax.rem(f + 2 * k, self.n_f)), device_id_type=MESH
+            )
+        pl.semaphore_signal(self.barrier, 1, device_id=(z, self.partner), device_id_type=MESH)
+
+    def meet(self):
+        pl.semaphore_wait(self.barrier, self.n_dp - 1 + self.half)
+
+    def slot(self, k):
+        return lax.rem(self.mine + k, self.half)
+
+    def core_copy(self, c, k):
+        cut, slot = self.chunks[c], self.slot(k)
+        return pltpu.make_async_remote_copy(
+            self.part.at[:, 2 * slot + 1 - self.parity, :, cut], self.got1.at[slot, :, :, cut],
+            self.sems[0].at[c, k], self.sems[1].at[c, k],
+            device_id=(self.z, self.partner), device_id_type=MESH,
+        )
+
+    def chip_copy(self, c, k):
+        cut = self.chunks[c]
+        return pltpu.make_async_remote_copy(
+            self.sum1.at[self.slot(k), :, :, cut], self.got2.at[k, :, :, cut],
+            self.sems[2].at[c, k], self.sems[3].at[c, k],
+            device_id=(self.z, lax.rem(self.f + 2 * k, self.n_f)), device_id_type=MESH,
+        )
+
+    def plane_copy(self, c, k):
+        cut, there = self.chunks[c], lax.rem(self.z + k, self.n_dp)
+        return pltpu.make_async_remote_copy(
+            self.sum2.at[there, :, cut], self.got3.at[k, :, cut],
+            self.sems[4].at[c, k], self.sems[5].at[c, k],
+            device_id=(there, self.f), device_id_type=MESH,
+        )
+
+    def start_core(self, c):
+        for k in self.order:
+            self.core_copy(c, k).start()
+
+    def start_chip(self, c):
+        cut = self.chunks[c]
+        for k in self.order:
+            slot = self.slot(k)
+            self.core_copy(c, k).wait_recv()
+            self.sum1[slot, :, :, cut] = (
+                self.part[:, 2 * slot + self.parity, :, cut].astype(F32)
+                + self.got1[slot, :, :, cut].astype(F32)
+            ).astype(BF16)
+            if k:
+                self.chip_copy(c, k).start()
+
+    def start_plane(self, c):
+        cut = self.chunks[c]
+        total = self.sum1[self.mine, :, :, cut].astype(F32)
+        for k in range(1, self.half):
+            self.chip_copy(c, k).wait_recv()
+            total = total + self.got2[k, :, :, cut].astype(F32)
+        self.sum2[:, :, cut] = total.astype(BF16)
+        for k in range(1, self.n_dp):
+            self.plane_copy(c, k).start()
+
+    def close(self, c):
+        cut = self.chunks[c]
+        total = self.sum2[self.z, :, cut].astype(F32)
+        for k in range(1, self.n_dp):
+            self.plane_copy(c, k).wait_recv()
+            total = total + self.got3[k, :, cut].astype(F32)
+        self.out[:, cut] = total
+
+    def drain(self):
+        for c in range(len(self.chunks)):
+            for k in range(self.half):
+                self.core_copy(c, k).wait_send()
+            for k in range(1, self.half):
+                self.chip_copy(c, k).wait_send()
+            for k in range(1, self.n_dp):
+                self.plane_copy(c, k).wait_send()
+
+
+def reducer_scratch(n_chunks, n_dp, n_f, share, columns):
+    half = n_f // 2
+    return [
+        pltpu.VMEM((half, n_dp, share, columns), BF16),
+        pltpu.VMEM((half, n_dp, share, columns), BF16),
+        pltpu.VMEM((half, n_dp, share, columns), BF16),
+        pltpu.VMEM((n_dp, share, columns), BF16),
+        pltpu.VMEM((n_dp, share, columns), BF16),
+        pltpu.SemaphoreType.DMA((n_chunks, half)),
+        pltpu.SemaphoreType.DMA((n_chunks, half)),
+        pltpu.SemaphoreType.DMA((n_chunks, half)),
+        pltpu.SemaphoreType.DMA((n_chunks, half)),
+        pltpu.SemaphoreType.DMA((n_chunks, n_dp)),
+        pltpu.SemaphoreType.DMA((n_chunks, n_dp)),
+    ]
+
+
+def input_grad(x_ref, dh_ref, d_ref, w_ref, vec_scr, grad_ref):
+    width = dh_ref.shape[1]
+    normed, inv_scale = norm_parts(x_ref)
+    entered = jnp.zeros_like(normed)
+    for part in range(3):
+        entered = entered + dot(d_ref[part], w_ref[:, part * width : (part + 1) * width], NT)
+    grad_ref[...] = dh_ref[...] + norm_back(entered * vec_scr[0:1, :], normed, inv_scale)
+
+
+def norm1_grads(weighted, bias_grad, vec_ref, gv_ref):
+    gain, bias = vec_ref[:, 0:1].astype(F32), vec_ref[:, 1:2].astype(F32)
+    lane = lax.broadcasted_iota(jnp.int32, (1, LANES), 1)
+    found = jnp.transpose(gv_ref[...])
+    found = jnp.where(lane == 0, (weighted - bias * bias_grad) / gain, found)
+    return jnp.where(lane == 1, bias_grad, found).astype(BF16)
+
+
+def last_kernel(
+    n_long, n_rows, part_ref, long_ref, short_ref, dh_ref, d_ref, w_ref, vec_ref,
+    h_ref, col_ref, y_ref, out_ref, lg_ref, sg_ref, lo_ref, so_ref, vec_scr, *scratch,
+):
+    i = pl.program_id(0)
+    reducer = Reducer(part_ref, out_ref, column_chunks(part_ref.shape[3]), scratch)
+
+    @pl.when(i == 0)
+    def _():
+        reducer.greet()
+        vec_scr[...] = vectors(vec_ref)
+        reducer.meet()
+        for c in range(N_CHUNKS):
+            reducer.start_core(c)
+
+    def back(x_ref, grad_ref):
+        input_grad(x_ref[...], dh_ref, d_ref, w_ref, vec_scr, grad_ref)
+
+    pl.when(i < n_long)(lambda: back(long_ref, lg_ref))
+    pl.when((i >= n_long) & (i < n_rows))(lambda: back(short_ref, sg_ref))
+
+    @pl.when(i == 0)
+    def _():
+        for c in range(N_CHUNKS):
+            reducer.start_chip(c)
+
+    def finish(out):
+        out[...] = h_ref[...] + combine_rows(col_ref, y_ref)
+
+    pl.when((i >= n_rows) & (i < n_rows + n_long))(lambda: finish(lo_ref))
+    pl.when((i >= n_rows + n_long) & (i < 2 * n_rows))(lambda: finish(so_ref))
+
+    @pl.when(i == 2 * n_rows - 1)
+    def _():
+        for c in range(N_CHUNKS):
+            reducer.start_plane(c)
+        for c in range(N_CHUNKS):
+            reducer.close(c)
+        reducer.drain()
+
+
+def last_stage(partial, long_x, short_x, d_h, d_qkv, dense, h, slot_col, y_back):
+    n_dp, n_f, share, columns = partial.shape
     count, width = d_h.shape
     n_long, n_short = long_x.shape[0] // ROWS, short_x.shape[0] // ROWS
     n_rows = n_long + n_short
-    row = pl.BlockSpec((ROWS, width), lambda i: (i, 0))
+    slots = y_back.shape[0]
+    row = pl.BlockSpec((ROWS, width), lambda i: (jnp.minimum(i, n_rows - 1), 0))
+    late = lambda i: (jnp.clip(i - n_rows, 0, n_rows - 1), 0)
     return pl.pallas_call(
-        functools.partial(input_back_kernel, n_long, n_rows, width),
-        grid=(n_rows,),
-        in_specs=long_short(width, n_long)
-        + [
+        functools.partial(last_kernel, n_long, n_rows),
+        grid=(2 * n_rows,),
+        in_specs=[
+            constant(partial.shape),
+            pl.BlockSpec((ROWS, width), lambda i: (jnp.minimum(i, n_long - 1), 0)),
+            pl.BlockSpec((ROWS, width), lambda i: (jnp.clip(i - n_long, 0, n_short - 1), 0)),
             row,
-            row,
-            row,
-            row,
+            pl.BlockSpec((3, ROWS, width), lambda i: (0, jnp.minimum(i, n_rows - 1), 0)),
             constant((width, 3 * width)),
             pl.BlockSpec((width, LANES), lambda i: (0, 4 * width // LANES)),
-            constant((width, width)),
-            constant((8, width)),
-        ],
-        out_specs=long_short(width, n_long)
-        + [pl.BlockSpec((width, 4 * width + LANES), lambda i: (0, 0))],
+            pl.BlockSpec((ROWS, width), late),
+            pl.BlockSpec((ROWS, 1), late),
+            constant((slots, width)),
+        ],
+        out_specs=[
+            pl.BlockSpec((share, columns), lambda i: (0, 0)),
+            pl.BlockSpec((ROWS, width), lambda i: (jnp.minimum(i, n_long - 1), 0)),
+            pl.BlockSpec((ROWS, width), lambda i: (jnp.clip(i - n_long, 0, n_short - 1), 0)),
+            pl.BlockSpec((ROWS, width), lambda i: (jnp.clip(i - n_rows, 0, n_long - 1), 0)),
+            pl.BlockSpec(
+                (ROWS, width), lambda i: (jnp.clip(i - n_rows - n_long, 0, n_short - 1), 0)
+            ),
+        ],
         out_shape=[
+            jax.ShapeDtypeStruct((share, columns), F32),
             jax.ShapeDtypeStruct(long_x.shape, F32),
             jax.ShapeDtypeStruct(short_x.shape, F32),
-            jax.ShapeDtypeStruct((width, 4 * width + LANES), BF16),
+            jax.ShapeDtypeStruct(long_x.shape, F32),
+            jax.ShapeDtypeStruct(short_x.shape, F32),
+        ],
+        scratch_shapes=[pltpu.VMEM((8, width), F32)]
+        + reducer_scratch(N_CHUNKS, n_dp, n_f, share, columns),
+        compiler_params=params(collective_id=1, has_side_effects=True),
+        cost_estimate=cost(2 * count * width * (3 * width + slots), 60e6),
+        name="last_stage",
+    )(partial, long_x, short_x, d_h, d_qkv, dense, dense, h, slot_col, y_back)
+
+
+def close_kernel(
+    n_long, n_rows, proj_ref, gv_ref, long_ref, short_ref, dp_ref, dh_ref, d_ref, w_ref, vec_ref,
+    h_ref, col_ref, y_ref, out_ref, lg_ref, sg_ref, lo_ref, so_ref,
+    vec_scr, rows_ref, part_ref, stat_ref, *scratch,
+):
+    i = pl.program_id(0)
+    n_dp, n_f, share, columns = part_ref.shape
+    width = dh_ref.shape[1]
+    chunks = [slice(c * width, (c + 1) * width) for c in range(3)] + [slice(3 * width, columns)]
+    reducer = Reducer(part_ref, out_ref, chunks, scratch)
+    begin_back, begin_out = 3, 3 + n_rows
+
+    def scatter(value, cut):
+        for index in range(n_dp * n_f):
+            part_ref[index // n_f, index % n_f, :, cut] = value[
+                index * share : (index + 1) * share
+            ].astype(BF16)
+
+    @pl.when(i == 0)
+    def _():
+        reducer.greet()
+        vec_scr[...] = vectors(vec_ref)
+        part_ref[:, :, :, :width] = proj_ref[...]
+        reducer.meet()
+        reducer.start_core(0)
+        n = long_ref.shape[0]
+        for ref, first in ((long_ref, 0), (short_ref, n)):
+            for start in range(0, ref.shape[0], ROWS):
+                normed, _ = norm_parts(ref[start : start + ROWS, :])
+                rows_ref[first + start : first + start + ROWS, :] = (
+                    normed * vec_scr[0:1, :] + vec_scr[1:2, :]
+                ).astype(BF16)
+        stat_ref[...] = jnp.zeros_like(stat_ref)
+        reducer.start_chip(0)
+
+    for part in range(3):
+
+        @pl.when(i == part)
+        def _(part=part):
+            value = dot(rows_ref[...], dp_ref[0], TN)
+            scatter(value, slice((part + 1) * width, (part + 2) * width))
+            weight = w_ref[:, part * width : (part + 1) * width].astype(F32)
+            sums = jnp.sum(dp_ref[0].astype(F32), 0, keepdims=True)
+            stat_ref[:, 0:1] = stat_ref[:, 0:1] + jnp.sum(weight * value, 1, keepdims=True)
+            stat_ref[:, 1:2] = stat_ref[:, 1:2] + jnp.sum(weight * sums, 1, keepdims=True)
+            if part == 2:
+                found = norm1_grads(stat_ref[:, 0:1], stat_ref[:, 1:2], vec_ref, gv_ref)
+                scatter(found.astype(F32), slice(4 * width, columns))
+            reducer.start_core(part + 1)
+            if part:
+                reducer.start_chip(part)
+
+    @pl.when(i == begin_back)
+    def _():
+        reducer.start_chip(3)
+
+    def back(x_ref, index, grad_ref):
+        rows = pl.ds(pl.multiple_of(index * ROWS, ROWS), ROWS)
+        input_grad(x_ref[rows, :], dh_ref, d_ref, w_ref, vec_scr, grad_ref)
+
+    j = i - begin_back
+    pl.when((j >= 0) & (j < n_long))(lambda: back(long_ref, j, lg_ref))
+    pl.when((j >= n_long) & (j < n_rows))(lambda: back(short_ref, j - n_long, sg_ref))
+
+    def finish(out):
+        out[...] = h_ref[...] + combine_rows(col_ref, y_ref)
+
+    m = i - begin_out
+    pl.when((m >= 0) & (m < n_long))(lambda: finish(lo_ref))
+    pl.when((m >= n_long) & (m < n_rows))(lambda: finish(so_ref))
+
+    @pl.when(i == begin_out - 1)
+    def _():
+        reducer.start_plane(0)
+
+    @pl.when(i == begin_out)
+    def _():
+        reducer.start_plane(1)
+
+    @pl.when(i == begin_out + n_rows - 1)
+    def _():
+        reducer.start_plane(2)
+        reducer.start_plane(3)
+        for c in range(4):
+            reducer.close(c)
+        reducer.drain()
+
+
+def close_stage(grad_proj, grad_vec, long_x, short_x, d_h, d_qkv, dense, h, slot_col, y_back):
+    n_dp, n_f, share = grad_proj.shape[:3]
+    count, width = d_h.shape
+    columns = 4 * width + LANES
+    n_long, n_short = long_x.shape[0] // ROWS, short_x.shape[0] // ROWS
+    n_rows = n_long + n_short
+    slots = y_back.shape[0]
+    step = lambda i, base, last: jnp.clip(i - base, 0, last)
+    return pl.pallas_call(
+        functools.partial(close_kernel, n_long, n_rows),
+        grid=(3 + 2 * n_rows,),
+        in_specs=[
+            constant(grad_proj.shape),
+            constant(grad_vec.shape),
+            constant(long_x.shape),
+            constant(short_x.shape),
+            pl.BlockSpec((1, count, width), lambda i: (jnp.minimum(i, 2), 0, 0)),
+            pl.BlockSpec((ROWS, width), lambda i: (step(i, 3, n_rows - 1), 0)),
+            pl.BlockSpec((3, ROWS, width), lambda i: (0, step(i, 3, n_rows - 1), 0)),
+            constant((width, 3 * width)),
+            pl.BlockSpec((width, LANES), lambda i: (0, 4 * width // LANES)),
+            pl.BlockSpec((ROWS, width), lambda i: (step(i, 3 + n_rows, n_rows - 1), 0)),
+            pl.BlockSpec((ROWS, 1), lambda i: (step(i, 3 + n_rows, n_rows - 1), 0)),
+            constant((slots, width)),
+        ],
+        out_specs=[
+            pl.BlockSpec((share, columns), lambda i: (0, 0)),
+            pl.BlockSpec((ROWS, width), lambda i: (step(i, 3, n_long - 1), 0)),
+            pl.BlockSpec((ROWS, width), lambda i: (step(i, 3 + n_long, n_short - 1), 0)),
+            pl.BlockSpec((ROWS, width), lambda i: (step(i, 3 + n_rows, n_long - 1), 0)),
+            pl.BlockSpec((ROWS, width), lambda i: (step(i, 3 + n_rows + n_long, n_short - 1), 0)),
+        ],
+        out_shape=[
+            jax.ShapeDtypeStruct((share, columns), F32),
+            jax.ShapeDtypeStruct(long_x.shape, F32),
+            jax.ShapeDtypeStruct(short_x.shape, F32),
+            jax.ShapeDtypeStruct(long_x.shape, F32),
+            jax.ShapeDtypeStruct(short_x.shape, F32),
         ],
         scratch_shapes=[
-            pltpu.VMEM((width, 3 * width), F32),
             pltpu.VMEM((8, width), F32),
-            pltpu.VMEM((LANES, width), F32),
-        ],
-        compiler_params=params(),
-        cost_estimate=cost(12 * count * width * width, 20 * count * width),
-        name="input_back",
-    )(long_x, short_x, d_h, dq, dk, dv, dense, dense, grad_proj, grad_vec)
+            pltpu.VMEM((count, width), BF16),
+            pltpu.VMEM((n_dp, n_f, share, columns), BF16),
+            pltpu.VMEM((width, LANES), F32),
+        ]
+        + reducer_scratch(4, n_dp, n_f, share, columns),
+        compiler_params=params(collective_id=4, has_side_effects=True),
+        cost_estimate=cost(2 * count * width * (6 * width + slots), 60e6),
+        name="close_stage",
+    )(grad_proj, grad_vec, long_x, short_x, d_qkv, d_h, d_qkv, dense, dense, h, slot_col, y_back)
 
 
 def on_device(
@@ -964,15 +1311,28 @@
         xl, xs, o, dense, slot_row, g_there, up, n_f, cap
     )
     grad_down = lax.psum_scatter(grad_down, "dp", scatter_dimension=0, tiled=True).astype(F32)
-    y, db_back, grad_up = back_experts(b_there, g_there, act, slope, up, down, n_f, cap)
+    y0, db0, gu0 = own_experts(
+        lax.axis_index("dp").reshape(1), b_there, g_there, act, slope, up, w_down[0], n_f, cap
+    )
+    y, db_back, grad_up = back_experts(
+        b_there, g_there, act, slope, up, down, y0, db0, gu0, n_dp, n_f, cap
+    )
     db_back = db_back.reshape(slots, width)
     grad_up = lax.psum_scatter(grad_up, "dp", scatter_dimension=1, tiled=True).astype(F32)
     y_back = exchange(y)
     d_h, d_o, grad_proj, grad_vec = hidden_back(h, slot_col, db_back, gl, gs, o, dense)
-    long_out, short_out = finish(h, slot_col, y_back, n_long, n_short)
-    dq, dk, dv = attend_back(qkv, o, d_o, lse, long_len, short_len, seqs)
-    long_grad, short_grad, grads = input_back(xl, xs, d_h, dq, dk, dv, dense, grad_proj, grad_vec)
-    owned = scatter_dense(grads.reshape(n_dp, n_f, share, own.shape[1]), n_dp, n_f)
+    d_qkv = attend_back(qkv, o, d_o, lse, long_len, short_len, seqs)
+    if share % 8 == 0:
+        owned, long_grad, short_grad, long_out, short_out = close_stage(
+            grad_proj.reshape(n_dp, n_f, share, width), grad_vec,
+            xl, xs, d_h, d_qkv, dense, h, slot_col, y_back,
+        )
+    else:
+        partial = dense_grads(xl, xs, d_qkv, dense, grad_proj, grad_vec)
+        owned, long_grad, short_grad, long_out, short_out = last_stage(
+            partial.reshape(n_dp, n_f, share, own.shape[1]),
+            xl, xs, d_h, d_qkv, dense, h, slot_col, y_back,
+        )
     return (
         long_out.reshape(long_x.shape),
         short_out.reshape(short_x.shape),
@@ -980,8 +1340,8 @@
         short_grad.reshape(short_x.shape),
         owned[:, 4 * width],
         owned[:, 4 * width + 1],
-        owned[:, : 3 * width],
-        owned[:, 3 * width : 4 * width].T,
+        owned[:, width : 4 * width],
+        owned[:, :width].T,
         owned[:, 4 * width + 2],
         owned[:, 4 * width + 3],
         grad_up[None],

time: 450 us -> 416 us (0.924)
  Pallas kernels: 400 us -> 349 us
  local copies, waits for them, and re-layouts: 9.99 us -> 17.1 us
  starting transfers between devices: 10.8 us -> 16 us
  waiting for transfers between devices: 1.46 us -> 6.17 us
    pallas_call x1, Pallas kernels: 67.6 us -> 49.6 us  [gather_dense(): pl.pallas_call(functools.partial(gather_kernel, n_dp, n_f, cap), out_shap...]
    pallas_call x1, Pallas kernels: 52.2 us -> 35.1 us  [attend_back(): pl.pallas_call(functools.partial(attend_back_kernel, seqs), grid=(pairs,)...]
    pallas_call x1, Pallas kernels: 82.1 us -> 71.8 us  [forward_experts(): pl.pallas_call(functools.partial(forward_kernel, n_f, n_long, n_rows), gr...]
    unnamed x9 -> x21, local copies, waits for them, and re-layouts: 5.14 us -> 12.2 us
    pallas_call x1, Pallas kernels: 27.8 us -> 21.9 us  [attend(): pl.pallas_call(functools.partial(attend_kernel, seqs), grid=(pairs,), in_...]
    all_to_all x2, starting transfers between devices: 10.7 us -> 15.7 us  [exchange(): lax.all_to_all(rows.reshape(n_f, cap, width), 'fsdp', split_axis=0, conca...]
    pallas_call x4 -> x3, Pallas kernels: 140 us -> 140 us  [the longest x1 69.9 us: close_stage(): pl.pallas_call(functools.partial(close_kernel, n_long, n_rows), grid=(3 +...]
  transfers between devices with their start and end apart: 6 -> 6, of which waited for: 0 -> 2; matrix products, arithmetic and copies ran while one was open for 2% -> 3% of each run, Pallas kernels for 90% -> 85%
where the time goes in v3:
time: 416 us; the launch traced here: 411 us
  Pallas kernels  349 us (84%)
  local copies, waits for them, and re-layouts  17.1 us (4%)
  starting transfers between devices  16 us (4%)
  between operations  15.4 us (4%)
  other arithmetic  7.23 us (2%)
  waiting for transfers between devices  6.17 us (1%)
    pallas_call x1, Pallas kernels, forward_experts(): pl.pallas_call(functools.partial(forward_kernel, n_f, n_long, n_rows), gr...  71.8 us
    pallas_call x1, Pallas kernels, close_stage(): pl.pallas_call(functools.partial(close_kernel, n_long, n_rows), grid=(3 +...  69.9 us
    pallas_call x1, Pallas kernels, back_experts(): pl.pallas_call(functools.partial(back_kernel, n_dp, n_f), grid=(n_f + n_d...  50.4 us
    pallas_call x1, Pallas kernels, gather_dense(): pl.pallas_call(functools.partial(gather_kernel, n_dp, n_f, cap), out_shap...  49.6 us
    pallas_call x1, Pallas kernels, attend_back(): pl.pallas_call(functools.partial(attend_back_kernel, seqs), grid=(pairs,)...  35.1 us
    pallas_call x1, Pallas kernels, attend(): pl.pallas_call(functools.partial(attend_kernel, seqs), grid=(pairs,), in_...  21.9 us
    pallas_call x1, Pallas kernels, hidden_back(): pl.pallas_call(functools.partial(hidden_back_kernel, n_long, n_rows), gri...  19.5 us
    pallas_call x1, Pallas kernels, own_experts(): pl.pallas_call(functools.partial(own_kernel, n_f), grid_spec=pltpu.Prefet...  19.3 us
  transfers between devices with their start and end apart: 6, of which 2 were waited for; matrix products, arithmetic and copies ran while one was open for 3% of the time, Pallas kernels for 85%

profile of v3, /device:TPU:12, one launch (start us, length us, event | category | flops | bytes accessed | tf_op | source)
XLA Modules:
  0.0 410.8 jit_solution(1701869223105204926)
XLA Ops:
  7.2 0.7 all-gather.3.cloned.1.call-update
  8.0 0.7 all-gather.5.cloned.1.call-update
  8.7 0.7 pad_maximum_fusion
  9.5 1.9 copy.38.ids_ref
  11.4 0.7 fusion.1.own_ref
  12.1 49.6 %gather_dense.1 = (bf16[4,8,24,3200]{3,2,1,0:T(8,128)(2,1)}, s32[1536,1]{1,0:T(8,128)}, s32[8,1536]{1,0:T(8,128)}, bf16[2048,768]{1,0:T(8,128)(2,1)}) custom-call(bf16[24,3200]{1,0:T(8,128)(2,1)} %fusion.1.own_ref, s32[1536,1]{1,0:T(8,128)} %copy.38.ids_ref, f32[1024,768]{1,0:T(8,128)} %bitcast.47, f32[512,768]{1,0:T(8,128)} %bitcast.58), custom_call_target="tpu_custom_call" | custom-call | bytes 100000000 | tf_op jit(solution)/shard_map/gather_dense/pallas_call | solution.py:158
  61.7 5.6 %all-to-all-start = ((bf16[8,256,768]{2,1,0:T(8,128)(2,1)}), bf16[8,256,768]{2,1,0:T(8,128)(2,1)S(1)}, u32[]{:S(2)}, u32[]{:S(2)}) async-start(bf16[8,256,768]{2,1,0:T(8,128)(2,1)} %bitcast.52), calls=%async_computation | async-start | bytes 6291456 | tf_op jit(solution)/shard_map/all_to_all | solution.py:1302
  67.2 0.2 reduce-scatter.5.cloned.1.call-start
  68.7 11.6 %make_qkv.1.q_ref.k_ref.v_ref = bf16[1536,2304]{1,0:T(8,128)(2,1)} custom-call(f32[1024,768]{1,0:T(8,128)} %bitcast.53, f32[512,768]{1,0:T(8,128)} %bitcast.60, bf16[768,3200]{1,0:T(8,128)(2,1)} %bitcast.32, bf16[768,3200]{1,0:T(8,128)(2,1)} %bitcast.33), custom_call_target="tpu_custom_call" | custom-call | flops 5435817984 | bytes 15335424 | tf_op jit(solution)/shard_map/make_qkv/pallas_call | solution.py:254
  80.3 21.9 %attend.1 = (bf16[1536,768]{1,0:T(8,128)(2,1)}, f32[128,1536]{1,0:T(8,128)}) custom-call(s32[1]{0:T(128)S(6)} %copy.43.long_len, s32[1]{0:T(128)S(6)} %copy.44.short_len, bf16[1536,2304]{1,0:T(8,128)(2,1)} %make_qkv.1.q_ref.k_ref.v_ref, bf16[1536,2304]{1,0:T(8,128)(2,1)} %make_qkv.1.q_ref.k_ref.v_ref, bf16[1536,2304]{1,0:T(8,128)(2,1)} %make_qkv.1.q_ref.k_ref.v_ref), custom_call_target="tpu_custom_call" | custom-call | flops 16000000000 | bytes 9437184 | tf_op jit(solution)/shard_map/attend/pallas_call | solution.py:347
  102.2 2.0 all-to-all-done
  104.2 2.7 all-gather.3.cloned.1.call-done
  106.9 71.8 %forward_experts.1 = (f32[1536,768]{1,0:T(8,128)}, bf16[2048,768]{1,0:T(8,128)(2,1)}, bf16[2048,3072]{1,0:T(8,128)(2,1)}, bf16[2048,3072]{1,0:T(8,128)(2,1)}, bf16[3072,768]{1,0:T(8,128)(2,1)}) custom-call(f32[1024,768]{1,0:T(8,128)} %bitcast.54, f32[512,768]{1,0:T(8,128)} %bitcast.61, bf16[1536,768]{1,0:T(8,128)(2,1)} %get-tuple-element.39.o_ref, ...), custom_call_target="tpu_custom_call" | custom-call | flops 24159191040 | bytes 60000000 | tf_op jit(solution)/shard_map/forward_experts/pallas_call | solution.py:556
  178.8 19.3 %own_experts.1 = (f32[2048,768]{1,0:T(8,128)}, f32[2048,768]{1,0:T(8,128)}, bf16[768,768]{1,0:T(8,128)(2,1)}) custom-call(s32[1]{0:T(128)} %bitcast.14.z_ref, bf16[2048,768]{1,0:T(8,128)(2,1)} %get-tuple-element.44.b_ref, bf16[2048,768]{1,0:T(8,128)(2,1)} %bitcast.41, bf16[2048,3072]{1,0:T(8,128)(2,1)} %get-tuple-element.45.act_ref, ...), custom_call_target="tpu_custom_call" | custom-call | flops 9663676416 | bytes 30000000 | tf_op jit(solution)/shard_map/own_experts/pallas_call | solution.py:626
  198.1 50.4 %back_experts.1 = (bf16[2048,768]{1,0:T(8,128)(2,1)}, bf16[8,256,768]{2,1,0:T(8,128)(2,1)}, bf16[768,3072]{1,0:T(8,128)(2,1)}) custom-call(bf16[2048,768]{1,0:T(8,128)(2,1)} %get-tuple-element.44.b_ref, bf16[2048,768]{1,0:T(8,128)(2,1)} %bitcast.42, bf16[2048,3072]{1,0:T(8,128)(2,1)} %get-tuple-element.45.act_ref, ...), custom_call_target="tpu_custom_call" | custom-call | flops 28991029248 | bytes 60000000 | tf_op jit(solution)/shard_map/back_experts/pallas_call | solution.py:736
  248.6 10.1 %all-to-all-start.1 = ((bf16[8,256,768]{2,1,0:T(8,128)(2,1)}), bf16[8,256,768]{2,1,0:T(8,128)(2,1)S(1)}, u32[]{:S(2)}, u32[]{:S(2)}) async-start(bf16[8,256,768]{2,1,0:T(8,128)(2,1)} %bitcast.18), calls=%async_computation.1 | async-start | bytes 6291456 | tf_op jit(solution)/shard_map/all_to_all | solution.py:1302
  258.7 19.5 %hidden_back.1 = (f32[1536,768]{1,0:T(8,128)}, bf16[1536,768]{1,0:T(8,128)(2,1)}, bf16[768,768]{1,0:T(8,128)(2,1)}, f32[128,768]{1,0:T(8,128)}) custom-call(f32[1536,768]{1,0:T(8,128)} %get-tuple-element.42.h_ref, s32[1536,1]{1,0:T(8,128)} %get-tuple-element.43.col_ref, bf16[2048,768]{1,0:T(8,128)(2,1)} %bitcast.69, f32[1024,768]{1,0:T(8,128)} %bitcast.48, ...), custom_call_target="tpu_custom_call" | custom-call | flops 8455716864 | bytes 18874368 | tf_op jit(solution)/shard_map/hidden_back/pallas_call | solution.py:816
  278.2 35.1 %attend_back.1.dp_ref.d_ref = bf16[3,1536,768]{2,1,0:T(8,128)(2,1)} custom-call(s32[1]{0:T(128)S(6)} %copy.43.long_len, s32[1]{0:T(128)S(6)} %copy.44.short_len, bf16[1536,2304]{1,0:T(8,128)(2,1)} %make_qkv.1.q_ref.k_ref.v_ref, bf16[1536,2304]{1,0:T(8,128)(2,1)} %make_qkv.1.q_ref.k_ref.v_ref, bf16[1536,2304]{1,0:T(8,128)(2,1)} %make_qkv.1.q_ref.k_ref.v_ref, ...), custom_call_target="tpu_custom_call" | custom-call | flops 40000000000 | bytes 18874368 | tf_op jit(solution)/shard_map/attend_back/pallas_call | solution.py:433
  313.3 1.7 copy-done.1
  314.9 69.9 %close_stage.1 = (f32[24,3200]{1,0:T(8,128)}, f32[1024,768]{1,0:T(8,128)}, f32[512,768]{1,0:T(8,128)}, f32[1024,768]{1,0:T(8,128)}, f32[512,768]{1,0:T(8,128)}) custom-call(bf16[4,8,24,768]{3,2,1,0:T(8,128)(2,1)} %bitcast.70, f32[128,768]{1,0:T(8,128)} %get-tuple-element.52.gv_ref, f32[1024,768]{1,0:T(8,128)} %bitcast.55, f32[512,768]{1,0:T(8,128)} %bitcast.62, ...), custom_call_target="tpu_custom_call" | custom-call | flops 15703474176 | bytes 60000000 | tf_op jit(solution)/shard_map/close_stage/pallas_call | solution.py:1231
  384.8 1.6 slice.20
  386.4 1.6 slice_reduce_fusion
  388.0 1.5 slice_bitcast_fusion
  389.6 3.0 bitcast_convert_fusion
  392.6 2.8 bitcast_convert_fusion.1
  395.4 1.7 copy.45
  397.1 0.9 copy-done.5
  397.9 1.1 copy.46
  399.1 1.3 copy-done.2
  400.4 1.7 copy.47
  402.1 0.9 copy-done.4
  402.9 1.1 copy.48
  (22 shorter events, 0.3 us)
Async XLA Ops:
  7.2 4.2 %copy-start.7 = (bf16[768,24]{0,1:T(8,128)(2,1)S(1)}, bf16[768,24]{0,1:T(8,128)(2,1)}, u32[]{:S(2)}) copy-start(bf16[768,24]{0,1:T(8,128)(2,1)} %param.23) | copy-start | bytes 110596
  7.2 4.2 %copy-start.6 = (bf16[24,2304]{1,0:T(8,128)(2,1)S(1)}, bf16[24,2304]{1,0:T(8,128)(2,1)}, u32[]{:S(2)}) copy-start(bf16[24,2304]{1,0:T(8,128)(2,1)} %param.22) | copy-start | bytes 331780
  7.2 99.7 %all-gather.3.cloned.1.call-start = ((), (), s32[]{:S(2)}) async-start(), calls=%async_computation.4 | async-start | bytes 5898240 | tf_op jit(solution)/shard_map/all_gather | solution.py:1289
  7.9 190.2 %all-gather.5.cloned.1.call-start = ((), (), s32[]{:S(2)}) async-start(), calls=%async_computation.5 | async-start | bytes 5898240 | tf_op jit(solution)/shard_map/all_gather | solution.py:1290
  61.7 42.5 %all-to-all-start = ((bf16[8,256,768]{2,1,0:T(8,128)(2,1)}), bf16[8,256,768]{2,1,0:T(8,128)(2,1)S(1)}, u32[]{:S(2)}, u32[]{:S(2)}) async-start(bf16[8,256,768]{2,1,0:T(8,128)(2,1)} %bitcast.52), calls=%async_computation | async-start | bytes 6291456 | tf_op jit(solution)/shard_map/all_to_all | solution.py:1302
  67.2 322.3 %reduce-scatter.5.cloned.1.call-start = ((), (), s32[]{:S(2)}) async-start(), calls=%async_computation.7 | async-start | bytes 5898240 | tf_op jit(solution)/shard_map/reduce_scatter | solution.py:1313
  104.2 2.8 copy-start
  178.7 213.8 %reduce-scatter.3.cloned.1.call-start = ((), (), s32[]{:S(2)}) async-start(), calls=%async_computation.6 | async-start | bytes 5898240 | tf_op jit(solution)/shard_map/reduce_scatter | solution.py:1321
  248.6 64.7 %all-to-all-start.1 = ((bf16[8,256,768]{2,1,0:T(8,128)(2,1)}), bf16[8,256,768]{2,1,0:T(8,128)(2,1)S(1)}, u32[]{:S(2)}, u32[]{:S(2)}) async-start(bf16[8,256,768]{2,1,0:T(8,128)(2,1)} %bitcast.18), calls=%async_computation.1 | async-start | bytes 6291456 | tf_op jit(solution)/shard_map/all_to_all | solution.py:1302
  313.3 1.7 copy-start.1
  389.5 5.9 %copy-start.3 = (f32[1024,768]{1,0:T(8,128)S(1)}, f32[1024,768]{1,0:T(8,128)}, u32[]{:S(2)}) copy-start(f32[1024,768]{1,0:T(8,128)} %get-tuple-element.57) | copy-start | bytes 9437188
  395.4 2.5 copy-start.5
  397.9 2.5 copy-start.2
  400.4 2.5 copy-start.4
Sparse Core Ops, SparseCore 0:
  9.6 97.2 all-gather.2
  108.5 88.9 all-gather.4
  199.8 86.2 reduce-scatter.4
  288.2 98.9 reduce-scatter.2

commit v4 on v3

--- a/solution.py
+++ b/solution.py
@@ -207,16 +207,15 @@
 
 def peers(n_f):
     f = lax.axis_index("fsdp")
-    half = n_f // 2
-    chip, core = f // 2, lax.rem(f, 2)
-
-    def to(k):
-        return lax.rem(chip + k // 2, half) * 2 + lax.rem(core + lax.rem(k, 2), 2)
-
-    def source(k):
-        return lax.rem(chip + half - k // 2, half) * 2 + lax.rem(core + lax.rem(k, 2), 2)
-
-    return f, to, source
+
+    def partner(k):
+        place, digit = 0, 1
+        while digit < n_f:
+            place = place + digit * lax.rem(f // digit + k // digit, 2)
+            digit *= 2
+        return place
+
+    return f, partner
 
 
 def greet(n_f, to):
@@ -224,6 +223,31 @@
     barrier = pltpu.get_barrier_semaphore()
     for k in range(1, n_f):
         pl.semaphore_signal(barrier, 1, device_id=(z, to(k)), device_id_type=MESH)
+
+
+class Homeward:
+    def __init__(self, n_f, ks, y_ref, yb_ref, send, recv):
+        self.f, self.to = peers(n_f)
+        self.n_f, self.ks = n_f, ks
+        self.z = lax.axis_index("dp")
+        self.y, self.yb, self.send, self.recv = y_ref, yb_ref, send, recv
+
+    def transfer(self, k):
+        return pltpu.make_async_remote_copy(
+            self.y.at[self.to(k)], self.yb.at[self.f], self.send.at[k], self.recv.at[k],
+            device_id=(self.z, self.to(k)), device_id_type=MESH,
+        )
+
+    def begin(self):
+        greet(self.n_f, self.to)
+        pl.semaphore_wait(pltpu.get_barrier_semaphore(), self.n_f - 1)
+        for k in self.ks:
+            self.transfer(k).start()
+
+    def end(self):
+        for k in self.ks:
+            self.transfer(k).wait_recv()
+            self.transfer(k).wait_send()
 
 
 def qkv_kernel(n_long, width, long_ref, short_ref, w_ref, vec_ref, qkv_ref, vec_scr):
@@ -368,15 +392,20 @@
 
 
 def attend_back_kernel(
-    seqs, long_len, short_len, q_ref, k_ref, v_ref, o_ref, do_ref, lse_ref,
-    d_ref, dkt_ref, dvt_ref, lse_scr,
+    seqs, n_f, long_len, short_len, q_ref, k_ref, v_ref, o_ref, do_ref, lse_ref, y_ref, _,
+    d_ref, yb_ref, dkt_ref, dvt_ref, lse_scr, send, recv, l_sem,
 ):
     pair = pl.program_id(0)
     masks = head_masks()
     lane = lax.broadcasted_iota(jnp.int32, (1, LANES), 1)
 
+    home = Homeward(n_f, range(3 * n_f // 4, n_f), y_ref, yb_ref, send, recv)
+    keep = pltpu.make_async_copy(y_ref.at[home.f], yb_ref.at[home.f], l_sem)
+
     @pl.when(pair == 0)
     def _():
+        home.begin()
+        keep.start()
         lse_scr[...] = jnp.transpose(lse_ref[...])
 
     causal = lax.broadcasted_iota(jnp.int32, (ATTEND_BACK, ATTEND_BACK), 1) <= (
@@ -424,14 +453,20 @@
         d_ref[1, rows, :] = jnp.transpose(dkt_ref[:, :length]).astype(BF16)
         d_ref[2, rows, :] = jnp.transpose(dvt_ref[:, :length]).astype(BF16)
 
-
-def attend_back(qkv, o, d_o, lse, long_len, short_len, seqs):
+    @pl.when(pair == pl.num_programs(0) - 1)
+    def _():
+        keep.wait()
+        home.end()
+
+
+def attend_back(qkv, o, d_o, lse, long_len, short_len, seqs, y, y_back):
     count, width = o.shape
+    n_f = y.shape[0]
     pairs = width // LANES
     longest = max(length for _, length, _, _ in seqs)
     one = pl.BlockSpec((count, LANES), lambda i: (0, i))
     return pl.pallas_call(
-        functools.partial(attend_back_kernel, seqs),
+        functools.partial(attend_back_kernel, seqs, n_f),
         grid=(pairs,),
         in_specs=[pl.BlockSpec(memory_space=pltpu.SMEM)] * 2
         + [
@@ -441,18 +476,30 @@
             one,
             one,
             constant((LANES, count)),
-        ],
-        out_specs=pl.BlockSpec((3, count, LANES), lambda i: (0, 0, i)),
-        out_shape=jax.ShapeDtypeStruct((3, count, width), BF16),
+            pl.BlockSpec(memory_space=pl.ANY),
+            pl.BlockSpec(memory_space=pl.ANY),
+        ],
+        out_specs=[
+            pl.BlockSpec((3, count, LANES), lambda i: (0, 0, i)),
+            pl.BlockSpec(memory_space=pl.ANY),
+        ],
+        input_output_aliases={9: 1},
+        out_shape=[
+            jax.ShapeDtypeStruct((3, count, width), BF16),
+            jax.ShapeDtypeStruct(y.shape, BF16),
+        ],
         scratch_shapes=[
             pltpu.VMEM((LANES, longest), F32),
             pltpu.VMEM((LANES, longest), F32),
             pltpu.VMEM((count, LANES), F32),
-        ],
-        compiler_params=params(),
+            pltpu.SemaphoreType.DMA((n_f,)),
+            pltpu.SemaphoreType.DMA((n_f,)),
+            pltpu.SemaphoreType.DMA,
+        ],
+        compiler_params=params(collective_id=5, has_side_effects=True),
         cost_estimate=cost(40e9, 16 * count * width, 10e6),
         name="attend_back",
-    )(long_len, short_len, qkv, qkv, qkv, o, d_o, lse)
+    )(long_len, short_len, qkv, qkv, qkv, o, d_o, lse, y, y_back)
 
 
 def gelu_parts(pre):
@@ -471,7 +518,7 @@
 ):
     i = pl.program_id(0)
     z = lax.axis_index("dp")
-    f, to, source = peers(n_f)
+    f, partner = peers(n_f)
     cap, width = out_buf.shape[1:]
     n_up = n_rows + n_f
     n_down = n_up + n_f
@@ -480,12 +527,12 @@
     def transfer(k):
         return pltpu.make_async_remote_copy(
             out_buf.at[k], in_buf.at[f], send.at[k], recv.at[k],
-            device_id=(z, to(k)), device_id_type=MESH,
+            device_id=(z, partner(k)), device_id_type=MESH,
         )
 
     @pl.when(i == 0)
     def _():
-        greet(n_f, to)
+        greet(n_f, partner)
         vec_scr[...] = vectors(vec_ref)
 
     def body(x_ref):
@@ -506,7 +553,7 @@
     @pl.when((i >= n_rows) & (i < n_up - 1))
     def _():
         k = i - n_rows + 1
-        out_buf[k] = dispatch_block(row_ref, rows_ref[...], to(k) * cap, cap)
+        out_buf[k] = dispatch_block(row_ref, rows_ref[...], partner(k) * cap, cap)
         transfer(k).start()
 
     @pl.when(i == n_up - 1)
@@ -519,7 +566,7 @@
 
     @pl.when((i >= n_up) & (i < n_down))
     def _():
-        origin = source(i - n_up)
+        origin = partner(i - n_up)
         rows = in_buf[origin]
         here = pl.ds(pl.multiple_of(origin * cap, cap), cap)
         for first in range(0, up_ref.shape[1], width):
@@ -601,12 +648,12 @@
     n_f, z_ref, b_ref, g_ref, act_ref, slope_ref, up_ref, down_ref, y_ref, db_ref, gu_ref, all_ref
 ):
     i = pl.program_id(0)
-    _, _, source = peers(n_f)
+    _, partner = peers(n_f)
     cap = y_ref.shape[0]
 
     @pl.when(i < n_f)
     def _():
-        here = pl.ds(pl.multiple_of(source(i) * cap, cap), cap)
+        here = pl.ds(pl.multiple_of(partner(i) * cap, cap), cap)
         d_act = dot(g_ref[here, :], down_ref[...], NT)
         d_pre = (d_act * slope_ref[...].astype(F32)).astype(BF16)
         all_ref[here, :] = d_pre
@@ -656,7 +703,7 @@
 ):
     i = pl.program_id(0)
     z = lax.axis_index("dp")
-    f, to, source = peers(n_f)
+    f, partner = peers(n_f)
     cap, width = out_buf.shape[1:]
     piece = gu_ref.shape[1]
     barrier = pltpu.get_barrier_semaphore()
@@ -664,7 +711,7 @@
     def transfer(k):
         return pltpu.make_async_remote_copy(
             out_buf.at[k], db_ref.at[f], send.at[k], recv.at[k],
-            device_id=(z, source(k)), device_id_type=MESH,
+            device_id=(z, partner(k)), device_id_type=MESH,
         )
 
     def other(m):
@@ -674,12 +721,12 @@
 
     @pl.when(i == 0)
     def _():
-        greet(n_f, to)
+        greet(n_f, partner)
 
     @pl.when(i < n_f)
     def _():
         k = n_f - 1 - i
-        here = pl.ds(pl.multiple_of(source(k) * cap, cap), cap)
+        here = pl.ds(pl.multiple_of(partner(k) * cap, cap), cap)
         g = g_ref[here, :]
         d_b = db0_ref[...]
         for m in range(1, n_dp):
@@ -703,7 +750,7 @@
 
     @pl.when(i < n_f)
     def _():
-        here = pl.ds(pl.multiple_of(source(n_f - 1 - i) * cap, cap), cap)
+        here = pl.ds(pl.multiple_of(partner(n_f - 1 - i) * cap, cap), cap)
         y = y0_ref[...]
         for m in range(1, n_dp):
             y = y + dot(act_ref[:, other(m)], down_ref[other(m), :])
@@ -777,10 +824,12 @@
 
 
 def hidden_back_kernel(
-    n_long, n_rows, h_ref, col_ref, db_ref, long_ref, short_ref, o_ref, w_ref, vec_ref,
-    dh_ref, do_ref, gp_ref, gv_ref, acc_ref, vec_scr,
+    n_f, n_long, n_rows, h_ref, col_ref, db_ref, long_ref, short_ref, o_ref, w_ref, vec_ref, y_ref,
+    dh_ref, do_ref, gp_ref, gv_ref, yb_ref, acc_ref, vec_scr, send, recv,
 ):
     i = pl.program_id(0)
+    home = Homeward(n_f, range(1, 3 * n_f // 4), y_ref, yb_ref, send, recv)
+    pl.when(i == 0)(home.begin)
 
     @pl.when(i == 0)
     def _():
@@ -805,16 +854,18 @@
     @pl.when(i == n_rows - 1)
     def _():
         gp_ref[...] = acc_ref[...].astype(BF16)
-
-
-def hidden_back(h, slot_col, db_back, long_cot, short_cot, o, dense):
+        home.end()
+
+
+def hidden_back(h, slot_col, db_back, long_cot, short_cot, o, dense, y):
+    n_f = y.shape[0]
     count, width = h.shape
     slots = db_back.shape[0]
     n_long, n_short = long_cot.shape[0] // ROWS, short_cot.shape[0] // ROWS
     n_rows = n_long + n_short
     row = pl.BlockSpec((ROWS, width), lambda i: (i, 0))
     return pl.pallas_call(
-        functools.partial(hidden_back_kernel, n_long, n_rows),
+        functools.partial(hidden_back_kernel, n_f, n_long, n_rows),
         grid=(n_rows,),
         in_specs=[row, pl.BlockSpec((ROWS, 1), lambda i: (i, 0)), constant((slots, width))]
         + long_short(width, n_long)
@@ -822,24 +873,32 @@
             row,
             pl.BlockSpec((width, width), lambda i: (0, 3)),
             pl.BlockSpec((width, LANES), lambda i: (0, 4 * width // LANES)),
+            pl.BlockSpec(memory_space=pl.ANY),
         ],
         out_specs=[
             row,
             row,
             pl.BlockSpec((width, width), lambda i: (0, 0)),
             pl.BlockSpec((LANES, width), lambda i: (0, 0)),
+            pl.BlockSpec(memory_space=pl.ANY),
         ],
         out_shape=[
             jax.ShapeDtypeStruct((count, width), F32),
             jax.ShapeDtypeStruct((count, width), BF16),
             jax.ShapeDtypeStruct((width, width), BF16),
             jax.ShapeDtypeStruct((LANES, width), F32),
-        ],
-        scratch_shapes=[pltpu.VMEM((width, width), F32), pltpu.VMEM((8, width), F32)],
-        compiler_params=params(),
+            jax.ShapeDtypeStruct(y.shape, BF16),
+        ],
+        scratch_shapes=[
+            pltpu.VMEM((width, width), F32),
+            pltpu.VMEM((8, width), F32),
+            pltpu.SemaphoreType.DMA((n_f,)),
+            pltpu.SemaphoreType.DMA((n_f,)),
+        ],
+        compiler_params=params(collective_id=6, has_side_effects=True),
         cost_estimate=cost(2 * (slots + 2 * width) * count * width, 16 * count * width),
         name="hidden_back",
-    )(h, slot_col, db_back, long_cot, short_cot, o, dense, dense)
+    )(h, slot_col, db_back, long_cot, short_cot, o, dense, dense, y)
 
 
 def grads_kernel(
@@ -1203,17 +1262,12 @@
     pl.when((m >= 0) & (m < n_long))(lambda: finish(lo_ref))
     pl.when((m >= n_long) & (m < n_rows))(lambda: finish(so_ref))
 
-    @pl.when(i == begin_out - 1)
-    def _():
-        reducer.start_plane(0)
-
-    @pl.when(i == begin_out)
-    def _():
-        reducer.start_plane(1)
+    pl.when(i == begin_back + 1)(lambda: reducer.start_plane(0))
+    pl.when(i == begin_out - 1)(lambda: reducer.start_plane(1))
+    pl.when(i == begin_out + n_rows - 2)(lambda: reducer.start_plane(2))
 
     @pl.when(i == begin_out + n_rows - 1)
     def _():
-        reducer.start_plane(2)
         reducer.start_plane(3)
         for c in range(4):
             reducer.close(c)
@@ -1272,6 +1326,61 @@
     )(grad_proj, grad_vec, long_x, short_x, d_qkv, d_h, d_qkv, dense, dense, h, slot_col, y_back)
 
 
+def ship_kernel(n_long, width, *refs):
+    i = pl.program_id(0)
+    arrays_in, (owned_ref, down_ref), rest = refs[:4], refs[4:6], refs[6:]
+    arrays_out, (qkv_ref, proj_ref, vec_ref, grad_ref, pad_ref) = rest[:4], rest[4:]
+    for first in (0, 2):
+
+        @pl.when(i < n_long)
+        def _():
+            arrays_out[first][...] = arrays_in[first][...]
+
+        @pl.when(i >= n_long)
+        def _():
+            arrays_out[first + 1][...] = arrays_in[first + 1][...]
+
+    grad_ref[...] = down_ref[...].astype(F32)
+
+    @pl.when(i == 0)
+    def _():
+        share = owned_ref.shape[0]
+        qkv_ref[...] = owned_ref[:, width : 4 * width]
+        pad_ref[...] = jnp.zeros_like(pad_ref)
+        pad_ref[:share, :width] = owned_ref[:, :width]
+        pad_ref[:share, width:] = owned_ref[:, 4 * width :]
+        turned = jnp.transpose(pad_ref[...])
+        proj_ref[...] = turned[:width, :share]
+        vec_ref[...] = turned[width : width + 8, :share]
+
+
+def ship(arrays, owned, grad_down):
+    width = arrays[0].shape[1]
+    n_long, n_short = arrays[0].shape[0] // ROWS, arrays[1].shape[0] // ROWS
+    steps = n_long + n_short
+    share = owned.shape[0]
+    piece = pl.BlockSpec((grad_down.shape[0] // steps, width), lambda i: (i, 0))
+    whole = lambda shape: pl.BlockSpec(shape, lambda i: (0, 0))
+    return pl.pallas_call(
+        functools.partial(ship_kernel, n_long, width),
+        grid=(steps,),
+        in_specs=long_short(width, n_long) * 2 + [constant(owned.shape), piece],
+        out_specs=long_short(width, n_long) * 2
+        + [whole((share, 3 * width)), whole((width, share)), whole((8, share)), piece],
+        out_shape=[jax.ShapeDtypeStruct(a.shape, a.dtype) for a in arrays]
+        + [
+            jax.ShapeDtypeStruct((share, 3 * width), F32),
+            jax.ShapeDtypeStruct((width, share), F32),
+            jax.ShapeDtypeStruct((8, share), F32),
+            jax.ShapeDtypeStruct(grad_down.shape, F32),
+        ],
+        scratch_shapes=[pltpu.VMEM((LANES, width + LANES), F32)],
+        compiler_params=params(),
+        cost_estimate=cost(0, sum(8 * a.size for a in arrays)),
+        name="ship",
+    )(*arrays, owned, grad_down)
+
+
 def on_device(
     n_dp, n_f, long_x, short_x, long_len, short_len, expert_ids, ln1_gain, ln1_bias,
     w_qkv, w_proj, ln2_gain, ln2_bias, w_up, w_down, long_cot, short_cot,
@@ -1310,7 +1419,7 @@
     h, b_there, act, slope, grad_down = forward_experts(
         xl, xs, o, dense, slot_row, g_there, up, n_f, cap
     )
-    grad_down = lax.psum_scatter(grad_down, "dp", scatter_dimension=0, tiled=True).astype(F32)
+    grad_down = lax.psum_scatter(grad_down, "dp", scatter_dimension=0, tiled=True)
     y0, db0, gu0 = own_experts(
         lax.axis_index("dp").reshape(1), b_there, g_there, act, slope, up, w_down[0], n_f, cap
     )
@@ -1319,9 +1428,14 @@
     )
     db_back = db_back.reshape(slots, width)
     grad_up = lax.psum_scatter(grad_up, "dp", scatter_dimension=1, tiled=True).astype(F32)
-    y_back = exchange(y)
-    d_h, d_o, grad_proj, grad_vec = hidden_back(h, slot_col, db_back, gl, gs, o, dense)
-    d_qkv = attend_back(qkv, o, d_o, lse, long_len, short_len, seqs)
+    y = y.reshape(n_f, cap, width)
+    d_h, d_o, grad_proj, grad_vec, y_back = hidden_back(
+        h, slot_col, db_back, gl, gs, o, dense, y
+    )
+    d_qkv, y_back = attend_back(
+        qkv, o, d_o, lse, long_len, short_len, seqs, y, y_back
+    )
+    y_back = y_back.reshape(slots, width)
     if share % 8 == 0:
         owned, long_grad, short_grad, long_out, short_out = close_stage(
             grad_proj.reshape(n_dp, n_f, share, width), grad_vec,
@@ -1333,17 +1447,20 @@
             partial.reshape(n_dp, n_f, share, own.shape[1]),
             xl, xs, d_h, d_qkv, dense, h, slot_col, y_back,
         )
+    (long_grad, short_grad, long_out, short_out, grad_qkv, grad_proj, grad_vec, grad_down) = ship(
+        (long_grad, short_grad, long_out, short_out), owned, grad_down
+    )
     return (
         long_out.reshape(long_x.shape),
         short_out.reshape(short_x.shape),
         long_grad.reshape(long_x.shape),
         short_grad.reshape(short_x.shape),
-        owned[:, 4 * width],
-        owned[:, 4 * width + 1],
-        owned[:, width : 4 * width],
-        owned[:, :width].T,
-        owned[:, 4 * width + 2],
-        owned[:, 4 * width + 3],
+        grad_vec[0],
+        grad_vec[1],
+        grad_qkv,
+        grad_proj,
+        grad_vec[2],
+        grad_vec[3],
         grad_up[None],
         grad_down[None],
     )

time: 416 us -> 406 us (0.976)
  Pallas kernels: 349 us -> 363 us
  local copies, waits for them, and re-layouts: 17.1 us -> 5.08 us
  starting transfers between devices: 16 us -> 5.91 us
    pallas_call x2 -> x3, Pallas kernels: 54.6 us -> 72.1 us  [the longest x1 37.1 us: attend_back(): pl.pallas_call(functools.partial(attend_back_kernel, seqs, n_f), grid=(pa...]
    all_to_all x2 -> x1, starting transfers between devices: 15.7 us -> 5.58 us  [exchange(): lax.all_to_all(rows.reshape(n_f, cap, width), 'fsdp', split_axis=0, conca...]
    unnamed x21 -> x8, local copies, waits for them, and re-layouts: 12.2 us -> 3.65 us
  transfers between devices with their start and end apart: 6 -> 5, of which waited for: 2 -> 2; matrix products, arithmetic and copies ran while one was open for 3% -> 2% of each run, Pallas kernels for 85% -> 91%
where the time goes in v4:
time: 406 us; the launch traced here: 400 us
  Pallas kernels  363 us (89%)
  between operations  15.5 us (4%)
  waiting for transfers between devices  6.16 us (2%)
  starting transfers between devices  5.91 us (1%)
  local copies, waits for them, and re-layouts  5.08 us (1%)
  other arithmetic  4.24 us (1%)
    pallas_call x1, Pallas kernels, forward_experts(): pl.pallas_call(functools.partial(forward_kernel, n_f, n_long, n_rows), gr...  72.2 us
    pallas_call x1, Pallas kernels, close_stage(): pl.pallas_call(functools.partial(close_kernel, n_long, n_rows), grid=(3 +...  66.4 us
    pallas_call x1, Pallas kernels, back_experts(): pl.pallas_call(functools.partial(back_kernel, n_dp, n_f), grid=(n_f + n_d...  50 us
    pallas_call x1, Pallas kernels, gather_dense(): pl.pallas_call(functools.partial(gather_kernel, n_dp, n_f, cap), out_shap...  49.6 us
    pallas_call x1, Pallas kernels, attend_back(): pl.pallas_call(functools.partial(attend_back_kernel, seqs, n_f), grid=(pa...  37.1 us
    pallas_call x1, Pallas kernels, hidden_back(): pl.pallas_call(functools.partial(hidden_back_kernel, n_f, n_long, n_rows)...  26.3 us
    pallas_call x1, Pallas kernels, attend(): pl.pallas_call(functools.partial(attend_kernel, seqs), grid=(pairs,), in_...  21.9 us
    pallas_call x1, Pallas kernels, own_experts(): pl.pallas_call(functools.partial(own_kernel, n_f), grid_spec=pltpu.Prefet...  19.4 us
  transfers between devices with their start and end apart: 5, of which 2 were waited for; matrix products, arithmetic and copies ran while one was open for 2% of the time, Pallas kernels for 91%

profile of v4, /device:TPU:12, one launch (start us, length us, event | category | flops | bytes accessed | tf_op | source)
XLA Modules:
  0.0 400.2 jit_solution(1344831228671775361)
XLA Ops:
  7.2 0.0 copy-start.2
  7.2 0.0 all-gather.3.cloned.1.call-start
  7.2 0.7 all-gather.3.cloned.1.call-update
  7.9 0.0 all-gather.5.cloned.1.call-start
  8.0 0.7 all-gather.5.cloned.1.call-update
  8.7 0.7 pad_maximum_fusion
  9.4 0.1 copy.34
  9.5 1.9 copy.35.ids_ref
  11.4 0.7 fusion.1.own_ref
  12.1 49.6 %gather_dense.1 = (bf16[4,8,24,3200]{3,2,1,0:T(8,128)(2,1)}, s32[1536,1]{1,0:T(8,128)}, s32[8,1536]{1,0:T(8,128)}, bf16[2048,768]{1,0:T(8,128)(2,1)}) custom-call(bf16[24,3200]{1,0:T(8,128)(2,1)} %fusion.1.own_ref, s32[1536,1]{1,0:T(8,128)} %copy.35.ids_ref, f32[1024,768]{1,0:T(8,128)} %bitcast.51, f32[512,768]{1,0:T(8,128)} %bitcast.57), custom_call_target="tpu_custom_call" | custom-call | bytes 100000000 | tf_op jit(solution)/shard_map/gather_dense/pallas_call | solution.py:158
  61.6 5.6 %all-to-all-start = ((bf16[8,256,768]{2,1,0:T(8,128)(2,1)}), bf16[8,256,768]{2,1,0:T(8,128)(2,1)S(1)}, u32[]{:S(2)}, u32[]{:S(2)}) async-start(bf16[8,256,768]{2,1,0:T(8,128)(2,1)} %bitcast.53), calls=%async_computation | async-start | bytes 6291456 | tf_op jit(solution)/shard_map/all_to_all | solution.py:1411
  67.2 0.2 reduce-scatter.3.cloned.1.call-start
  68.7 11.6 %make_qkv.1.q_ref.k_ref.v_ref = bf16[1536,2304]{1,0:T(8,128)(2,1)} custom-call(f32[1024,768]{1,0:T(8,128)} %bitcast.54, f32[512,768]{1,0:T(8,128)} %bitcast.59, bf16[768,3200]{1,0:T(8,128)(2,1)} %bitcast.36, bf16[768,3200]{1,0:T(8,128)(2,1)} %bitcast.37), custom_call_target="tpu_custom_call" | custom-call | flops 5435817984 | bytes 15335424 | tf_op jit(solution)/shard_map/make_qkv/pallas_call | solution.py:278
  80.3 21.9 %attend.1 = (bf16[1536,768]{1,0:T(8,128)(2,1)}, f32[128,1536]{1,0:T(8,128)}) custom-call(s32[1]{0:T(128)S(6)} %copy.38.long_len, s32[1]{0:T(128)S(6)} %copy.39.short_len, bf16[1536,2304]{1,0:T(8,128)(2,1)} %make_qkv.1.q_ref.k_ref.v_ref, bf16[1536,2304]{1,0:T(8,128)(2,1)} %make_qkv.1.q_ref.k_ref.v_ref, bf16[1536,2304]{1,0:T(8,128)(2,1)} %make_qkv.1.q_ref.k_ref.v_ref), custom_call_target="tpu_custom_call" | custom-call | flops 16000000000 | bytes 9437184 | tf_op jit(solution)/shard_map/attend/pallas_call | solution.py:371
  102.2 1.9 all-to-all-done
  104.1 2.8 all-gather.3.cloned.1.call-done
  106.9 0.0 copy-done
  106.9 72.2 %forward_experts.1 = (f32[1536,768]{1,0:T(8,128)}, bf16[2048,768]{1,0:T(8,128)(2,1)}, bf16[2048,3072]{1,0:T(8,128)(2,1)}, bf16[2048,3072]{1,0:T(8,128)(2,1)}, bf16[3072,768]{1,0:T(8,128)(2,1)}) custom-call(f32[1024,768]{1,0:T(8,128)} %bitcast.55, f32[512,768]{1,0:T(8,128)} %bitcast.60, bf16[1536,768]{1,0:T(8,128)(2,1)} %get-tuple-element.50.o_ref, ...), custom_call_target="tpu_custom_call" | custom-call | flops 24159191040 | bytes 60000000 | tf_op jit(solution)/shard_map/forward_experts/pallas_call | solution.py:603
  179.1 0.0 reduce-scatter.3.cloned.1.call-update
  179.2 0.0 reduce-scatter.5.cloned.1.call-start
  179.2 19.4 %own_experts.1 = (f32[2048,768]{1,0:T(8,128)}, f32[2048,768]{1,0:T(8,128)}, bf16[768,768]{1,0:T(8,128)(2,1)}) custom-call(s32[1]{0:T(128)} %bitcast.14.z_ref, bf16[2048,768]{1,0:T(8,128)(2,1)} %get-tuple-element.55.b_ref, bf16[2048,768]{1,0:T(8,128)(2,1)} %bitcast.45, bf16[2048,3072]{1,0:T(8,128)(2,1)} %get-tuple-element.56.act_ref, ...), custom_call_target="tpu_custom_call" | custom-call | flops 9663676416 | bytes 30000000 | tf_op jit(solution)/shard_map/own_experts/pallas_call | solution.py:673
  198.6 0.0 all-gather.5.cloned.1.call-done
  198.6 50.0 %back_experts.1 = (bf16[2048,768]{1,0:T(8,128)(2,1)}, bf16[8,256,768]{2,1,0:T(8,128)(2,1)}, bf16[768,3072]{1,0:T(8,128)(2,1)}) custom-call(bf16[2048,768]{1,0:T(8,128)(2,1)} %get-tuple-element.55.b_ref, bf16[2048,768]{1,0:T(8,128)(2,1)} %bitcast.46, bf16[2048,3072]{1,0:T(8,128)(2,1)} %get-tuple-element.56.act_ref, ...), custom_call_target="tpu_custom_call" | custom-call | flops 28991029248 | bytes 60000000 | tf_op jit(solution)/shard_map/back_experts/pallas_call | solution.py:783
  248.6 0.0 reduce-scatter.5.cloned.1.call-update
  248.7 26.3 %hidden_back.1 = (f32[1536,768]{1,0:T(8,128)}, bf16[1536,768]{1,0:T(8,128)(2,1)}, bf16[768,768]{1,0:T(8,128)(2,1)}, f32[128,768]{1,0:T(8,128)}, bf16[8,256,768]{2,1,0:T(8,128)(2,1)}) custom-call(f32[1536,768]{1,0:T(8,128)} %get-tuple-element.53.h_ref, s32[1536,1]{1,0:T(8,128)} %get-tuple-element.54.col_ref, bf16[2048,768]{1,0:T(8,128)(2,1)} %bitcast.75, ...), custom_call_target="tpu_custom_call" | custom-call | flops 8455716864 | bytes 18874368 | tf_op jit(solution)/shard_map/hidden_back/pallas_call | solution.py:867
  275.0 37.1 %attend_back.1 = (bf16[3,1536,768]{2,1,0:T(8,128)(2,1)}, bf16[8,256,768]{2,1,0:T(8,128)(2,1)}) custom-call(s32[1]{0:T(128)S(6)} %copy.38.long_len, s32[1]{0:T(128)S(6)} %copy.39.short_len, bf16[1536,2304]{1,0:T(8,128)(2,1)} %make_qkv.1.q_ref.k_ref.v_ref, bf16[1536,2304]{1,0:T(8,128)(2,1)} %make_qkv.1.q_ref.k_ref.v_ref, ...), custom_call_target="tpu_custom_call", output_to_operand_aliasing={{1}: (9, {})} | custom-call | flops 40000000000 | bytes 18874368 | tf_op jit(solution)/shard_map/attend_back/pallas_call | solution.py:468
  312.1 66.4 %close_stage.1 = (f32[24,3200]{1,0:T(8,128)}, f32[1024,768]{1,0:T(8,128)}, f32[512,768]{1,0:T(8,128)}, f32[1024,768]{1,0:T(8,128)}, f32[512,768]{1,0:T(8,128)}) custom-call(bf16[4,8,24,768]{3,2,1,0:T(8,128)(2,1)} %bitcast.77, f32[128,768]{1,0:T(8,128)} %get-tuple-element.64.gv_ref, f32[1024,768]{1,0:T(8,128)} %bitcast.56, f32[512,768]{1,0:T(8,128)} %bitcast.61, ...), custom_call_target="tpu_custom_call" | custom-call | flops 15703474176 | bytes 60000000 | tf_op jit(solution)/shard_map/close_stage/pallas_call | solution.py:1285
  378.6 0.0 reduce-scatter.3.cloned.1.call-done.refs_5_
  378.6 8.7 %ship.1 = (f32[1024,768]{1,0:T(8,128)}, f32[512,768]{1,0:T(8,128)}, f32[1024,768]{1,0:T(8,128)}, f32[512,768]{1,0:T(8,128)}, f32[24,2304]{1,0:T(8,128)}, /*index...) custom-call(f32[1024,768]{1,0:T(8,128)} %get-tuple-element.71.refs_0_, f32[512,768]{1,0:T(8,128)} %get-tuple-element.72.refs_1_, ...), custom_call_target="tpu_custom_call" | custom-call | bytes 18874368 | tf_op jit(solution)/shard_map/ship/pallas_call | solution.py:1364
  387.3 1.8 copy.36
  389.1 1.3 slice_bitcast_fusion
  390.4 2.8 bitcast_convert_fusion
  (5 shorter events, 0.0 us)
Async XLA Ops:
  7.2 4.2 %copy-start.2 = (bf16[768,24]{0,1:T(8,128)(2,1)S(1)}, bf16[768,24]{0,1:T(8,128)(2,1)}, u32[]{:S(2)}) copy-start(bf16[768,24]{0,1:T(8,128)(2,1)} %param.23) | copy-start | bytes 110596
  7.2 4.2 %copy-start.1 = (bf16[24,2304]{1,0:T(8,128)(2,1)S(1)}, bf16[24,2304]{1,0:T(8,128)(2,1)}, u32[]{:S(2)}) copy-start(bf16[24,2304]{1,0:T(8,128)(2,1)} %param.22) | copy-start | bytes 331780
  7.2 99.7 %all-gather.3.cloned.1.call-start = ((), (), s32[]{:S(2)}) async-start(), calls=%async_computation.3 | async-start | bytes 5898240 | tf_op jit(solution)/shard_map/all_gather | solution.py:1398
  7.9 190.7 %all-gather.5.cloned.1.call-start = ((), (), s32[]{:S(2)}) async-start(), calls=%async_computation.4 | async-start | bytes 5898240 | tf_op jit(solution)/shard_map/all_gather | solution.py:1399
  61.6 42.5 %all-to-all-start = ((bf16[8,256,768]{2,1,0:T(8,128)(2,1)}), bf16[8,256,768]{2,1,0:T(8,128)(2,1)S(1)}, u32[]{:S(2)}, u32[]{:S(2)}) async-start(bf16[8,256,768]{2,1,0:T(8,128)(2,1)} %bitcast.53), calls=%async_computation | async-start | bytes 6291456 | tf_op jit(solution)/shard_map/all_to_all | solution.py:1411
  67.2 311.4 %reduce-scatter.3.cloned.1.call-start = ((), (), s32[]{:S(2)}) async-start(), calls=%async_computation.5 | async-start | bytes 5898240 | tf_op jit(solution)/shard_map/reduce_scatter | solution.py:1422
  104.1 2.8 copy-start
  179.2 211.2 %reduce-scatter.5.cloned.1.call-start = ((), (), s32[]{:S(2)}) async-start(), calls=%async_computation.6 | async-start | bytes 5898240 | tf_op jit(solution)/shard_map/reduce_scatter | solution.py:1430
Sparse Core Ops, SparseCore 0:
  9.6 97.2 all-gather.2
  108.5 88.9 all-gather.4
  199.8 86.2 reduce-scatter.2
  288.2 98.9 reduce-scatter.4

commit v5 on v4

--- a/solution.py
+++ b/solution.py
@@ -240,6 +240,8 @@
 
     def begin(self):
         greet(self.n_f, self.to)
+
+    def launch(self):
         pl.semaphore_wait(pltpu.get_barrier_semaphore(), self.n_f - 1)
         for k in self.ks:
             self.transfer(k).start()
@@ -407,6 +409,7 @@
         home.begin()
         keep.start()
         lse_scr[...] = jnp.transpose(lse_ref[...])
+        home.launch()
 
     causal = lax.broadcasted_iota(jnp.int32, (ATTEND_BACK, ATTEND_BACK), 1) <= (
         lax.broadcasted_iota(jnp.int32, (ATTEND_BACK, ATTEND_BACK), 0)
@@ -836,6 +839,7 @@
         vec_scr[...] = vectors(vec_ref)
         acc_ref[...] = jnp.zeros_like(acc_ref)
         gv_ref[...] = jnp.zeros_like(gv_ref)
+        home.launch()
 
     def body(cot_ref):
         d_b = combine_rows(col_ref, db_ref)
@@ -1329,7 +1333,7 @@
 def ship_kernel(n_long, width, *refs):
     i = pl.program_id(0)
     arrays_in, (owned_ref, down_ref), rest = refs[:4], refs[4:6], refs[6:]
-    arrays_out, (qkv_ref, proj_ref, vec_ref, grad_ref, pad_ref) = rest[:4], rest[4:]
+    arrays_out, (qkv_ref, proj_ref, grad_ref), vec_refs, pad_ref = rest[:4], rest[4:7], rest[7:11], rest[11]
     for first in (0, 2):
 
         @pl.when(i < n_long)
@@ -1347,11 +1351,11 @@
         share = owned_ref.shape[0]
         qkv_ref[...] = owned_ref[:, width : 4 * width]
         pad_ref[...] = jnp.zeros_like(pad_ref)
-        pad_ref[:share, :width] = owned_ref[:, :width]
-        pad_ref[:share, width:] = owned_ref[:, 4 * width :]
+        pad_ref[:share, :] = owned_ref[:, 4 * width :]
+        proj_ref[...] = owned_ref[:, :width]
         turned = jnp.transpose(pad_ref[...])
-        proj_ref[...] = turned[:width, :share]
-        vec_ref[...] = turned[width : width + 8, :share]
+        for row, vec_ref in enumerate(vec_refs):
+            vec_ref[...] = turned[row : row + 1, :share]
 
 
 def ship(arrays, owned, grad_down):
@@ -1366,15 +1370,16 @@
         grid=(steps,),
         in_specs=long_short(width, n_long) * 2 + [constant(owned.shape), piece],
         out_specs=long_short(width, n_long) * 2
-        + [whole((share, 3 * width)), whole((width, share)), whole((8, share)), piece],
+        + [whole((share, 3 * width)), whole((share, width)), piece]
+        + [whole((1, share))] * 4,
         out_shape=[jax.ShapeDtypeStruct(a.shape, a.dtype) for a in arrays]
         + [
             jax.ShapeDtypeStruct((share, 3 * width), F32),
-            jax.ShapeDtypeStruct((width, share), F32),
-            jax.ShapeDtypeStruct((8, share), F32),
+            jax.ShapeDtypeStruct((share, width), F32),
             jax.ShapeDtypeStruct(grad_down.shape, F32),
-        ],
-        scratch_shapes=[pltpu.VMEM((LANES, width + LANES), F32)],
+        ]
+        + [jax.ShapeDtypeStruct((1, share), F32)] * 4,
+        scratch_shapes=[pltpu.VMEM((LANES, LANES), F32)],
         compiler_params=params(),
         cost_estimate=cost(0, sum(8 * a.size for a in arrays)),
         name="ship",
@@ -1427,7 +1432,7 @@
         b_there, g_there, act, slope, up, down, y0, db0, gu0, n_dp, n_f, cap
     )
     db_back = db_back.reshape(slots, width)
-    grad_up = lax.psum_scatter(grad_up, "dp", scatter_dimension=1, tiled=True).astype(F32)
+    grad_up = lax.psum_scatter(grad_up, "dp", scatter_dimension=1, tiled=True)
     y = y.reshape(n_f, cap, width)
     d_h, d_o, grad_proj, grad_vec, y_back = hidden_back(
         h, slot_col, db_back, gl, gs, o, dense, y
@@ -1447,20 +1452,22 @@
             partial.reshape(n_dp, n_f, share, own.shape[1]),
             xl, xs, d_h, d_qkv, dense, h, slot_col, y_back,
         )
-    (long_grad, short_grad, long_out, short_out, grad_qkv, grad_proj, grad_vec, grad_down) = ship(
+    (long_grad, short_grad, long_out, short_out, grad_qkv, grad_proj, grad_down, *grad_vec) = ship(
         (long_grad, short_grad, long_out, short_out), owned, grad_down
     )
+    grad_up, grad_down = lax.optimization_barrier((grad_up, grad_down))
+    grad_up = grad_up.astype(F32)
     return (
         long_out.reshape(long_x.shape),
         short_out.reshape(short_x.shape),
         long_grad.reshape(long_x.shape),
         short_grad.reshape(short_x.shape),
-        grad_vec[0],
-        grad_vec[1],
+        grad_vec[0].reshape(-1),
+        grad_vec[1].reshape(-1),
         grad_qkv,
-        grad_proj,
-        grad_vec[2],
-        grad_vec[3],
+        grad_proj.T,
+        grad_vec[2].reshape(-1),
+        grad_vec[3].reshape(-1),
         grad_up[None],
         grad_down[None],
     )

time: 406 us -> 403 us (level)
  transfers between devices with their start and end apart: 5 -> 5, of which waited for: 2 -> 3; matrix products, arithmetic and copies ran while one was open for 2% -> 1% of each run, Pallas kernels for 91% -> 91%
where the time goes in v5:
time: 403 us; the launch traced here: 397 us
  Pallas kernels  363 us (90%)
  between operations  15.5 us (4%)
  waiting for transfers between devices  6.26 us (2%)
  starting transfers between devices  5.91 us (1%)
  other arithmetic  4.24 us (1%)
    pallas_call x1, Pallas kernels, forward_experts(): pl.pallas_call(functools.partial(forward_kernel, n_f, n_long, n_rows), gr...  72.3 us
    pallas_call x1, Pallas kernels, close_stage(): pl.pallas_call(functools.partial(close_kernel, n_long, n_rows), grid=(3 +...  66.5 us
    pallas_call x1, Pallas kernels, back_experts(): pl.pallas_call(functools.partial(back_kernel, n_dp, n_f), grid=(n_f + n_d...  50.2 us
    pallas_call x1, Pallas kernels, gather_dense(): pl.pallas_call(functools.partial(gather_kernel, n_dp, n_f, cap), out_shap...  49.6 us
    pallas_call x1, Pallas kernels, attend_back(): pl.pallas_call(functools.partial(attend_back_kernel, seqs, n_f), grid=(pa...  36.8 us
    pallas_call x1, Pallas kernels, hidden_back(): pl.pallas_call(functools.partial(hidden_back_kernel, n_f, n_long, n_rows)...  26.3 us
    pallas_call x1, Pallas kernels, attend(): pl.pallas_call(functools.partial(attend_kernel, seqs), grid=(pairs,), in_...  21.9 us
    pallas_call x1, Pallas kernels, own_experts(): pl.pallas_call(functools.partial(own_kernel, n_f), grid_spec=pltpu.Prefet...  19.4 us
  transfers between devices with their start and end apart: 5, of which 3 were waited for; matrix products, arithmetic and copies ran while one was open for 1% of the time, Pallas kernels for 91%

profile of v5, /device:TPU:12, one launch (start us, length us, event | category | flops | bytes accessed | tf_op | source)
XLA Modules:
  0.0 397.0 jit_solution(3624789744669281102)
XLA Ops:
  7.2 0.0 copy-start.2
  7.2 0.0 copy-start.1
  7.2 0.0 all-gather.3.cloned.1.call-start
  7.2 0.7 all-gather.3.cloned.1.call-update
  7.9 0.0 all-gather.5.cloned.1.call-start
  8.0 0.7 all-gather.5.cloned.1.call-update
  8.7 0.7 pad_maximum_fusion
  9.4 0.1 copy.33
  9.5 1.9 copy.34.ids_ref
  11.4 0.0 copy-done.2
  11.4 0.7 fusion.1.own_ref
  12.1 49.6 %gather_dense.1 = (bf16[4,8,24,3200]{3,2,1,0:T(8,128)(2,1)}, s32[1536,1]{1,0:T(8,128)}, s32[8,1536]{1,0:T(8,128)}, bf16[2048,768]{1,0:T(8,128)(2,1)}) custom-call(bf16[24,3200]{1,0:T(8,128)(2,1)} %fusion.1.own_ref, s32[1536,1]{1,0:T(8,128)} %copy.34.ids_ref, f32[1024,768]{1,0:T(8,128)} %bitcast.48, f32[512,768]{1,0:T(8,128)} %bitcast.54), custom_call_target="tpu_custom_call" | custom-call | bytes 100000000 | tf_op jit(solution)/shard_map/gather_dense/pallas_call | solution.py:158
  61.7 5.6 %all-to-all-start = ((bf16[8,256,768]{2,1,0:T(8,128)(2,1)}), bf16[8,256,768]{2,1,0:T(8,128)(2,1)S(1)}, u32[]{:S(2)}, u32[]{:S(2)}) async-start(bf16[8,256,768]{2,1,0:T(8,128)(2,1)} %bitcast.50), calls=%async_computation | async-start | bytes 6291456 | tf_op jit(solution)/shard_map/all_to_all | solution.py:1416
  67.2 0.2 reduce-scatter.3.cloned.1.call-start
  68.7 11.6 %make_qkv.1.q_ref.k_ref.v_ref = bf16[1536,2304]{1,0:T(8,128)(2,1)} custom-call(f32[1024,768]{1,0:T(8,128)} %bitcast.51, f32[512,768]{1,0:T(8,128)} %bitcast.56, bf16[768,3200]{1,0:T(8,128)(2,1)} %bitcast.33, bf16[768,3200]{1,0:T(8,128)(2,1)} %bitcast.34), custom_call_target="tpu_custom_call" | custom-call | flops 5435817984 | bytes 15335424 | tf_op jit(solution)/shard_map/make_qkv/pallas_call | solution.py:280
  80.3 21.9 %attend.1 = (bf16[1536,768]{1,0:T(8,128)(2,1)}, f32[128,1536]{1,0:T(8,128)}) custom-call(s32[1]{0:T(128)S(6)} %copy.36.long_len, s32[1]{0:T(128)S(6)} %copy.37.short_len, bf16[1536,2304]{1,0:T(8,128)(2,1)} %make_qkv.1.q_ref.k_ref.v_ref, bf16[1536,2304]{1,0:T(8,128)(2,1)} %make_qkv.1.q_ref.k_ref.v_ref, bf16[1536,2304]{1,0:T(8,128)(2,1)} %make_qkv.1.q_ref.k_ref.v_ref), custom_call_target="tpu_custom_call" | custom-call | flops 16000000000 | bytes 9437184 | tf_op jit(solution)/shard_map/attend/pallas_call | solution.py:373
  102.2 2.0 all-to-all-done
  104.2 2.8 all-gather.3.cloned.1.call-done
  106.9 72.3 %forward_experts.1 = (f32[1536,768]{1,0:T(8,128)}, bf16[2048,768]{1,0:T(8,128)(2,1)}, bf16[2048,3072]{1,0:T(8,128)(2,1)}, bf16[2048,3072]{1,0:T(8,128)(2,1)}, bf16[3072,768]{1,0:T(8,128)(2,1)}) custom-call(f32[1024,768]{1,0:T(8,128)} %bitcast.52, f32[512,768]{1,0:T(8,128)} %bitcast.57, bf16[1536,768]{1,0:T(8,128)(2,1)} %get-tuple-element.55.o_ref, ...), custom_call_target="tpu_custom_call" | custom-call | flops 24159191040 | bytes 60000000 | tf_op jit(solution)/shard_map/forward_experts/pallas_call | solution.py:606
  179.2 0.0 reduce-scatter.3.cloned.1.call-update
  179.2 0.0 reduce-scatter.5.cloned.1.call-start
  179.3 19.4 %own_experts.1 = (f32[2048,768]{1,0:T(8,128)}, f32[2048,768]{1,0:T(8,128)}, bf16[768,768]{1,0:T(8,128)(2,1)}) custom-call(s32[1]{0:T(128)} %bitcast.14.z_ref, bf16[2048,768]{1,0:T(8,128)(2,1)} %get-tuple-element.60.b_ref, bf16[2048,768]{1,0:T(8,128)(2,1)} %bitcast.42, bf16[2048,3072]{1,0:T(8,128)(2,1)} %get-tuple-element.61.act_ref, ...), custom_call_target="tpu_custom_call" | custom-call | flops 9663676416 | bytes 30000000 | tf_op jit(solution)/shard_map/own_experts/pallas_call | solution.py:676
  198.7 0.0 all-gather.5.cloned.1.call-done
  198.7 50.2 %back_experts.1 = (bf16[2048,768]{1,0:T(8,128)(2,1)}, bf16[8,256,768]{2,1,0:T(8,128)(2,1)}, bf16[768,3072]{1,0:T(8,128)(2,1)}) custom-call(bf16[2048,768]{1,0:T(8,128)(2,1)} %get-tuple-element.60.b_ref, bf16[2048,768]{1,0:T(8,128)(2,1)} %bitcast.43, bf16[2048,3072]{1,0:T(8,128)(2,1)} %get-tuple-element.61.act_ref, ...), custom_call_target="tpu_custom_call" | custom-call | flops 28991029248 | bytes 60000000 | tf_op jit(solution)/shard_map/back_experts/pallas_call | solution.py:786
  248.9 0.0 reduce-scatter.5.cloned.1.call-update
  248.9 26.3 %hidden_back.1 = (f32[1536,768]{1,0:T(8,128)}, bf16[1536,768]{1,0:T(8,128)(2,1)}, bf16[768,768]{1,0:T(8,128)(2,1)}, f32[128,768]{1,0:T(8,128)}, bf16[8,256,768]{2,1,0:T(8,128)(2,1)}) custom-call(f32[1536,768]{1,0:T(8,128)} %get-tuple-element.58.h_ref, s32[1536,1]{1,0:T(8,128)} %get-tuple-element.59.col_ref, bf16[2048,768]{1,0:T(8,128)(2,1)} %bitcast.77, ...), custom_call_target="tpu_custom_call" | custom-call | flops 8455716864 | bytes 18874368 | tf_op jit(solution)/shard_map/hidden_back/pallas_call | solution.py:871
  275.2 36.8 %attend_back.1 = (bf16[3,1536,768]{2,1,0:T(8,128)(2,1)}, bf16[8,256,768]{2,1,0:T(8,128)(2,1)}) custom-call(s32[1]{0:T(128)S(6)} %copy.36.long_len, s32[1]{0:T(128)S(6)} %copy.37.short_len, bf16[1536,2304]{1,0:T(8,128)(2,1)} %make_qkv.1.q_ref.k_ref.v_ref, bf16[1536,2304]{1,0:T(8,128)(2,1)} %make_qkv.1.q_ref.k_ref.v_ref, ...), custom_call_target="tpu_custom_call", output_to_operand_aliasing={{1}: (9, {})} | custom-call | flops 40000000000 | bytes 18874368 | tf_op jit(solution)/shard_map/attend_back/pallas_call | solution.py:471
  312.0 66.5 %close_stage.1 = (f32[24,3200]{1,0:T(8,128)}, f32[1024,768]{1,0:T(8,128)}, f32[512,768]{1,0:T(8,128)}, f32[1024,768]{1,0:T(8,128)}, f32[512,768]{1,0:T(8,128)}) custom-call(bf16[4,8,24,768]{3,2,1,0:T(8,128)(2,1)} %bitcast.79, f32[128,768]{1,0:T(8,128)} %get-tuple-element.69.gv_ref, f32[1024,768]{1,0:T(8,128)} %bitcast.53, f32[512,768]{1,0:T(8,128)} %bitcast.58, ...), custom_call_target="tpu_custom_call" | custom-call | flops 15703474176 | bytes 60000000 | tf_op jit(solution)/shard_map/close_stage/pallas_call | solution.py:1289
  378.6 0.0 reduce-scatter.3.cloned.1.call-done.refs_5_
  378.6 8.5 %ship.1 = (f32[1024,768]{1,0:T(8,128)}, f32[512,768]{1,0:T(8,128)}, f32[1024,768]{1,0:T(8,128)}, f32[512,768]{1,0:T(8,128)}, f32[24,2304]{1,0:T(8,128)}, /*index...) custom-call(f32[1024,768]{1,0:T(8,128)} %get-tuple-element.76.refs_0, ...), custom_call_target="tpu_custom_call" | custom-call | bytes 18874368 | tf_op jit(solution)/shard_map/ship/pallas_call | solution.py:1368
  387.1 0.1 reduce-scatter.5.cloned.1.call-done
  387.2 2.8 bitcast_convert_fusion
  (3 shorter events, 0.0 us)
Async XLA Ops:
  7.2 4.2 %copy-start.2 = (bf16[768,24]{0,1:T(8,128)(2,1)S(1)}, bf16[768,24]{0,1:T(8,128)(2,1)}, u32[]{:S(2)}) copy-start(bf16[768,24]{0,1:T(8,128)(2,1)} %param.23) | copy-start | bytes 110596
  7.2 4.2 %copy-start.1 = (bf16[24,2304]{1,0:T(8,128)(2,1)S(1)}, bf16[24,2304]{1,0:T(8,128)(2,1)}, u32[]{:S(2)}) copy-start(bf16[24,2304]{1,0:T(8,128)(2,1)} %param.22) | copy-start | bytes 331780
  7.2 99.7 %all-gather.3.cloned.1.call-start = ((), (), s32[]{:S(2)}) async-start(), calls=%async_computation.3 | async-start | bytes 5898240 | tf_op jit(solution)/shard_map/all_gather | solution.py:1403
  7.9 190.8 %all-gather.5.cloned.1.call-start = ((), (), s32[]{:S(2)}) async-start(), calls=%async_computation.4 | async-start | bytes 5898240 | tf_op jit(solution)/shard_map/all_gather | solution.py:1404
  61.7 42.5 %all-to-all-start = ((bf16[8,256,768]{2,1,0:T(8,128)(2,1)}), bf16[8,256,768]{2,1,0:T(8,128)(2,1)S(1)}, u32[]{:S(2)}, u32[]{:S(2)}) async-start(bf16[8,256,768]{2,1,0:T(8,128)(2,1)} %bitcast.50), calls=%async_computation | async-start | bytes 6291456 | tf_op jit(solution)/shard_map/all_to_all | solution.py:1416
  67.2 311.4 %reduce-scatter.3.cloned.1.call-start = ((), (), s32[]{:S(2)}) async-start(), calls=%async_computation.5 | async-start | bytes 5898240 | tf_op jit(solution)/shard_map/reduce_scatter | solution.py:1427
  104.2 2.8 copy-start
  179.2 208.0 %reduce-scatter.5.cloned.1.call-start = ((), (), s32[]{:S(2)}) async-start(), calls=%async_computation.6 | async-start | bytes 5898240 | tf_op jit(solution)/shard_map/reduce_scatter | solution.py:1435
Sparse Core Ops, SparseCore 0:
  9.6 97.2 all-gather.2
  108.5 88.9 all-gather.4
  199.8 86.2 reduce-scatter.2
  288.2 98.9 reduce-scatter.4

commit v6 on v5

--- a/solution.py
+++ b/solution.py
@@ -223,6 +223,14 @@
     barrier = pltpu.get_barrier_semaphore()
     for k in range(1, n_f):
         pl.semaphore_signal(barrier, 1, device_id=(z, to(k)), device_id_type=MESH)
+
+
+def early_blocks(n_f):
+    return [k for k in range(1, n_f) if k & (k - 1) == 0]
+
+
+def late_blocks(n_f):
+    return [k for k in range(1, n_f) if k & (k - 1) != 0]
 
 
 class Homeward:
@@ -401,7 +409,7 @@
     masks = head_masks()
     lane = lax.broadcasted_iota(jnp.int32, (1, LANES), 1)
 
-    home = Homeward(n_f, range(3 * n_f // 4, n_f), y_ref, yb_ref, send, recv)
+    home = Homeward(n_f, late_blocks(n_f), y_ref, yb_ref, send, recv)
     keep = pltpu.make_async_copy(y_ref.at[home.f], yb_ref.at[home.f], l_sem)
 
     @pl.when(pair == 0)
@@ -505,6 +513,81 @@
     )(long_len, short_len, qkv, qkv, qkv, o, d_o, lse, y, y_back)
 
 
+class Line:
+    def __init__(self, own_ref, all_ref, send, recv, l_sem):
+        self.own, self.all, self.send, self.recv = own_ref, all_ref, send, recv
+        self.n = all_ref.shape[0]
+        self.z = lax.axis_index("dp")
+        self.f = lax.axis_index("fsdp")
+        self.barrier = pltpu.get_barrier_semaphore()
+        self.keep = pltpu.make_async_copy(own_ref, all_ref.at[self.z], l_sem)
+        half = all_ref.shape[1] // 2
+        self.chunks = (pl.ds(0, half), pl.ds(half, half))
+        self.sides = (1, -1)
+
+    def exists(self, place):
+        return (place >= 0) & (place < self.n)
+
+    def copy(self, hop, index, chunk, plane):
+        side, rows = self.sides[index], self.chunks[chunk]
+        src = self.own.at[rows] if hop == 1 else self.all.at[plane, rows]
+        return pltpu.make_async_remote_copy(
+            src, self.all.at[plane, rows],
+            self.send.at[hop - 1, index, chunk], self.recv.at[hop - 1, index, chunk],
+            device_id=(self.z + side, self.f), device_id_type=MESH,
+        )
+
+    def greet(self):
+        for side in self.sides:
+
+            @pl.when(self.exists(self.z + side))
+            def _(side=side):
+                pl.semaphore_signal(
+                    self.barrier, 1, device_id=(self.z + side, self.f), device_id_type=MESH
+                )
+
+    def neighbours(self):
+        return jnp.minimum(self.z, 1) + jnp.minimum(self.n - 1 - self.z, 1)
+
+    def pass_on(self, hop, chunk):
+        for index, side in enumerate(self.sides):
+            plane = self.z - side * (hop - 1)
+
+            @pl.when(self.exists(self.z + side) & self.exists(plane))
+            def _(index=index, plane=plane):
+                self.copy(hop, index, chunk, plane).start()
+
+    def arrive(self, hop, chunk):
+        for index, side in enumerate(self.sides):
+            plane = self.z - side * hop
+
+            @pl.when(self.exists(plane))
+            def _(index=index, plane=plane):
+                self.copy(hop, index, chunk, plane).wait_recv()
+
+    def begin(self):
+        self.keep.start()
+        for chunk in range(2):
+            self.pass_on(1, chunk)
+
+    def event(self, number):
+        hop, chunk = 1 + number // 2, number % 2
+        self.arrive(hop, chunk)
+        self.pass_on(hop + 1, chunk)
+
+    def end(self):
+        self.keep.wait()
+        for chunk in range(2):
+            self.arrive(self.n - 1, chunk)
+            for hop in range(1, self.n):
+                for index, side in enumerate(self.sides):
+                    plane = self.z - side * (hop - 1)
+
+                    @pl.when(self.exists(self.z + side) & self.exists(plane))
+                    def _(index=index, plane=plane, hop=hop, chunk=chunk):
+                        self.copy(hop, index, chunk, plane).wait_send()
+
+
 def gelu_parts(pre):
     scale = 0.7978845608028654
     square = pre * pre
@@ -516,8 +599,8 @@
 
 def forward_kernel(
     n_f, n_long, n_rows, long_ref, short_ref, o_ref, w_ref, vec_ref, row_ref, g_ref, up_ref,
-    h_ref, there_ref, act_ref, slope_ref, gd_ref,
-    rows_ref, vec_scr, out_buf, in_buf, all_ref, send, recv,
+    own_ref, h_ref, there_ref, act_ref, slope_ref, gd_ref, down_ref,
+    rows_ref, vec_scr, out_buf, in_buf, all_ref, send, recv, line_send, line_recv, line_sem,
 ):
     i = pl.program_id(0)
     z = lax.axis_index("dp")
@@ -526,6 +609,8 @@
     n_up = n_rows + n_f
     n_down = n_up + n_f
     barrier = pltpu.get_barrier_semaphore()
+    line = Line(own_ref, down_ref, line_send, line_recv, line_sem)
+    n_events = 2 * (line.n - 2)
 
     def transfer(k):
         return pltpu.make_async_remote_copy(
@@ -536,7 +621,10 @@
     @pl.when(i == 0)
     def _():
         greet(n_f, partner)
+        line.greet()
         vec_scr[...] = vectors(vec_ref)
+        pl.semaphore_wait(barrier, n_f - 1 + line.neighbours())
+        line.begin()
 
     def body(x_ref):
         hidden = x_ref[...] + dot(o_ref[...], w_ref[...], NT)
@@ -549,10 +637,6 @@
     pl.when(i < n_long)(lambda: body(long_ref))
     pl.when((i >= n_long) & (i < n_rows))(lambda: body(short_ref))
 
-    @pl.when(i == n_rows)
-    def _():
-        pl.semaphore_wait(barrier, n_f - 1)
-
     @pl.when((i >= n_rows) & (i < n_up - 1))
     def _():
         k = i - n_rows + 1
@@ -566,6 +650,10 @@
     @pl.when((i > n_up) & (i < n_down))
     def _():
         transfer(i - n_up).wait_recv()
+
+    for number in range(n_events):
+        at = n_up + 1 + number * (n_f - 1) // (n_events - 1)
+        pl.when(i == at)(functools.partial(line.event, number))
 
     @pl.when((i >= n_up) & (i < n_down))
     def _():
@@ -590,9 +678,10 @@
     def _():
         for k in range(1, n_f):
             transfer(k).wait_send()
-
-
-def forward_experts(long_x, short_x, o, dense, slot_row, g_there, up, n_f, cap):
+        line.end()
+
+
+def forward_experts(long_x, short_x, o, dense, slot_row, g_there, up, own_down, n_dp, n_f, cap):
     width = long_x.shape[1]
     hidden = up.shape[1]
     n_long, n_short = long_x.shape[0] // ROWS, short_x.shape[0] // ROWS
@@ -615,6 +704,7 @@
             constant((8, count)),
             constant((slots, width)),
             constant((width, hidden)),
+            pl.BlockSpec(memory_space=pl.ANY),
         ],
         out_specs=[
             pl.BlockSpec((ROWS, width), lambda i: (jnp.minimum(i, n_rows - 1), 0)),
@@ -622,6 +712,7 @@
             tile,
             tile,
             pl.BlockSpec((width, width), lambda i: (jnp.clip(i - n_down, 0, n_hidden - 1), 0)),
+            pl.BlockSpec(memory_space=pl.ANY),
         ],
         out_shape=[
             jax.ShapeDtypeStruct((count, width), F32),
@@ -629,6 +720,7 @@
             jax.ShapeDtypeStruct((slots, hidden), BF16),
             jax.ShapeDtypeStruct((slots, hidden), BF16),
             jax.ShapeDtypeStruct((hidden, width), BF16),
+            jax.ShapeDtypeStruct((n_dp,) + own_down.shape, BF16),
         ],
         scratch_shapes=[
             pltpu.VMEM((count, width), BF16),
@@ -638,77 +730,26 @@
             pltpu.VMEM((slots, hidden), BF16),
             pltpu.SemaphoreType.DMA((n_f,)),
             pltpu.SemaphoreType.DMA((n_f,)),
+            pltpu.SemaphoreType.DMA((n_dp - 1, 2, 2)),
+            pltpu.SemaphoreType.DMA((n_dp - 1, 2, 2)),
+            pltpu.SemaphoreType.DMA,
         ],
         compiler_params=params(collective_id=2, has_side_effects=True),
         cost_estimate=cost(
             2 * slots * width * (count + 2 * hidden), 60e6, slots * hidden
         ),
         name="forward_experts",
-    )(long_x, short_x, o, dense, dense, slot_row, g_there, up)
-
-
-def own_kernel(
-    n_f, z_ref, b_ref, g_ref, act_ref, slope_ref, up_ref, down_ref, y_ref, db_ref, gu_ref, all_ref
-):
-    i = pl.program_id(0)
-    _, partner = peers(n_f)
-    cap = y_ref.shape[0]
-
-    @pl.when(i < n_f)
-    def _():
-        here = pl.ds(pl.multiple_of(partner(i) * cap, cap), cap)
-        d_act = dot(g_ref[here, :], down_ref[...], NT)
-        d_pre = (d_act * slope_ref[...].astype(F32)).astype(BF16)
-        all_ref[here, :] = d_pre
-        db_ref[...] = dot(d_pre, up_ref[...], NT)
-        y_ref[...] = dot(act_ref[...], down_ref[...])
-
-    @pl.when(i >= n_f)
-    def _():
-        gu_ref[...] = dot(b_ref[...], all_ref[...], TN).astype(BF16)
-
-
-def own_experts(z, b_there, g_there, act, slope, up, own_down, n_f, cap):
-    slots, width = b_there.shape
-    piece = own_down.shape[0]
-    tile = pl.BlockSpec((cap, piece), lambda i, z: (jnp.minimum(i, n_f - 1), z[0]))
-    out = pl.BlockSpec((cap, width), lambda i, z: (jnp.minimum(i, n_f - 1), 0))
-    return pl.pallas_call(
-        functools.partial(own_kernel, n_f),
-        grid_spec=pltpu.PrefetchScalarGridSpec(
-            num_scalar_prefetch=1,
-            grid=(n_f + 1,),
-            in_specs=[
-                constant((slots, width)),
-                constant((slots, width)),
-                tile,
-                tile,
-                pl.BlockSpec((width, piece), lambda i, z: (0, z[0])),
-                constant((piece, width)),
-            ],
-            out_specs=[out, out, pl.BlockSpec((width, piece), lambda i, z: (0, 0))],
-            scratch_shapes=[pltpu.VMEM((slots, piece), BF16)],
-        ),
-        out_shape=[
-            jax.ShapeDtypeStruct((slots, width), F32),
-            jax.ShapeDtypeStruct((slots, width), F32),
-            jax.ShapeDtypeStruct((width, piece), BF16),
-        ],
-        compiler_params=params(),
-        cost_estimate=cost(8 * slots * width * piece, 30e6),
-        name="own_experts",
-    )(z, b_there, g_there, act, slope, up, own_down)
+    )(long_x, short_x, o, dense, dense, slot_row, g_there, up, own_down)
 
 
 def back_kernel(
-    n_dp, n_f, b_ref, g_ref, act_ref, slope_ref, up_ref, down_ref, y0_ref, db0_ref, gu0_ref,
-    y_ref, db_ref, gu_ref, out_buf, all_ref, send, recv, l_sem,
+    n_f, b_ref, g_ref, act_ref, slope_ref, up_ref, down_ref, y_ref, db_ref, gu_ref,
+    out_buf, all_ref, send, recv, l_sem,
 ):
     i = pl.program_id(0)
     z = lax.axis_index("dp")
     f, partner = peers(n_f)
     cap, width = out_buf.shape[1:]
-    piece = gu_ref.shape[1]
     barrier = pltpu.get_barrier_semaphore()
 
     def transfer(k):
@@ -717,9 +758,6 @@
             device_id=(z, partner(k)), device_id_type=MESH,
         )
 
-    def other(m):
-        return pl.ds(pl.multiple_of(lax.rem(z + m, n_dp) * piece, piece), piece)
-
     keep = pltpu.make_async_copy(out_buf.at[0], db_ref.at[f], l_sem)
 
     @pl.when(i == 0)
@@ -731,12 +769,13 @@
         k = n_f - 1 - i
         here = pl.ds(pl.multiple_of(partner(k) * cap, cap), cap)
         g = g_ref[here, :]
-        d_b = db0_ref[...]
-        for m in range(1, n_dp):
-            d_act = dot(g, down_ref[other(m), :], NT)
-            d_pre = (d_act * slope_ref[:, other(m)].astype(F32)).astype(BF16)
-            all_ref[here, other(m)] = d_pre
-            d_b = d_b + dot(d_pre, up_ref[:, other(m)], NT)
+        d_b = jnp.zeros((cap, width), F32)
+        for first in range(0, up_ref.shape[1], width):
+            cut = slice(first, first + width)
+            d_act = dot(g, down_ref[cut, :], NT)
+            d_pre = (d_act * slope_ref[:, cut].astype(F32)).astype(BF16)
+            all_ref[here, cut] = d_pre
+            d_b = d_b + dot(d_pre, up_ref[:, cut], NT)
         out_buf[k] = d_b.astype(BF16)
 
     @pl.when(i == 0)
@@ -754,18 +793,11 @@
     @pl.when(i < n_f)
     def _():
         here = pl.ds(pl.multiple_of(partner(n_f - 1 - i) * cap, cap), cap)
-        y = y0_ref[...]
-        for m in range(1, n_dp):
-            y = y + dot(act_ref[:, other(m)], down_ref[other(m), :])
-        y_ref[here, :] = y.astype(BF16)
-
-    @pl.when((i >= n_f) & (i - n_f == z))
-    def _():
-        gu_ref[...] = gu0_ref[...]
-
-    @pl.when((i >= n_f) & (i - n_f != z))
-    def _():
-        cut = pl.ds(pl.multiple_of((i - n_f) * piece, piece), piece)
+        y_ref[here, :] = dot(act_ref[...], down_ref[...]).astype(BF16)
+
+    @pl.when(i >= n_f)
+    def _():
+        cut = pl.ds(pl.multiple_of((i - n_f) * width, width), width)
         gu_ref[...] = dot(b_ref[...], all_ref[:, cut], TN).astype(BF16)
 
     @pl.when(i == pl.num_programs(0) - 1)
@@ -777,15 +809,14 @@
             transfer(k).wait_send()
 
 
-def back_experts(b_there, g_there, act, slope, up, down, y0, db0, gu0, n_dp, n_f, cap):
+def back_experts(b_there, g_there, act, slope, up, down, n_f, cap):
     slots, width = b_there.shape
     hidden = up.shape[1]
-    piece = hidden // n_dp
+    n_hidden = hidden // width
     tile = pl.BlockSpec((cap, hidden), lambda i: (jnp.maximum(n_f - 1 - i, 0), 0))
-    begun = pl.BlockSpec((cap, width), lambda i: (jnp.maximum(n_f - 1 - i, 0), 0))
     return pl.pallas_call(
-        functools.partial(back_kernel, n_dp, n_f),
-        grid=(n_f + n_dp,),
+        functools.partial(back_kernel, n_f),
+        grid=(n_f + n_hidden,),
         in_specs=[
             constant((slots, width)),
             constant((slots, width)),
@@ -793,14 +824,11 @@
             tile,
             constant((width, hidden)),
             constant((hidden, width)),
-            begun,
-            begun,
-            constant((width, piece)),
         ],
         out_specs=[
             pl.BlockSpec((slots, width), lambda i: (0, 0)),
             pl.BlockSpec(memory_space=pl.ANY),
-            pl.BlockSpec((width, piece), lambda i: (0, jnp.maximum(i - n_f, 0))),
+            pl.BlockSpec((width, width), lambda i: (0, jnp.maximum(i - n_f, 0))),
         ],
         out_shape=[
             jax.ShapeDtypeStruct((slots, width), BF16),
@@ -815,9 +843,9 @@
             pltpu.SemaphoreType.DMA,
         ],
         compiler_params=params(collective_id=3, has_side_effects=True),
-        cost_estimate=cost(6 * slots * width * hidden, 60e6),
+        cost_estimate=cost(8 * slots * width * hidden, 60e6),
         name="back_experts",
-    )(b_there, g_there, act, slope, up, down, y0, db0, gu0)
+    )(b_there, g_there, act, slope, up, down)
 
 
 def combine_rows(col_ref, slots_ref):
@@ -831,7 +859,7 @@
     dh_ref, do_ref, gp_ref, gv_ref, yb_ref, acc_ref, vec_scr, send, recv,
 ):
     i = pl.program_id(0)
-    home = Homeward(n_f, range(1, 3 * n_f // 4), y_ref, yb_ref, send, recv)
+    home = Homeward(n_f, early_blocks(n_f), y_ref, yb_ref, send, recv)
     pl.when(i == 0)(home.begin)
 
     @pl.when(i == 0)
@@ -1401,7 +1429,6 @@
     slots = experts * cap
 
     up = lax.all_gather(w_up, "dp", axis=2, tiled=True)[0]
-    down = lax.all_gather(w_down, "dp", axis=1, tiled=True)[0]
 
     vec = jnp.stack([ln1_gain, ln1_bias, ln2_gain, ln2_bias], 1)
     own = jnp.concatenate(
@@ -1421,16 +1448,12 @@
     g_there = exchange(g_slots)
     qkv = make_qkv(xl, xs, dense)
     o, lse = attend(qkv, long_len, short_len, seqs)
-    h, b_there, act, slope, grad_down = forward_experts(
-        xl, xs, o, dense, slot_row, g_there, up, n_f, cap
+    h, b_there, act, slope, grad_down, down = forward_experts(
+        xl, xs, o, dense, slot_row, g_there, up, w_down[0], n_dp, n_f, cap
     )
+    down = down.reshape(-1, width)
     grad_down = lax.psum_scatter(grad_down, "dp", scatter_dimension=0, tiled=True)
-    y0, db0, gu0 = own_experts(
-        lax.axis_index("dp").reshape(1), b_there, g_there, act, slope, up, w_down[0], n_f, cap
-    )
-    y, db_back, grad_up = back_experts(
-        b_there, g_there, act, slope, up, down, y0, db0, gu0, n_dp, n_f, cap
-    )
+    y, db_back, grad_up = back_experts(b_there, g_there, act, slope, up, down, n_f, cap)
     db_back = db_back.reshape(slots, width)
     grad_up = lax.psum_scatter(grad_up, "dp", scatter_dimension=1, tiled=True)
     y = y.reshape(n_f, cap, width)

time: 403 us -> 399 us (0.990)
    pallas_call x1, Pallas kernels: 72.3 us -> 88 us  [forward_experts(): pl.pallas_call(functools.partial(forward_kernel, n_f, n_long, n_rows), gr...]
    pallas_call x2 -> x1, Pallas kernels: 69.5 us -> 56 us  [back_experts(): pl.pallas_call(functools.partial(back_kernel, n_f), grid=(n_f + n_hidden,...]
    pallas_call x1, Pallas kernels: 26.3 us -> 22.2 us  [hidden_back(): pl.pallas_call(functools.partial(hidden_back_kernel, n_f, n_long, n_rows)...]
  transfers between devices with their start and end apart: 5 -> 4, of which waited for: 3 -> 3; matrix products, arithmetic and copies ran while one was open for 1% -> 1% of each run, Pallas kernels for 91% -> 69%
where the time goes in v6:
time: 399 us; the launch traced here: 393 us
  Pallas kernels  359 us (90%)
  between operations  15.3 us (4%)
  starting transfers between devices  6.11 us (2%)
  waiting for transfers between devices  5.16 us (1%)
  other arithmetic  5.16 us (1%)
    pallas_call x1, Pallas kernels, forward_experts(): pl.pallas_call(functools.partial(forward_kernel, n_f, n_long, n_rows), gr...  88 us
    pallas_call x1, Pallas kernels, close_stage(): pl.pallas_call(functools.partial(close_kernel, n_long, n_rows), grid=(3 +...  64.9 us
    pallas_call x1, Pallas kernels, back_experts(): pl.pallas_call(functools.partial(back_kernel, n_f), grid=(n_f + n_hidden,...  56 us
    pallas_call x1, Pallas kernels, gather_dense(): pl.pallas_call(functools.partial(gather_kernel, n_dp, n_f, cap), out_shap...  49.7 us
    pallas_call x1, Pallas kernels, attend_back(): pl.pallas_call(functools.partial(attend_back_kernel, seqs, n_f), grid=(pa...  36.7 us
    pallas_call x1, Pallas kernels, hidden_back(): pl.pallas_call(functools.partial(hidden_back_kernel, n_f, n_long, n_rows)...  22.2 us
    pallas_call x1, Pallas kernels, attend(): pl.pallas_call(functools.partial(attend_kernel, seqs), grid=(pairs,), in_...  21.9 us
    pallas_call x1, Pallas kernels, make_qkv(): pl.pallas_call(functools.partial(qkv_kernel, n_long, width), grid=(n_long...  11.5 us
  transfers between devices with their start and end apart: 4, of which 3 were waited for; matrix products, arithmetic and copies ran while one was open for 1% of the time, Pallas kernels for 69%

profile of v6, /device:TPU:12, one launch (start us, length us, event | category | flops | bytes accessed | tf_op | source)
XLA Modules:
  0.0 393.2 jit_solution(18313250580288027837)
XLA Ops:
  7.2 0.0 all-gather.2.cloned.1.call-start
  7.2 0.7 all-gather.2.cloned.1.call-update
  7.9 0.7 pad_maximum_fusion
  8.6 0.1 copy.33
  8.7 1.9 copy.34.ids_ref
  10.6 1.6 fusion.1.own_ref
  12.2 49.7 %gather_dense.1 = (bf16[4,8,24,3200]{3,2,1,0:T(8,128)(2,1)}, s32[1536,1]{1,0:T(8,128)}, s32[8,1536]{1,0:T(8,128)}, bf16[2048,768]{1,0:T(8,128)(2,1)}) custom-call(bf16[24,3200]{1,0:T(8,128)(2,1)} %fusion.1.own_ref, s32[1536,1]{1,0:T(8,128)} %copy.34.ids_ref, f32[1024,768]{1,0:T(8,128)} %bitcast.40, f32[512,768]{1,0:T(8,128)} %bitcast.48), custom_call_target="tpu_custom_call" | custom-call | bytes 100000000 | tf_op jit(solution)/shard_map/gather_dense/pallas_call | solution.py:158
  61.9 5.6 %all-to-all-start = ((bf16[8,256,768]{2,1,0:T(8,128)(2,1)}), bf16[8,256,768]{2,1,0:T(8,128)(2,1)S(1)}, u32[]{:S(2)}, u32[]{:S(2)}) async-start(bf16[8,256,768]{2,1,0:T(8,128)(2,1)} %bitcast.44), calls=%async_computation | async-start | bytes 6291456 | tf_op jit(solution)/shard_map/all_to_all | solution.py:1443
  67.4 0.5 reduce-scatter.3.cloned.1.call-start
  69.2 11.5 %make_qkv.1.q_ref.k_ref.v_ref = bf16[1536,2304]{1,0:T(8,128)(2,1)} custom-call(f32[1024,768]{1,0:T(8,128)} %bitcast.45, f32[512,768]{1,0:T(8,128)} %bitcast.50, bf16[768,3200]{1,0:T(8,128)(2,1)} %bitcast.32, bf16[768,3200]{1,0:T(8,128)(2,1)} %bitcast.33), custom_call_target="tpu_custom_call" | custom-call | flops 5435817984 | bytes 15335424 | tf_op jit(solution)/shard_map/make_qkv/pallas_call | solution.py:288
  80.7 21.9 %attend.1 = (bf16[1536,768]{1,0:T(8,128)(2,1)}, f32[128,1536]{1,0:T(8,128)}) custom-call(s32[1]{0:T(128)S(6)} %copy.36.long_len, s32[1]{0:T(128)S(6)} %copy.37.short_len, bf16[1536,2304]{1,0:T(8,128)(2,1)} %make_qkv.1.q_ref.k_ref.v_ref, bf16[1536,2304]{1,0:T(8,128)(2,1)} %make_qkv.1.q_ref.k_ref.v_ref, bf16[1536,2304]{1,0:T(8,128)(2,1)} %make_qkv.1.q_ref.k_ref.v_ref), custom_call_target="tpu_custom_call" | custom-call | flops 16000000000 | bytes 9437184 | tf_op jit(solution)/shard_map/attend/pallas_call | solution.py:381
  102.6 1.7 all-to-all-done
  104.3 0.0 copy-start
  104.3 2.7 all-gather.2.cloned.1.call-done
  107.0 0.0 copy-done
  107.0 88.0 %forward_experts.1 = (f32[1536,768]{1,0:T(8,128)}, bf16[2048,768]{1,0:T(8,128)(2,1)}, bf16[2048,3072]{1,0:T(8,128)(2,1)}, bf16[2048,3072]{1,0:T(8,128)(2,1)}, bf...) custom-call(f32[1024,768]{1,0:T(8,128)} %bitcast.46, f32[512,768]{1,0:T(8,128)} %bitcast.51, ...), custom_call_target="tpu_custom_call" | custom-call | flops 24159191040 | bytes 60000000 | tf_op jit(solution)/shard_map/forward_experts/pallas_call | solution.py:695
  195.0 0.0 reduce-scatter.3.cloned.1.call-update
  195.0 0.0 reduce-scatter.5.cloned.1.call-start
  195.1 56.0 %back_experts.1 = (bf16[2048,768]{1,0:T(8,128)(2,1)}, bf16[8,256,768]{2,1,0:T(8,128)(2,1)}, bf16[768,3072]{1,0:T(8,128)(2,1)}) custom-call(bf16[2048,768]{1,0:T(8,128)(2,1)} %get-tuple-element.58.b_ref, bf16[2048,768]{1,0:T(8,128)(2,1)} %bitcast.43, bf16[2048,3072]{1,0:T(8,128)(2,1)} %get-tuple-element.59.act_ref, ...), custom_call_target="tpu_custom_call" | custom-call | flops 38654705664 | bytes 60000000 | tf_op jit(solution)/shard_map/back_experts/pallas_call | solution.py:817
  251.1 0.0 reduce-scatter.5.cloned.1.call-update
  251.2 22.2 %hidden_back.1 = (f32[1536,768]{1,0:T(8,128)}, bf16[1536,768]{1,0:T(8,128)(2,1)}, bf16[768,768]{1,0:T(8,128)(2,1)}, f32[128,768]{1,0:T(8,128)}, bf16[8,256,768]{2,1,0:T(8,128)(2,1)}) custom-call(f32[1536,768]{1,0:T(8,128)} %get-tuple-element.56.h_ref, s32[1536,1]{1,0:T(8,128)} %get-tuple-element.57.col_ref, bf16[2048,768]{1,0:T(8,128)(2,1)} %bitcast.74, ...), custom_call_target="tpu_custom_call" | custom-call | flops 8455716864 | bytes 18874368 | tf_op jit(solution)/shard_map/hidden_back/pallas_call | solution.py:899
  273.3 36.7 %attend_back.1 = (bf16[3,1536,768]{2,1,0:T(8,128)(2,1)}, bf16[8,256,768]{2,1,0:T(8,128)(2,1)}) custom-call(s32[1]{0:T(128)S(6)} %copy.36.long_len, s32[1]{0:T(128)S(6)} %copy.37.short_len, bf16[1536,2304]{1,0:T(8,128)(2,1)} %make_qkv.1.q_ref.k_ref.v_ref, bf16[1536,2304]{1,0:T(8,128)(2,1)} %make_qkv.1.q_ref.k_ref.v_ref, ...), custom_call_target="tpu_custom_call", output_to_operand_aliasing={{1}: (9, {})} | custom-call | flops 40000000000 | bytes 18874368 | tf_op jit(solution)/shard_map/attend_back/pallas_call | solution.py:479
  310.1 64.9 %close_stage.1 = (f32[24,3200]{1,0:T(8,128)}, f32[1024,768]{1,0:T(8,128)}, f32[512,768]{1,0:T(8,128)}, f32[1024,768]{1,0:T(8,128)}, f32[512,768]{1,0:T(8,128)}) custom-call(bf16[4,8,24,768]{3,2,1,0:T(8,128)(2,1)} %bitcast.76, f32[128,768]{1,0:T(8,128)} %get-tuple-element.65.gv_ref, f32[1024,768]{1,0:T(8,128)} %bitcast.47, f32[512,768]{1,0:T(8,128)} %bitcast.52, ...), custom_call_target="tpu_custom_call" | custom-call | flops 15703474176 | bytes 60000000 | tf_op jit(solution)/shard_map/close_stage/pallas_call | solution.py:1317
  375.0 0.0 reduce-scatter.3.cloned.1.call-done.refs_5_
  375.0 8.5 %ship.1 = (f32[1024,768]{1,0:T(8,128)}, f32[512,768]{1,0:T(8,128)}, f32[1024,768]{1,0:T(8,128)}, f32[512,768]{1,0:T(8,128)}, f32[24,2304]{1,0:T(8,128)}, /*index...) custom-call(f32[1024,768]{1,0:T(8,128)} %get-tuple-element.72.refs_0, ...), custom_call_target="tpu_custom_call" | custom-call | bytes 18874368 | tf_op jit(solution)/shard_map/ship/pallas_call | solution.py:1396
  383.5 0.1 reduce-scatter.5.cloned.1.call-done
  383.6 2.8 bitcast_convert_fusion
Async XLA Ops:
  7.2 99.8 %all-gather.2.cloned.1.call-start = ((), (), s32[]{:S(2)}) async-start(), calls=%async_computation.3 | async-start | bytes 5898240 | tf_op jit(solution)/shard_map/all_gather | solution.py:1431
  61.9 42.5 %all-to-all-start = ((bf16[8,256,768]{2,1,0:T(8,128)(2,1)}), bf16[8,256,768]{2,1,0:T(8,128)(2,1)S(1)}, u32[]{:S(2)}, u32[]{:S(2)}) async-start(bf16[8,256,768]{2,1,0:T(8,128)(2,1)} %bitcast.44), calls=%async_computation | async-start | bytes 6291456 | tf_op jit(solution)/shard_map/all_to_all | solution.py:1443
  67.4 307.6 %reduce-scatter.3.cloned.1.call-start = ((), (), s32[]{:S(2)}) async-start(), calls=%async_computation.4 | async-start | bytes 5898240 | tf_op jit(solution)/shard_map/reduce_scatter | solution.py:1455
  104.3 2.7 copy-start
  195.0 188.6 %reduce-scatter.5.cloned.1.call-start = ((), (), s32[]{:S(2)}) async-start(), calls=%async_computation.5 | async-start | bytes 5898240 | tf_op jit(solution)/shard_map/reduce_scatter | solution.py:1458
Sparse Core Ops, SparseCore 0:
  9.6 97.3 all-gather.1
  195.2 87.1 reduce-scatter.2
  284.7 98.8 reduce-scatter.4
